TPU v7x, 32 devices: a whole 2x2x4 slice. The times are simulated.
32 devices in a mesh: dp: 8 (over z, x), tensor: 4 (over y, core).
Axes of the slice: x: 2, y: 2, z: 4, core: 2. Of those that a mesh axis runs over, the one named last changes fastest.
Arguments:
- tokens: bfloat16 [16384, 1024], P('dp'), may hold values from -6 to 6
- cotangent: bfloat16 [16384, 1024], P(('dp', 'tensor')), may hold values from -6 to 6
- norm1_gain: float32 [1024], replicated, may hold values from 0.5 to 1.5
- norm2_gain: float32 [1024], replicated, may hold values from 0.5 to 1.5
- query_weight: bfloat16 [1024, 1024], P('dp', 'tensor'), may hold values from -0.1875 to 0.1875
- key_weight: bfloat16 [1024, 1024], P('dp', 'tensor'), may hold values from -0.1875 to 0.1875
- value_weight: bfloat16 [1024, 2048], P('dp', 'tensor'), may hold values from -0.1875 to 0.1875
- outgate_weight: bfloat16 [1024, 2048], P('dp', 'tensor'), may hold values from -0.1875 to 0.1875
- alpha_weight: bfloat16 [1024, 8], P('dp', 'tensor'), may hold values from -0.1875 to 0.1875
- beta_weight: bfloat16 [1024, 8], P('dp', 'tensor'), may hold values from -0.1875 to 0.1875
- conv_query: float32 [4, 1024], P(None, 'tensor'), may hold values from -3 to 3
- conv_key: float32 [4, 1024], P(None, 'tensor'), may hold values from -3 to 3
- conv_value: float32 [4, 2048], P(None, 'tensor'), may hold values from -3 to 3
- decay_log: float32 [8], P('tensor'), may hold values from 0 to 2.77
- decay_bias: float32 [8], P('tensor'), may hold values from -4.6 to -2.3
- onorm_gain: float32 [256], replicated, may hold values from 0.5 to 1.5
- output_weight: bfloat16 [2048, 1024], P('tensor', 'dp'), may hold values from -0.25 to 0.25
- gate_weight: bfloat16 [1024, 2816], P('dp', 'tensor'), may hold values from -0.1875 to 0.1875
- up_weight: bfloat16 [1024, 2816], P('dp', 'tensor'), may hold values from -0.1875 to 0.1875
- down_weight: bfloat16 [2816, 1024], P('tensor', 'dp'), may hold values from -0.109375 to 0.109375
Outputs:
- block_output: bfloat16 [16384, 1024], P(('dp', 'tensor'))
- tokens_grad: float32 [16384, 1024], P(('dp', 'tensor'))
- norm1_gain_grad: float32 [1024], P('tensor')
- norm2_gain_grad: float32 [1024], P('tensor')
- query_weight_grad: float32 [1024, 1024], P('dp', 'tensor')
- key_weight_grad: float32 [1024, 1024], P('dp', 'tensor')
- value_weight_grad: float32 [1024, 2048], P('dp', 'tensor')
- outgate_weight_grad: float32 [1024, 2048], P('dp', 'tensor')
- alpha_weight_grad: float32 [1024, 8], P('dp', 'tensor')
- beta_weight_grad: float32 [1024, 8], P('dp', 'tensor')
- conv_query_grad: float32 [4, 1024], P(None, 'tensor')
- conv_key_grad: float32 [4, 1024], P(None, 'tensor')
- conv_value_grad: float32 [4, 2048], P(None, 'tensor')
- decay_log_grad: float32 [8], P('tensor')
- decay_bias_grad: float32 [8], P('tensor')
- onorm_gain_grad: float32 [256], P('tensor')
- output_weight_grad: float32 [2048, 1024], P('tensor', 'dp')
- gate_weight_grad: float32 [1024, 2816], P('dp', 'tensor')
- up_weight_grad: float32 [1024, 2816], P('dp', 'tensor')
- down_weight_grad: float32 [2816, 1024], P('tensor', 'dp')
All inputs are finite; a program needn't handle non-finite values.
Results may differ from a plain program's by a relative error of at most 0.012.
Values may be sent and summed in bfloat16 or wider, within the bound.
No kernel may reach another device: no remote copies, remote signals or barrier semaphores. Data moves between devices by JAX's collectives and lax.ppermute only.
A program may use at most 384 MiB of HBM per device.

v0:
```python
import jax
import jax.numpy as jnp
from jax import lax
from jax.sharding import PartitionSpec as P

STRETCH = 64
SEQ = 2048


HIGH = lax.Precision.HIGHEST
EPS_NORM = 1e-05


def matmul_high(left_side, right_side):
    return jnp.einsum("...ij,...jk->...ik", left_side, right_side, precision=HIGH)


def dot_plain(left_side, right_side):
    return jnp.dot(left_side, right_side, preferred_element_type=jnp.float32)


def dot_right_t(left_side, right_side):
    return lax.dot_general(
        left_side, right_side, (((1,), (1,)), ((), ())), preferred_element_type=jnp.float32
    )


def dot_left_t(left_side, right_side):
    return lax.dot_general(
        left_side, right_side, (((0,), (0,)), ((), ())), preferred_element_type=jnp.float32
    )


def norm_one(inputs, gain):
    return inputs * lax.rsqrt(jnp.mean(inputs * inputs, axis=-1, keepdims=True) + EPS_NORM) * gain


def unit_rows(inputs):
    return inputs * lax.rsqrt(jnp.sum(inputs * inputs, axis=-1, keepdims=True) + 1e-06)


def short_conv(raw_rows, weight):
    kernel_len = weight.shape[0]
    length = raw_rows.shape[1]
    padded = jnp.pad(raw_rows, ((0, 0), (kernel_len - 1, 0), (0, 0)))
    total = padded[:, 0:length] * weight[0]
    for offset in range(1, kernel_len):
        total = total + padded[:, offset : offset + length] * weight[offset]
    return jax.nn.silu(total)


def unit_inverse(coupling, block_len):
    identity = jnp.eye(block_len, dtype=coupling.dtype)
    result = identity - coupling
    power = coupling
    span = 2
    while span < block_len:
        power = matmul_high(power, power)
        result = matmul_high(result, identity + power)
        span = span * 2
    return result


def to_blocks(array, block_len):
    seq_count, length, head_count = (array.shape[0], array.shape[1], array.shape[2])
    shaped = array.reshape(seq_count, length // block_len, block_len, head_count, -1)
    return jnp.moveaxis(shaped, 3, 1)


def delta_rule(queries, key_rows, values, decays, beta_rates, block_len):
    seq_count, length, head_count, key_dim = queries.shape
    q_blocks = to_blocks(queries, block_len)
    k_blocks = to_blocks(key_rows, block_len)
    v_blocks = to_blocks(values, block_len)
    cumulative = jnp.cumsum(to_blocks(decays[..., None], block_len)[..., 0], axis=-1)
    beta_blocks = to_blocks(beta_rates[..., None], block_len)[..., 0]
    positions = jnp.arange(block_len)
    causal = positions[:, None] >= positions[None, :]
    strict = positions[:, None] > positions[None, :]
    gaps = jnp.where(causal, cumulative[..., :, None] - cumulative[..., None, :], 0.0)
    fading = jnp.where(causal, jnp.exp(gaps), 0.0)
    key_key = jnp.einsum("...id,...jd->...ij", k_blocks, k_blocks, precision=HIGH)
    coupling = jnp.where(strict, beta_blocks[..., :, None] * fading * key_key, 0.0)
    inverse = unit_inverse(coupling, block_len)
    targets = jnp.concatenate(
        [
            (beta_blocks * jnp.exp(cumulative))[..., None] * k_blocks,
            beta_blocks[..., None] * v_blocks,
        ],
        axis=-1,
    )
    solved = matmul_high(inverse, targets)
    key_part = solved[..., :key_dim]
    value_part = solved[..., key_dim:]
    query_key = jnp.einsum("...id,...jd->...ij", q_blocks, k_blocks, precision=HIGH) * fading
    query_fade = q_blocks * jnp.exp(cumulative)[..., None]
    key_fade = k_blocks * jnp.exp(cumulative[..., -1:] - cumulative)[..., None]
    block_fade = jnp.exp(cumulative[..., -1])
    sequence = tuple(
        (
            jnp.moveaxis(member, 2, 0)
            for member in (key_part, value_part, query_fade, key_fade, query_key, block_fade)
        )
    )

    def advance(state, block):
        key_now, value_now, query_now, fade_now, scores_now, decay_now = block
        fresh = value_now - matmul_high(key_now, state)
        output = matmul_high(query_now, state) + matmul_high(scores_now, fresh)
        state = decay_now[..., None, None] * state + jnp.einsum(
            "...ck,...cv->...kv", fade_now, fresh, precision=HIGH
        )
        return (state, output)

    start = jnp.zeros((seq_count, head_count, key_dim, values.shape[-1]), jnp.float32)
    final_state, outputs = lax.scan(jax.checkpoint(advance), start, sequence)
    return jnp.transpose(outputs, (1, 0, 3, 2, 4)).reshape(seq_count, length, head_count, -1)


def local_mixer(
    query_raw,
    key_raw,
    value_raw,
    gate_raw,
    alpha_raw,
    beta_raw,
    conv_query,
    conv_key,
    conv_value,
    decay_log,
    decay_bias,
    onorm_gain,
    seq_count,
    head_count,
):
    row_count = query_raw.shape[0]
    length = row_count // seq_count

    def conv_heads(raw_rows, weight):
        return short_conv(raw_rows.reshape(seq_count, length, -1), weight).reshape(
            seq_count, length, head_count, -1
        )

    queries = unit_rows(conv_heads(query_raw, conv_query))
    queries = queries * queries.shape[-1] ** (-0.5)
    key_rows = unit_rows(conv_heads(key_raw, conv_key))
    values = conv_heads(value_raw, conv_value)
    beta_rates = jax.nn.sigmoid(beta_raw).reshape(seq_count, length, head_count)
    decays = (-jnp.exp(decay_log) * jax.nn.softplus(alpha_raw + decay_bias)).reshape(
        seq_count, length, head_count
    )
    mixed = delta_rule(queries, key_rows, values, decays, beta_rates, STRETCH)
    gates = gate_raw.reshape(seq_count, length, head_count, -1)
    normed = (
        mixed
        * lax.rsqrt(jnp.mean(mixed * mixed, axis=-1, keepdims=True) + EPS_NORM)
        * onorm_gain
        * jax.nn.silu(gates)
    )
    return normed.reshape(row_count, -1)


def swiglu(gate, upward):
    return jax.nn.silu(gate) * upward


def per_device(
    tokens,
    cotangent,
    norm1_gain,
    norm2_gain,
    query_weight,
    key_weight,
    value_weight,
    outgate_weight,
    alpha_weight,
    beta_weight,
    conv_query,
    conv_key,
    conv_value,
    decay_log,
    decay_bias,
    onorm_gain,
    output_weight,
    gate_weight,
    up_weight,
    down_weight,
):
    tensor_index = lax.axis_index("tensor")
    tensor_count = lax.axis_size("tensor")
    tok_count = tokens.shape[0]
    part_rows = cotangent.shape[0]
    seq_count = tok_count // SEQ
    width = tokens.shape[1]
    gain_share = width // tensor_count
    gain_start = tensor_index * gain_share
    w_query, w_key, w_value, w_outgate, w_alpha, w_beta, w_output, w_gate, w_up, w_down = (
        lax.all_gather(query_weight, "dp", axis=0, tiled=True),
        lax.all_gather(key_weight, "dp", axis=0, tiled=True),
        lax.all_gather(value_weight, "dp", axis=0, tiled=True),
        lax.all_gather(outgate_weight, "dp", axis=0, tiled=True),
        lax.all_gather(alpha_weight, "dp", axis=0, tiled=True),
        lax.all_gather(beta_weight, "dp", axis=0, tiled=True),
        lax.all_gather(output_weight, "dp", axis=1, tiled=True),
        lax.all_gather(gate_weight, "dp", axis=0, tiled=True),
        lax.all_gather(up_weight, "dp", axis=0, tiled=True),
        lax.all_gather(down_weight, "dp", axis=1, tiled=True),
    )
    inputs = tokens.astype(jnp.float32)
    inverse_rms = lax.rsqrt(jnp.mean(inputs * inputs, axis=-1, keepdims=True) + EPS_NORM)
    scaled_in = inputs * inverse_rms
    hidden_one = (scaled_in * norm1_gain).astype(jnp.bfloat16)
    query_raw = dot_plain(hidden_one, w_query)
    key_raw = dot_plain(hidden_one, w_key)
    value_raw = dot_plain(hidden_one, w_value)
    gate_raw = dot_plain(hidden_one, w_outgate)
    alpha_raw = dot_plain(hidden_one, w_alpha)
    beta_raw = dot_plain(hidden_one, w_beta)
    head_local = w_alpha.shape[1]
    row_start = tensor_index * part_rows
    input_rows = lax.dynamic_slice_in_dim(inputs, row_start, part_rows, 0)
    inverse_rows = lax.dynamic_slice_in_dim(inverse_rms, row_start, part_rows, 0)

    def mixer_piece(
        q_in, k_in, v_in, g_in, a_in, b_in, c_query, c_key, c_value, d_log, d_bias, o_gain
    ):
        return local_mixer(
            q_in,
            k_in,
            v_in,
            g_in,
            a_in,
            b_in,
            c_query,
            c_key,
            c_value,
            d_log,
            d_bias,
            o_gain,
            seq_count,
            head_local,
        )

    normed, mixer_back = jax.vjp(
        mixer_piece,
        query_raw,
        key_raw,
        value_raw,
        gate_raw,
        alpha_raw,
        beta_raw,
        conv_query,
        conv_key,
        conv_value,
        decay_log,
        decay_bias,
        onorm_gain,
    )
    normed_low = normed.astype(jnp.bfloat16)
    mixer_out = lax.psum(dot_plain(normed_low, w_output), "tensor")
    middle = inputs + mixer_out
    hidden_two_f, norm_two_back = jax.vjp(norm_one, middle, norm2_gain)
    hidden_two = hidden_two_f.astype(jnp.bfloat16)
    middle_rows = lax.dynamic_slice_in_dim(middle, row_start, part_rows, 0)
    gate = dot_plain(hidden_two, w_gate)
    upward = dot_plain(hidden_two, w_up)
    active, active_back = jax.vjp(swiglu, gate, upward)
    active_low = active.astype(jnp.bfloat16)
    branch_part = lax.psum_scatter(
        dot_plain(active_low, w_down).astype(jnp.bfloat16),
        "tensor",
        scatter_dimension=0,
        tiled=True,
    ).astype(jnp.float32)
    block_output = (middle_rows + branch_part).astype(jnp.bfloat16)
    cot_all = lax.all_gather(cotangent, "tensor", axis=0, tiled=True)
    down_grad = dot_left_t(active_low, cot_all)
    active_grad = dot_right_t(cot_all, w_down)
    gate_grad_f, up_grad_f = active_back(active_grad)
    gate_grad = gate_grad_f.astype(jnp.bfloat16)
    up_grad = up_grad_f.astype(jnp.bfloat16)
    gate_w_grad = dot_left_t(hidden_two, gate_grad)
    up_w_grad = dot_left_t(hidden_two, up_grad)
    hidden_two_part = dot_right_t(gate_grad, w_gate) + dot_right_t(up_grad, w_up)
    hidden_two_grad = lax.psum(hidden_two_part, "tensor")
    middle_norm_grad, norm2_whole = norm_two_back(hidden_two_grad)
    middle_grad = cot_all.astype(jnp.float32) + middle_norm_grad
    middle_low = middle_grad.astype(jnp.bfloat16)
    grad_rows = lax.dynamic_slice_in_dim(middle_grad, row_start, part_rows, 0)
    columns = jnp.arange(width)
    owned = (columns >= gain_start) & (columns < gain_start + gain_share)
    norm2_term = jnp.where(owned, norm2_whole, 0.0)
    output_w_grad = dot_left_t(normed_low, middle_low)
    normed_grad = dot_right_t(middle_low, w_output)
    (
        query_g,
        key_g,
        value_g,
        outgate_g,
        alpha_g,
        beta_g,
        convq_grad,
        convk_grad,
        convv_grad,
        dlog_grad,
        dbias_grad,
        onorm_part,
    ) = mixer_back(normed_grad)
    raw_grads = tuple(
        (
            member.astype(jnp.bfloat16)
            for member in (query_g, key_g, value_g, outgate_g, alpha_g, beta_g)
        )
    )
    proj_weights = (w_query, w_key, w_value, w_outgate, w_alpha, w_beta)
    query_w_grad = dot_left_t(hidden_one, raw_grads[0])
    key_w_grad = dot_left_t(hidden_one, raw_grads[1])
    value_w_grad = dot_left_t(hidden_one, raw_grads[2])
    outgate_w_grad = dot_left_t(hidden_one, raw_grads[3])
    alpha_w_grad = dot_left_t(hidden_one, raw_grads[4])
    beta_w_grad = dot_left_t(hidden_one, raw_grads[5])
    hidden_one_part = dot_right_t(raw_grads[0], proj_weights[0])
    for position in range(1, 6):
        hidden_one_part = hidden_one_part + dot_right_t(raw_grads[position], proj_weights[position])
    gain_one_part = jnp.sum(hidden_one_part * scaled_in, axis=0)
    hidden_one_rows, gain_one_share, onorm_share, gain_two_share = (
        lax.psum_scatter(
            hidden_one_part.astype(jnp.bfloat16), "tensor", scatter_dimension=0, tiled=True
        ).astype(jnp.float32),
        lax.psum_scatter(
            gain_one_part.astype(jnp.bfloat16), "tensor", scatter_dimension=0, tiled=True
        ).astype(jnp.float32),
        lax.psum_scatter(
            onorm_part.astype(jnp.bfloat16), "tensor", scatter_dimension=0, tiled=True
        ).astype(jnp.float32),
        lax.psum_scatter(
            norm2_term.astype(jnp.bfloat16), "tensor", scatter_dimension=0, tiled=True
        ).astype(jnp.float32),
    )
    gained = hidden_one_rows * norm1_gain
    tokens_grad = (
        grad_rows
        + inverse_rows * gained
        - input_rows * inverse_rows**3 * jnp.mean(input_rows * gained, axis=-1, keepdims=True)
    )
    (
        query_total,
        key_total,
        value_total,
        outgate_total,
        alpha_total,
        beta_total,
        output_total,
        gate_total,
        up_total,
        down_total,
    ) = (
        lax.psum_scatter(query_w_grad, "dp", scatter_dimension=0, tiled=True),
        lax.psum_scatter(key_w_grad, "dp", scatter_dimension=0, tiled=True),
        lax.psum_scatter(value_w_grad, "dp", scatter_dimension=0, tiled=True),
        lax.psum_scatter(outgate_w_grad, "dp", scatter_dimension=0, tiled=True),
        lax.psum_scatter(alpha_w_grad, "dp", scatter_dimension=0, tiled=True),
        lax.psum_scatter(beta_w_grad, "dp", scatter_dimension=0, tiled=True),
        lax.psum_scatter(output_w_grad, "dp", scatter_dimension=1, tiled=True),
        lax.psum_scatter(gate_w_grad, "dp", scatter_dimension=0, tiled=True),
        lax.psum_scatter(up_w_grad, "dp", scatter_dimension=0, tiled=True),
        lax.psum_scatter(down_grad, "dp", scatter_dimension=1, tiled=True),
    )
    (
        convq_total,
        convk_total,
        convv_total,
        dlog_total,
        dbias_total,
        onorm_total,
        gain_one_total,
        gain_two_total,
    ) = lax.psum(
        (
            convq_grad,
            convk_grad,
            convv_grad,
            dlog_grad,
            dbias_grad,
            onorm_share,
            gain_one_share,
            gain_two_share,
        ),
        "dp",
    )
    return (
        block_output,
        tokens_grad,
        gain_one_total,
        gain_two_total,
        query_total,
        key_total,
        value_total,
        outgate_total,
        alpha_total,
        beta_total,
        convq_total,
        convk_total,
        convv_total,
        dlog_total,
        dbias_total,
        onorm_total,
        output_total,
        gate_total,
        up_total,
        down_total,
    )


def solution(mesh):
    return jax.shard_map(
        per_device,
        mesh=mesh,
        in_specs=(
            P("dp", None),
            P(("dp", "tensor"), None),
            P(),
            P(),
            P("dp", "tensor"),
            P("dp", "tensor"),
            P("dp", "tensor"),
            P("dp", "tensor"),
            P("dp", "tensor"),
            P("dp", "tensor"),
            P(None, "tensor"),
            P(None, "tensor"),
            P(None, "tensor"),
            P("tensor"),
            P("tensor"),
            P(),
            P("tensor", "dp"),
            P("dp", "tensor"),
            P("dp", "tensor"),
            P("tensor", "dp"),
        ),
        out_specs=(
            P(("dp", "tensor"), None),
            P(("dp", "tensor"), None),
            P("tensor"),
            P("tensor"),
            P("dp", "tensor"),
            P("dp", "tensor"),
            P("dp", "tensor"),
            P("dp", "tensor"),
            P("dp", "tensor"),
            P("dp", "tensor"),
            P(None, "tensor"),
            P(None, "tensor"),
            P(None, "tensor"),
            P("tensor"),
            P("tensor"),
            P("tensor"),
            P("tensor", "dp"),
            P("dp", "tensor"),
            P("dp", "tensor"),
            P("tensor", "dp"),
        ),
        check_vma=False,
    )
```

profile of v0, /device:TPU:0, one launch (start us, length us, event | category | flops | bytes accessed | tf_op | source)
XLA Modules:
  0.0 2340.9 jit_solution(16562086644421391141)
XLA Ops:
  12.8 34.0 %all_gather.34 = bf16[1024,256]{1,0:T(8,128)(2,1)S(1)} all-gather(bf16[128,256]{1,0:T(8,128)(2,1)S(1)} %copy-done.109), channel_id=1, replica_groups=mesh['dp'=8,'tensor'=4] {'dp'}, dimensions={0}, use_global_device_ids=true | all-gather | bytes 589824 | tf_op jit(solution)/shard_map/all_gather | solution.py:199
  64.3 19.8 all_gather.33
  88.2 16.2 all_gather.35
  159.3 31.2 %all_gather.37 = bf16[1024,256]{1,0:T(8,128)(2,1)S(1)} all-gather(bf16[128,256]{1,0:T(8,128)(2,1)S(1)} %copy-done.110), channel_id=1, replica_groups=mesh['dp'=8,'tensor'=4] {'dp'}, dimensions={0}, use_global_device_ids=true | all-gather | bytes 589824 | tf_op jit(solution)/shard_map/all_gather | solution.py:198
  282.5 197.2 %while.42 = (s32[]{:T(128)}, f32[1,2,128,256]{3,2,1,0:T(8,128)S(1)}, f32[32,1,2,64,256]{4,3,2,1,0:T(8,128)}, f32[32,1,2,128,256]{4,3,2,1,0:T(8,128)}, f32[32,1,2...) while((s32[]{:T(128)}, ...), condition=%wide.region_5.6_spmd.clone, body=%wide.region_4.5_spmd.clone.sunk | while | flops 176619520 | bytes 2756254 | solution.py:116
  516.5 149.1 %all-reduce.39.cloned.1.call-done = f32[2048,1024]{1,0:T(8,128)} async-done(((f32[2048,1024]{1,0:T(8,128)}), f32[2048,1024]{1,0:T(8,128)}) %all-reduce.39.cloned.1.call-update) | async-done | bytes 8388624 | tf_op jit(solution)/shard_map/psum | solution.py:260
  677.6 33.9 %all-gather.14.cloned.1.call-done = bf16[1024,704]{0,1:T(8,128)(2,1)} async-done(((bf16[128,704]{0,1:T(8,128)(2,1)}), bf16[1024,704]{0,1:T(8,128)(2,1)}) %all-gather.14.cloned.1.call-update) | async-done | bytes 1441808 | tf_op jit(solution)/shard_map/all_gather | solution.py:205
  719.8 35.8 %all-gather.16.cloned.1.call-done = bf16[1024,704]{0,1:T(8,128)(2,1)} async-done(((bf16[128,704]{0,1:T(8,128)(2,1)}), bf16[1024,704]{0,1:T(8,128)(2,1)}) %all-gather.16.cloned.1.call-update) | async-done | bytes 1441808 | tf_op jit(solution)/shard_map/all_gather | solution.py:206
  764.0 36.0 %all-gather.18.cloned.1.call-done = bf16[704,1024]{1,0:T(8,128)(2,1)} async-done(((bf16[704,128]{1,0:T(8,128)(2,1)}), bf16[704,1024]{1,0:T(8,128)(2,1)}) %all-gather.18.cloned.1.call-update) | async-done | bytes 1441808 | tf_op jit(solution)/shard_map/all_gather | solution.py:207
  799.9 34.5 %all-gather.20.cloned.1.call-done = bf16[2048,1024]{1,0:T(8,128)(2,1)} async-done(((bf16[512,1024]{1,0:T(8,128)(2,1)}), bf16[2048,1024]{1,0:T(8,128)(2,1)}) %all-gather.20.cloned.1.call-update) | async-done | bytes 4194320 | tf_op jit(solution)/shard_map/all_gather | solution.py:276
  834.4 11.8 multiply_convert_fusion.2
  871.6 137.3 %all-reduce.41.cloned.1.call-done = f32[2048,1024]{1,0:T(8,128)} async-done(((f32[2048,1024]{1,0:T(8,128)}), f32[2048,1024]{1,0:T(8,128)}) %all-reduce.41.cloned.1.call-update) | async-done | bytes 8388624 | tf_op jit(solution)/shard_map/psum | solution.py:285
  1023.0 11.3 fusion.69
  1057.8 347.6 %while.43 = (s32[]{:T(128)}, f32[1,2,128,256]{2,3,1,0:T(8,128)S(1)}, f32[32,1,2,64,128]{4,3,2,1,0:T(8,128)}, f32[32,1,2,64,256]{4,3,2,1,0:T(8,128)}, f32[32,1,2,...) while((s32[]{:T(128)}, ...), condition=%wide.region_15.16_spmd.clone, body=%wide.region_13.15_spmd.clone.sunk | while | flops 403177472 | bytes 7832851 | solution.py:116
  1405.4 12.5 fusion.74
  1697.4 18.4 multiply_reduce_fusion.2
  1787.7 38.1 %all-reduce.34 = (f32[256]{0:T(256)}, f32[256]{0:T(256)}, f32[4,256]{1,0:T(4,128)}, f32[4,256]{1,0:T(4,128)}, f32[4,512]{1,0:T(4,128)}, /*index=5*/f32[2]{0:T(128)}, f32[2]{0:T(128)}, f32[64]{0:T(128)}) all-reduce(f32[256]{0:T(256)S(1)} %dynamic-slice_convert_fusion.2, ...), channel_id=1, replica_groups=mesh['dp'=8,'tensor'=4] {'dp'}, use_global_device_ids=true, to_apply=%region_31.32 | all-reduce | flops 4676 | bytes 37408 | tf_op jit(solution)/shard_map/psum | solution.py:378
  1838.5 74.0 %reduce-scatter.33.cloned.1.call-done = f32[128,704]{0,1:T(8,128)} async-done(((f32[1024,704]{0,1:T(8,128)}), f32[128,704]{0,1:T(8,128)}) %reduce-scatter.33.cloned.1.call-update) | async-done | bytes 360464 | tf_op jit(solution)/shard_map/reduce_scatter | solution.py:366
  1912.5 75.4 %reduce-scatter.35.cloned.1.call-done = f32[704,128]{1,0:T(8,128)} async-done(((f32[704,1024]{1,0:T(8,128)}), f32[704,128]{1,0:T(8,128)}) %reduce-scatter.35.cloned.1.call-update) | async-done | bytes 360464 | tf_op jit(solution)/shard_map/reduce_scatter | solution.py:367
  1988.0 66.5 %reduce-scatter.23.cloned.1.call-done = f32[128,256]{1,0:T(8,128)} async-done(((f32[1024,256]{1,0:T(8,128)}), f32[128,256]{1,0:T(8,128)}) %reduce-scatter.23.cloned.1.call-update) | async-done | bytes 131088 | tf_op jit(solution)/shard_map/reduce_scatter | solution.py:359
  2054.5 66.7 %reduce-scatter.21.cloned.1.call-done = f32[128,256]{1,0:T(8,128)} async-done(((f32[1024,256]{1,0:T(8,128)}), f32[128,256]{1,0:T(8,128)}) %reduce-scatter.21.cloned.1.call-update) | async-done | bytes 131088 | tf_op jit(solution)/shard_map/reduce_scatter | solution.py:358
  2121.2 71.2 %reduce-scatter.29.cloned.1.call-done = f32[512,128]{1,0:T(8,128)} async-done(((f32[512,1024]{1,0:T(8,128)}), f32[512,128]{1,0:T(8,128)}) %reduce-scatter.29.cloned.1.call-update) | async-done | bytes 262160 | tf_op jit(solution)/shard_map/reduce_scatter | solution.py:364
  2192.5 70.6 %reduce-scatter.25.cloned.1.call-done = f32[128,512]{1,0:T(8,128)} async-done(((f32[1024,512]{1,0:T(8,128)}), f32[128,512]{1,0:T(8,128)}) %reduce-scatter.25.cloned.1.call-update) | async-done | bytes 262160 | tf_op jit(solution)/shard_map/reduce_scatter | solution.py:360
  2263.1 70.8 %reduce-scatter.27.cloned.1.call-done = f32[128,512]{1,0:T(8,128)} async-done(((f32[1024,512]{1,0:T(8,128)}), f32[128,512]{1,0:T(8,128)}) %reduce-scatter.27.cloned.1.call-update) | async-done | bytes 262160 | tf_op jit(solution)/shard_map/reduce_scatter | solution.py:361
  (1412 shorter events, 1204.2 us)
Async XLA Ops:
  7.2 243.4 %all-gather.8.cloned.1.call-start = ((), (), s32[]{:S(2)}) async-start(), calls=%async_computation.12 | async-start | bytes 1179648 | tf_op jit(solution)/shard_map/all_gather | solution.py:200
  7.9 488.0 %all-gather.10.cloned.1.call-start = ((), (), s32[]{:S(2)}) async-start(), calls=%async_computation.13 | async-start | bytes 1179648 | tf_op jit(solution)/shard_map/all_gather | solution.py:201
  8.7 497.4 %all-gather.12.cloned.1.call-start = ((), (), s32[]{:S(2)}) async-start(), calls=%async_computation.14 | async-start | bytes 1179648 | tf_op jit(solution)/shard_map/all_gather | solution.py:204
  9.4 656.2 %all-reduce.39.cloned.1.call-start = ((), (), s32[]{:S(2)}) async-start(), calls=%async_computation.15 | async-start | bytes 16777216 | tf_op jit(solution)/shard_map/psum | solution.py:260
  58.4 166.9 %copy-start.88 = (pred[64,64]{0,1:T(8,128)(4,1)}, pred[64,64]{0,1:T(8,128)(4,1)S(1)}, u32[]{:S(2)}) copy-start(pred[64,64]{0,1:T(8,128)(4,1)S(1)} %get-tuple-element.784) | copy-start | bytes 12292
  58.4 166.9 %copy-start.96 = (pred[64,64]{0,1:T(8,128)(4,1)}, pred[64,64]{0,1:T(8,128)(4,1)S(1)}, u32[]{:S(2)}) copy-start(pred[64,64]{0,1:T(8,128)(4,1)S(1)} %get-tuple-element.785) | copy-start | bytes 12292
  58.5 187.2 %copy-start.75 = (f32[64,64]{0,1:T(8,128)}, f32[64,64]{0,1:T(8,128)S(1)}, u32[]{:S(2)}) copy-start(f32[64,64]{0,1:T(8,128)S(1)} %fusion.209) | copy-start | bytes 49156
  513.7 197.8 %all-gather.14.cloned.1.call-start = ((), (), s32[]{:S(2)}) async-start(), calls=%async_computation.16 | async-start | bytes 1622016 | tf_op jit(solution)/shard_map/all_gather | solution.py:205
  514.3 241.3 %all-gather.16.cloned.1.call-start = ((), (), s32[]{:S(2)}) async-start(), calls=%async_computation.17 | async-start | bytes 1622016 | tf_op jit(solution)/shard_map/all_gather | solution.py:206
  514.9 285.0 %all-gather.18.cloned.1.call-start = ((), (), s32[]{:S(2)}) async-start(), calls=%async_computation.18 | async-start | bytes 1622016 | tf_op jit(solution)/shard_map/all_gather | solution.py:207
  515.7 318.7 %all-gather.20.cloned.1.call-start = ((), (), s32[]{:S(2)}) async-start(), calls=%async_computation.20 | async-start | bytes 5242880 | tf_op jit(solution)/shard_map/all_gather | solution.py:276
  516.4 492.5 %all-reduce.41.cloned.1.call-start = ((), (), s32[]{:S(2)}) async-start(), calls=%async_computation.21 | async-start | bytes 16777216 | tf_op jit(solution)/shard_map/psum | solution.py:285
  855.9 969.9 %reduce-scatter.39.cloned.1.call-start = ((), (), s32[]{:S(2)}) async-start(), calls=%async_computation.32 | async-start | bytes 589824
  1517.2 310.1 %reduce-scatter.37.cloned.1.call-start = ((), (), s32[]{:S(2)}) async-start(), calls=%async_computation.31 | async-start | bytes 589824
  1522.2 306.5 %reduce-scatter.17.cloned.1.call-start = ((), (), s32[]{:S(2)}) async-start(), calls=%async_computation.19 | async-start | bytes 5242880 | tf_op jit(solution)/shard_map/reduce_scatter | solution.py:269
  1530.0 301.9 %reduce-scatter.19.cloned.1.call-start = ((), (), s32[]{:S(2)}) async-start(), calls=%async_computation.22 | async-start | bytes 5242880 | tf_op jit(solution)/shard_map/reduce_scatter | solution.py:327
  1715.8 122.7 %reduce-scatter.31.cloned.1.call-start = ((), (), s32[]{:S(2)}) async-start(), calls=%async_computation.28 | async-start | bytes 3244032 | tf_op jit(solution)/shard_map/reduce_scatter | solution.py:365
  1723.6 188.9 %reduce-scatter.33.cloned.1.call-start = ((), (), s32[]{:S(2)}) async-start(), calls=%async_computation.29 | async-start | bytes 3244032 | tf_op jit(solution)/shard_map/reduce_scatter | solution.py:366
  1732.5 255.5 %reduce-scatter.35.cloned.1.call-start = ((), (), s32[]{:S(2)}) async-start(), calls=%async_computation.30 | async-start | bytes 3244032 | tf_op jit(solution)/shard_map/reduce_scatter | solution.py:367
  1741.0 313.5 %reduce-scatter.23.cloned.1.call-start = ((), (), s32[]{:S(2)}) async-start(), calls=%async_computation.24 | async-start | bytes 1179648 | tf_op jit(solution)/shard_map/reduce_scatter | solution.py:359
  1745.5 375.7 %reduce-scatter.21.cloned.1.call-start = ((), (), s32[]{:S(2)}) async-start(), calls=%async_computation.23 | async-start | bytes 1179648 | tf_op jit(solution)/shard_map/reduce_scatter | solution.py:358
  1750.2 442.3 %reduce-scatter.29.cloned.1.call-start = ((), (), s32[]{:S(2)}) async-start(), calls=%async_computation.27 | async-start | bytes 2359296 | tf_op jit(solution)/shard_map/reduce_scatter | solution.py:364
  1757.5 505.6 %reduce-scatter.25.cloned.1.call-start = ((), (), s32[]{:S(2)}) async-start(), calls=%async_computation.25 | async-start | bytes 2359296 | tf_op jit(solution)/shard_map/reduce_scatter | solution.py:360
  1765.1 568.8 %reduce-scatter.27.cloned.1.call-start = ((), (), s32[]{:S(2)}) async-start(), calls=%async_computation.26 | async-start | bytes 2359296 | tf_op jit(solution)/shard_map/reduce_scatter | solution.py:361
  (171 other events, 1875.2 us)
Sparse Core Ops, SparseCore 0:
  10.2 44.4 all-gather.7
  56.8 38.9 all-gather.9
  97.8 38.2 all-gather.11
  513.9 151.6 all-reduce.38
  667.5 43.9 all-gather.13
  713.4 42.1 all-gather.15
  757.7 42.1 all-gather.17
  801.5 32.8 all-gather.19
  856.0 152.8 all-reduce.40
  1517.3 62.0 reduce-scatter.38
  1583.1 60.8 reduce-scatter.36
  1646.4 43.5 reduce-scatter.16
  1715.9 44.7 reduce-scatter.18
  1764.7 72.4 reduce-scatter.30
  1841.2 71.3 reduce-scatter.32
  1916.5 71.4 reduce-scatter.34
  1991.8 62.6 reduce-scatter.22
  2058.7 62.4 reduce-scatter.20
  2125.3 67.0 reduce-scatter.28
  2196.4 66.6 reduce-scatter.24
  2267.2 66.6 reduce-scatter.26
where the time goes:
time: 2360 us; the launch traced here: 2340 us
  waiting for transfers between devices  927 us (39%)
  matrix products  738 us (31%)
  local copies, waits for them, and re-layouts  324 us (14%)
  other arithmetic  184 us (8%)
  blocking collectives  145 us (6%)
    dot_general x353, matrix products, matmul_high(): jnp.einsum('...ij,...jk->...ik', left_side, right_side, precision=HIGH)  423 us
    psum x1, waiting for transfers between devices, per_device(): mixer_out = lax.psum(dot_plain(normed_low, w_output), 'tensor')  149 us
    psum x1, waiting for transfers between devices, per_device(): hidden_two_grad = lax.psum(hidden_two_part, 'tensor')  137 us
    squeeze x160, local copies, waits for them, and re-layouts, delta_rule(): final_state, outputs = lax.scan(jax.checkpoint(advance), start, sequence)  114 us
    dot_general x96, matrix products, advance(): jnp.einsum('...ck,...cv->...kv', fade_now, fresh, precision=HIGH)  83.8 us
    dot_general x10, matrix products, dot_right_t(): lax.dot_general(left_side, right_side, (((1,), (1,)), ((), ())), preferre...  76.2 us
    reduce_scatter x1, waiting for transfers between devices, per_device(): lax.psum_scatter(down_grad, 'dp', scatter_dimension=1, tiled=True)  75.4 us
    reduce_scatter x1, waiting for transfers between devices, per_device(): lax.psum_scatter(up_w_grad, 'dp', scatter_dimension=0, tiled=True)  74 us
  transfers between devices with their start and end apart: 21, of which 13 were waited for; matrix products, arithmetic and copies ran while one was open for 29% of the time, Pallas kernels for 0%

commit v1 on v0

v1 whole, which is shorter than its diff:
```python
import functools
import jax
import jax.numpy as jnp
from jax import lax
from jax.sharding import PartitionSpec as P
from jax.experimental import pallas as pl
from jax.experimental.pallas import tpu as pltpu

SEQ = 2048
BLOCK = 256
HALF = 128
EPS_NORM = 1e-05
EPS_UNIT = 1e-06
BF = jnp.bfloat16
F32 = jnp.float32
HIGH = lax.Precision.HIGHEST


def mm(left, right):
    return lax.dot_general(
        left.astype(BF), right.astype(BF), (((1,), (0,)), ((), ())), preferred_element_type=F32
    )


def mm_nt(left, right):
    return lax.dot_general(
        left.astype(BF), right.astype(BF), (((1,), (1,)), ((), ())), preferred_element_type=F32
    )


def mm_tn(left, right):
    return lax.dot_general(
        left.astype(BF), right.astype(BF), (((0,), (0,)), ((), ())), preferred_element_type=F32
    )


def mm_exact(left, right):
    return lax.dot_general(
        left, right, (((1,), (0,)), ((), ())), precision=HIGH, preferred_element_type=F32
    )


def iota2(rows, columns):
    return (
        lax.broadcasted_iota(jnp.int32, (rows, columns), 0),
        lax.broadcasted_iota(jnp.int32, (rows, columns), 1),
    )


def unit_lower_inverse(blocks):
    size = blocks[0].shape[0]
    row, col = iota2(size, size)
    eye = jnp.where(row == col, 1.0, 0.0).astype(F32)
    first = jnp.where((row ^ col) == 1, 1.0, 0.0).astype(F32)
    results = [eye - block * first for block in blocks]
    lows = [block.astype(BF) for block in blocks]
    shift = 1
    while (1 << shift) < size:
        mask = jnp.where(((row >> shift) ^ (col >> shift)) == 1, 1.0, 0.0).astype(BF)
        halves = [result.astype(BF) for result in results]
        inner = [mm(low * mask, half).astype(BF) for low, half in zip(lows, halves)]
        results = [
            result - mm(half, part) for result, half, part in zip(results, halves, inner)
        ]
        shift += 1
    return results


def softplus(value):
    return jnp.maximum(value, 0.0) + jnp.log1p(jnp.exp(-jnp.abs(value)))


def lower_ones(size):
    row, col = iota2(size, size)
    return jnp.where(row >= col, 1.0, 0.0).astype(F32)


def fades(total, total_t, index):
    row, col = iota2(BLOCK, BLOCK)
    gaps = total[:, index : index + 1] - total_t[index : index + 1, :]
    fading = jnp.exp(jnp.where(row >= col, gaps, -1e30))
    return fading, row > col


def forward_kernel(
    heads,
    per_seq,
    x_ref,
    gain_ref,
    w_ref,
    taps_ref,
    rate_ref,
    bias_ref,
    onorm_ref,
    hidden_ref,
    raw_ref,
    normed_ref,
    mixed_ref,
    state_ref,
    inv_ref,
    solved_ref,
    query_eff_ref,
    keyw_ref,
    carry_ref,
    ext_ref,
):
    key_dim = state_ref.shape[2]
    value_dim = state_ref.shape[3]
    qk = heads * key_dim
    conv_width = taps_ref.shape[1]
    gate_at = conv_width
    small_at = gate_at + heads * value_dim
    step = pl.program_id(0)

    @pl.when(step % per_seq == 0)
    def _():
        carry_ref[...] = jnp.zeros_like(carry_ref)
        ext_ref[0:8, :] = jnp.zeros((8, conv_width), F32)

    @pl.when(step % per_seq != 0)
    def _():
        ext_ref[0:8, :] = ext_ref[BLOCK : BLOCK + 8, :]

    inputs = x_ref[...].astype(F32)
    inverse = lax.rsqrt(jnp.mean(inputs * inputs, axis=-1, keepdims=True) + EPS_NORM)
    hidden = (inputs * inverse * gain_ref[...]).astype(BF)
    hidden_ref[...] = hidden
    ext_ref[8:, :] = mm(hidden, w_ref[:, :conv_width])
    raw_ref[:, :conv_width] = ext_ref[8:, :]
    raw_ref[:, gate_at:] = mm(hidden, w_ref[:, gate_at:])

    small = raw_ref[:, small_at:]
    betas = jax.nn.sigmoid(small)
    decays = -rate_ref[...] * softplus(small + bias_ref[...])
    total = mm_exact(lower_ones(BLOCK), decays)
    total_t = total.T

    def conv(start, width):
        acc = taps_ref[0:1, start : start + width] * ext_ref[pl.ds(5, BLOCK), start : start + width]
        for tap in range(1, 4):
            acc = acc + (
                taps_ref[tap : tap + 1, start : start + width]
                * ext_ref[pl.ds(5 + tap, BLOCK), start : start + width]
            )
        return acc * jax.nn.sigmoid(acc)

    def unit(value):
        return value * lax.rsqrt(jnp.sum(value * value, axis=-1, keepdims=True) + EPS_UNIT)

    parts = []
    for head in range(heads):
        query = unit(conv(head * key_dim, key_dim)) * key_dim ** (-0.5)
        keys = unit(conv(qk + head * key_dim, key_dim))
        values = conv(2 * qk + head * value_dim, value_dim)
        beta = betas[:, heads + head : heads + head + 1]
        fading, strict = fades(total, total_t, head)
        key_low = keys.astype(BF)
        coupling = jnp.where(strict, beta * fading * mm_nt(key_low, key_low), 0.0)
        scores = (mm_nt(query, key_low) * fading).astype(BF)
        parts.append((query, keys, values, beta, coupling, scores))
    blocks = []
    for part in parts:
        coupling = part[4]
        blocks += [coupling[:HALF, :HALF], coupling[HALF:, HALF:]]
    inverses = unit_lower_inverse(blocks)
    for head in range(heads):
        query, keys, values, beta, coupling, scores = parts[head]
        top, bottom = inverses[2 * head], inverses[2 * head + 1]
        cross = -mm(bottom, mm(coupling[HALF:, :HALF], top))
        inverse_low = jnp.concatenate(
            [
                jnp.concatenate([top.astype(BF), jnp.zeros((HALF, HALF), BF)], axis=1),
                jnp.concatenate([cross.astype(BF), bottom.astype(BF)], axis=1),
            ],
            axis=0,
        )
        inv_ref[0, head] = inverse_low
        column = total[:, head : head + 1]
        last = total[BLOCK - 1 :, head : head + 1]
        grown = jnp.exp(column)
        targets = jnp.concatenate(
            [(((beta * grown) * keys)).astype(BF), (beta * values).astype(BF)], axis=1
        )
        solved = mm(inverse_low, targets)
        solved_low = solved.astype(BF)
        solved_ref[0, head] = solved_low
        spread = mm(scores, solved_low)
        query_eff = (query * grown - spread[:, :key_dim]).astype(BF)
        query_eff_ref[0, head] = query_eff
        key_fade = keys * jnp.exp(last - column)
        gathered = mm_tn(key_fade, solved_low)
        keyw = gathered[:, :key_dim].astype(BF)
        keyw_ref[0, head] = keyw
        state = carry_ref[head]
        state_ref[0, head] = state
        state_low = state.astype(BF)
        mixed = mm(query_eff, state_low) + spread[:, key_dim:]
        carry_ref[head] = jnp.exp(last) * state - mm(keyw, state_low) + gathered[:, key_dim:]
        span = slice(head * value_dim, (head + 1) * value_dim)
        mixed_ref[:, span] = mixed
        gate = raw_ref[:, gate_at + head * value_dim : gate_at + (head + 1) * value_dim]
        scale = lax.rsqrt(jnp.mean(mixed * mixed, axis=-1, keepdims=True) + EPS_NORM)
        normed_ref[:, span] = (
            mixed * scale * onorm_ref[...] * (gate * jax.nn.sigmoid(gate))
        ).astype(BF)


def mixer_forward(tokens, gain, weights, taps, rate, bias, onorm, heads):
    rows, width = tokens.shape
    total_width = weights.shape[1]
    conv_width = taps.shape[1]
    value_dim = onorm.shape[1]
    value_all = heads * value_dim
    key_dim = (conv_width - value_all) // (2 * heads)
    steps = rows // BLOCK
    whole = lambda shape: pl.BlockSpec(shape, lambda i: (0,) * len(shape))
    rows_of = lambda columns: pl.BlockSpec((BLOCK, columns), lambda i: (i, 0))
    each = lambda a, b: pl.BlockSpec((1, heads, a, b), lambda i: (i, 0, 0, 0))
    shape = jax.ShapeDtypeStruct
    return pl.pallas_call(
        functools.partial(forward_kernel, heads, SEQ // BLOCK),
        grid=(steps,),
        in_specs=[
            rows_of(width),
            whole((1, width)),
            whole((width, total_width)),
            whole(taps.shape),
            whole(rate.shape),
            whole(bias.shape),
            whole(onorm.shape),
        ],
        out_specs=[
            rows_of(width),
            rows_of(total_width),
            rows_of(value_all),
            rows_of(value_all),
            each(key_dim, value_dim),
            each(BLOCK, BLOCK),
            each(BLOCK, key_dim + value_dim),
            each(BLOCK, key_dim),
            each(key_dim, key_dim),
        ],
        out_shape=[
            shape((rows, width), BF),
            shape((rows, total_width), F32),
            shape((rows, value_all), BF),
            shape((rows, value_all), F32),
            shape((steps, heads, key_dim, value_dim), F32),
            shape((steps, heads, BLOCK, BLOCK), BF),
            shape((steps, heads, BLOCK, key_dim + value_dim), BF),
            shape((steps, heads, BLOCK, key_dim), BF),
            shape((steps, heads, key_dim, key_dim), BF),
        ],
        scratch_shapes=[
            pltpu.VMEM((heads, key_dim, value_dim), F32),
            pltpu.VMEM((BLOCK + 8, conv_width), F32),
        ],
        compiler_params=pltpu.CompilerParams(
            dimension_semantics=("arbitrary",), vmem_limit_bytes=56 * 1024 * 1024
        ),
        name="mixer_forward",
    )(tokens, gain, weights, taps, rate, bias, onorm)


def backward_kernel(
    heads,
    per_seq,
    place_ref,
    dmix_ref,
    wout_ref,
    raw_ref,
    halo_ref,
    mixed_ref,
    state_ref,
    inv_ref,
    solved_ref,
    query_eff_ref,
    keyw_ref,
    taps_ref,
    rate_ref,
    bias_ref,
    onorm_ref,
    draw_ref,
    dtaps_ref,
    dsmall_ref,
    donorm_ref,
    carry_ref,
    ext_ref,
    dext_ref,
):
    key_dim = state_ref.shape[2]
    value_dim = state_ref.shape[3]
    qk = heads * key_dim
    conv_width = taps_ref.shape[1]
    gate_at = conv_width
    small_at = gate_at + heads * value_dim
    step = pl.program_id(0)
    block = pl.num_programs(0) - 1 - step

    @pl.when(step == 0)
    def _():
        dtaps_ref[...] = jnp.zeros_like(dtaps_ref)
        dsmall_ref[...] = jnp.zeros_like(dsmall_ref)
        donorm_ref[...] = jnp.zeros_like(donorm_ref)

    @pl.when(step % per_seq == 0)
    def _():
        carry_ref[...] = jnp.zeros_like(carry_ref)
        dext_ref[BLOCK:, :] = jnp.zeros((8, conv_width), F32)

    @pl.when(step % per_seq != 0)
    def _():
        dext_ref[BLOCK:, :] = dext_ref[0:8, :]

    keep = jnp.where(block % per_seq == 0, 0.0, 1.0)
    ext_ref[0:8, :] = halo_ref[:, :conv_width] * keep
    ext_ref[8:, :] = raw_ref[:, :conv_width]

    small = raw_ref[:, small_at:]
    betas = jax.nn.sigmoid(small)
    shifted = small + bias_ref[...]
    decays = -rate_ref[...] * softplus(shifted)
    lower = lower_ones(BLOCK)
    total = mm_exact(lower, decays)
    total_t = total.T
    lane = lax.broadcasted_iota(jnp.int32, (1, HALF), 1)
    ones = jnp.ones((1, BLOCK), F32)

    def conv(start, width):
        acc = taps_ref[0:1, start : start + width] * ext_ref[pl.ds(5, BLOCK), start : start + width]
        for tap in range(1, 4):
            acc = acc + (
                taps_ref[tap : tap + 1, start : start + width]
                * ext_ref[pl.ds(5 + tap, BLOCK), start : start + width]
            )
        sig = jax.nn.sigmoid(acc)
        return acc * sig, sig * (1.0 + acc * (1.0 - sig))

    def back_unit(value, scale, grad):
        along = jnp.sum(value * grad, axis=-1, keepdims=True)
        return scale * grad - value * (scale * scale * scale * along)

    def inv_norm(value):
        return lax.rsqrt(jnp.sum(value * value, axis=-1, keepdims=True) + EPS_UNIT)

    small_grad = jnp.zeros((BLOCK, HALF), F32)
    total_grad = jnp.zeros((BLOCK, HALF), F32)
    col_rows = []
    dnormed = mm(dmix_ref[...], wout_ref[...])
    for head in range(heads):
        span = slice(head * value_dim, (head + 1) * value_dim)
        gate = raw_ref[:, gate_at + head * value_dim : gate_at + (head + 1) * value_dim]
        sig = jax.nn.sigmoid(gate)
        silu = gate * sig
        mixed = mixed_ref[:, span]
        scale = lax.rsqrt(jnp.mean(mixed * mixed, axis=-1, keepdims=True) + EPS_NORM)
        unit_mixed = mixed * scale
        grad = dnormed[:, span]
        onorm = onorm_ref[...]
        grad_unit = grad * unit_mixed
        donorm_ref[...] += jnp.sum(grad_unit * silu, axis=0, keepdims=True)
        draw_ref[:, gate_at + head * value_dim : gate_at + (head + 1) * value_dim] = (
            grad_unit * onorm * (sig * (1.0 + gate * (1.0 - sig)))
        ).astype(BF)
        grad_on = grad * onorm * silu
        along = jnp.mean(mixed * grad_on, axis=-1, keepdims=True)
        dmixed = scale * grad_on - mixed * (scale * scale * scale * along)
        dmixed_low = dmixed.astype(BF)

        query_pre, query_slope = conv(head * key_dim, key_dim)
        key_pre, key_slope = conv(qk + head * key_dim, key_dim)
        values, value_slope = conv(2 * qk + head * value_dim, value_dim)
        query_scale = inv_norm(query_pre)
        key_scale = inv_norm(key_pre)
        factor = key_dim ** (-0.5)
        query = query_pre * query_scale * factor
        keys = key_pre * key_scale
        beta = betas[:, heads + head : heads + head + 1]
        fading, strict = fades(total, total_t, head)
        query_low = query.astype(BF)
        key_low = keys.astype(BF)
        key_key = jnp.where(strict, mm_nt(key_low, key_low) * fading, 0.0)
        scores = mm_nt(query_low, key_low) * fading
        scores_low = scores.astype(BF)
        column = total[:, head : head + 1]
        last = total[BLOCK - 1 :, head : head + 1]
        grown = jnp.exp(column)
        rest = jnp.exp(last - column)
        key_fade = keys * rest
        key_fade_low = key_fade.astype(BF)

        state = state_ref[0, head]
        state_low = state.astype(BF)
        dstate = carry_ref[head]
        dstate_low = dstate.astype(BF)
        solved_low = solved_ref[0, head]
        key_part = solved_low[:, :key_dim]
        fresh = solved_low[:, key_dim:].astype(F32) - mm(key_part, state_low)
        fresh_low = fresh.astype(BF)
        dfresh = mm_tn(scores_low, dmixed_low) + mm(key_fade_low, dstate_low)
        dfresh_low = dfresh.astype(BF)
        carry_ref[head] = (
            jnp.exp(last) * dstate
            - mm_tn(keyw_ref[0, head], dstate_low)
            + mm_tn(query_eff_ref[0, head], dmixed_low)
        )
        dlast = jnp.exp(last) * jnp.sum(
            jnp.sum(state * dstate, axis=1, keepdims=True), axis=0, keepdims=True
        )
        dscores = mm_nt(dmixed_low, fresh_low)
        dquery_fade = mm_nt(dmixed_low, state_low)
        dkey_fade = mm_nt(fresh_low, dstate_low)
        dkey_part = -mm_nt(dfresh_low, state_low)
        dsolved = jnp.concatenate([dkey_part.astype(BF), dfresh_low], axis=1)
        dtargets = mm_tn(inv_ref[0, head], dsolved)
        dcoupling = -mm_nt(dtargets, solved_low)
        dkey_target = dtargets[:, :key_dim]
        dvalue_target = dtargets[:, key_dim:]

        pair = dcoupling * key_key
        dfade = beta * pair + dscores * scores
        dpair = (jnp.where(strict, dcoupling * (beta * fading), 0.0)).astype(BF)
        dquery_key = (dscores * fading).astype(BF)
        dquery = dquery_fade * grown + mm(dquery_key, key_low)
        fade_rows = jnp.sum(dkey_fade * key_fade, axis=-1, keepdims=True)
        grown_key = grown * keys
        target_rows = jnp.sum(dkey_target * grown_key, axis=-1, keepdims=True)
        dkeys = (
            dkey_fade * rest
            + dkey_target * (beta * grown)
            + mm(dpair, key_low)
            + mm_tn(dpair, key_low)
            + mm_tn(dquery_key, query_low)
        )
        dvalues = dvalue_target * beta
        dbeta = (
            jnp.sum(pair, axis=-1, keepdims=True)
            + target_rows
            + jnp.sum(dvalue_target * values, axis=-1, keepdims=True)
        )
        row_part = (
            jnp.sum(dfade, axis=-1, keepdims=True)
            + beta * target_rows
            + jnp.sum(dquery_fade * query, axis=-1, keepdims=True) * grown
            - fade_rows
        )
        dlast = dlast + jnp.sum(fade_rows, axis=0, keepdims=True)
        place = lax.broadcasted_iota(jnp.int32, (BLOCK, 1), 0)
        row_part = row_part + jnp.where(place == BLOCK - 1, dlast, 0.0)
        col_rows.append(jnp.sum(dfade, axis=0, keepdims=True))
        total_grad = total_grad + jnp.where(lane == head, row_part, 0.0)
        small_grad = small_grad + jnp.where(lane == heads + head, dbeta, 0.0)

        dquery_pre = back_unit(query_pre, query_scale, dquery * factor) * query_slope
        dkey_pre = back_unit(key_pre, key_scale, dkeys) * key_slope
        dext_ref[0:BLOCK, head * key_dim : (head + 1) * key_dim] = dquery_pre
        dext_ref[0:BLOCK, qk + head * key_dim : qk + (head + 1) * key_dim] = dkey_pre
        dext_ref[
            0:BLOCK, 2 * qk + head * value_dim : 2 * qk + (head + 1) * value_dim
        ] = dvalues * value_slope

    filler = jnp.zeros((HALF - heads, BLOCK), F32)
    total_grad = total_grad - jnp.concatenate(col_rows + [filler], axis=0).T
    row, col = iota2(BLOCK, BLOCK)
    upper = jnp.where(row <= col, 1.0, 0.0).astype(F32)
    ddecay = mm_exact(upper, total_grad)
    dalpha = ddecay * (-rate_ref[...]) * jax.nn.sigmoid(shifted)
    dsmall_ref[0:1, :] += jnp.sum(ddecay * decays, axis=0, keepdims=True)
    dsmall_ref[1:2, :] += jnp.sum(dalpha, axis=0, keepdims=True)
    draw_ref[:, small_at:] = (
        jnp.where(lane < heads, dalpha, small_grad * betas * (1.0 - betas))
    ).astype(BF)

    width = HALF
    for start in range(0, conv_width, width):
        span = slice(start, start + width)
        grad = dext_ref[0:BLOCK, span]
        acc = taps_ref[3:4, span] * grad
        for tap in range(3):
            acc = acc + taps_ref[tap : tap + 1, span] * dext_ref[pl.ds(3 - tap, BLOCK), span]
        draw_ref[:, span] = acc.astype(BF)
        for tap in range(4):
            dtaps_ref[tap : tap + 1, span] += jnp.sum(
                grad * ext_ref[pl.ds(5 + tap, BLOCK), span], axis=0, keepdims=True
            )


def mixer_backward(place, part_rows, dmix, wout_t, saved, taps, rate, bias, onorm, heads):
    raw, mixed, states, inverses, solved, query_eff, keyw = saved
    rows, width = dmix.shape
    total_width = raw.shape[1]
    conv_width = taps.shape[1]
    value_dim = onorm.shape[1]
    value_all = heads * value_dim
    key_dim = (conv_width - value_all) // (2 * heads)
    steps = rows // BLOCK
    last = steps - 1
    whole = lambda shape: pl.BlockSpec(shape, lambda i, p: (0,) * len(shape))
    rows_of = lambda columns: pl.BlockSpec((BLOCK, columns), lambda i, p: (last - i, 0))
    each = lambda a, b: pl.BlockSpec((1, heads, a, b), lambda i, p: (last - i, 0, 0, 0))
    shape = jax.ShapeDtypeStruct
    halo = pl.BlockSpec(
        (8, total_width), lambda i, p: (jnp.maximum((last - i) * (BLOCK // 8) - 1, 0), 0)
    )
    per = part_rows // BLOCK

    def mixed_order(i, place_ref):
        block = last - i
        return (((block // per) ^ place_ref[0]) * per + block % per, 0)

    return pl.pallas_call(
        functools.partial(backward_kernel, heads, SEQ // BLOCK),
        grid_spec=pltpu.PrefetchScalarGridSpec(
        num_scalar_prefetch=1,
        grid=(steps,),
        in_specs=[
            pl.BlockSpec((BLOCK, width), mixed_order),
            whole(wout_t.shape),
            rows_of(total_width),
            halo,
            rows_of(value_all),
            each(key_dim, value_dim),
            each(BLOCK, BLOCK),
            each(BLOCK, key_dim + value_dim),
            each(BLOCK, key_dim),
            each(key_dim, key_dim),
            whole(taps.shape),
            whole(rate.shape),
            whole(bias.shape),
            whole(onorm.shape),
        ],
        out_specs=[
            rows_of(total_width),
            whole((8, conv_width)),
            whole((8, HALF)),
            whole((1, value_dim)),
        ],
        scratch_shapes=[
            pltpu.VMEM((heads, key_dim, value_dim), F32),
            pltpu.VMEM((BLOCK + 8, conv_width), F32),
            pltpu.VMEM((BLOCK + 8, conv_width), F32),
        ],
        ),
        out_shape=[
            shape((rows, total_width), BF),
            shape((8, conv_width), F32),
            shape((8, HALF), F32),
            shape((1, value_dim), F32),
        ],
        compiler_params=pltpu.CompilerParams(
            dimension_semantics=("arbitrary",), vmem_limit_bytes=56 * 1024 * 1024
        ),
        name="mixer_backward",
    )(
        place, dmix, wout_t, raw, raw, mixed, states, inverses, solved, query_eff, keyw,
        taps, rate, bias, onorm,
    )


def dot_plain(left_side, right_side):
    return jnp.dot(left_side, right_side, preferred_element_type=F32)


def dot_right_t(left_side, right_side):
    return lax.dot_general(
        left_side, right_side, (((1,), (1,)), ((), ())), preferred_element_type=F32
    )


def dot_left_t(left_side, right_side):
    return lax.dot_general(
        left_side, right_side, (((0,), (0,)), ((), ())), preferred_element_type=F32
    )


def swap(value, flip):
    count = lax.axis_size("tensor")
    return lax.ppermute(value, "tensor", [(i, i ^ flip) for i in range(count)])


def gather_blocks(block):
    far = swap(block, 2)
    near = swap(block, 1)
    return [block, near, far, swap(far, 1)]


def scatter_sum(parts):
    far = parts[2].astype(F32) + swap(parts[3].astype(BF), 1).astype(F32)
    far = swap(far.astype(BF), 2).astype(F32)
    near = parts[0].astype(F32) + swap(parts[1].astype(BF), 1).astype(F32)
    return near + far


def pad_columns(value, width):
    return jnp.pad(value, ((0, 0), (0, width - value.shape[1])))


def round_up(value, unit):
    return -(-value // unit) * unit


def sum_dp(value):
    return lax.psum_scatter(value.astype(BF), "dp", scatter_dimension=0, tiled=True).astype(F32)


def per_device(
    tokens,
    cotangent,
    norm1_gain,
    norm2_gain,
    query_weight,
    key_weight,
    value_weight,
    outgate_weight,
    alpha_weight,
    beta_weight,
    conv_query,
    conv_key,
    conv_value,
    decay_log,
    decay_bias,
    onorm_gain,
    output_weight,
    gate_weight,
    up_weight,
    down_weight,
):
    me = lax.axis_index("tensor")
    tensor_count = lax.axis_size("tensor")
    part_rows = cotangent.shape[0]
    width = tokens.shape[1]
    heads = alpha_weight.shape[1]
    units = gate_weight.shape[1]
    padded = round_up(units, 256)
    query_cols = query_weight.shape[1]
    value_cols = value_weight.shape[1]
    conv_width = 2 * query_cols + value_cols
    value_dim = onorm_gain.shape[0]

    small = pad_columns(jnp.concatenate([alpha_weight, beta_weight], axis=1), HALF)
    w_first = lax.all_gather(
        jnp.concatenate([query_weight, key_weight, value_weight, outgate_weight, small], axis=1),
        "dp",
        axis=0,
        tiled=True,
    )
    w_second = lax.all_gather(
        jnp.concatenate(
            [
                output_weight.T,
                pad_columns(gate_weight, padded),
                pad_columns(up_weight, padded),
                pad_columns(down_weight.T, padded),
            ],
            axis=1,
        ),
        "dp",
        axis=0,
        tiled=True,
    )
    w_out_t = w_second[:, :value_cols]
    w_pair = w_second[:, value_cols : value_cols + 2 * padded]
    w_down_t = w_second[:, value_cols + 2 * padded :]

    taps = jnp.concatenate([conv_query, conv_key, conv_value], axis=1)
    rate = pad_columns(jnp.exp(decay_log)[None], HALF)
    bias = pad_columns(decay_bias[None], HALF)
    onorm = onorm_gain[None]
    hidden_one, raw, normed, *saved = mixer_forward(
        tokens, norm1_gain[None], w_first, taps, rate, bias, onorm, heads
    )

    def block_of(value, flip):
        return lax.dynamic_slice_in_dim(value, (me ^ flip) * part_rows, part_rows, 0)

    normed_blocks = [block_of(normed, flip) for flip in range(4)]
    mixer_rows = scatter_sum([dot_right_t(block, w_out_t) for block in normed_blocks])
    inputs = block_of(tokens, 0).astype(F32)
    middle = inputs + mixer_rows
    inverse_two = lax.rsqrt(jnp.mean(middle * middle, axis=-1, keepdims=True) + EPS_NORM)
    unit_two = middle * inverse_two
    hidden_two = jnp.concatenate(gather_blocks((unit_two * norm2_gain).astype(BF)), axis=0)
    cot_all = jnp.concatenate(gather_blocks(cotangent), axis=0)
    pair = dot_plain(hidden_two, w_pair)
    gate, upward = pair[:, :padded], pair[:, padded:]
    sig = jax.nn.sigmoid(gate)
    silu = gate * sig
    active = (silu * upward).astype(BF)
    branch = dot_right_t(active, w_down_t).astype(BF)
    branch_rows = scatter_sum(
        [branch[part_rows * flip : part_rows * (flip + 1)] for flip in range(4)]
    )
    block_output = (middle + branch_rows).astype(BF)
    active_grad = dot_plain(cot_all, w_down_t)
    pair_grad = jnp.concatenate(
        [
            (active_grad * upward * (sig * (1.0 + gate * (1.0 - sig)))).astype(BF),
            (active_grad * silu).astype(BF),
        ],
        axis=1,
    )
    hidden_two_part = dot_right_t(pair_grad, w_pair).astype(BF)
    hidden_two_grad = scatter_sum(
        [hidden_two_part[part_rows * flip : part_rows * (flip + 1)] for flip in range(4)]
    )
    gain_two_part = jnp.sum(hidden_two_grad * unit_two, axis=0)
    gained_two = hidden_two_grad * norm2_gain
    middle_grad = (
        cotangent.astype(F32)
        + inverse_two * gained_two
        - unit_two * inverse_two * inverse_two * jnp.mean(middle * gained_two, axis=-1, keepdims=True)
    )
    middle_low = jnp.concatenate(gather_blocks(middle_grad.astype(BF)), axis=0)
    ffn_total = sum_dp(
        jnp.concatenate(
            [
                dot_left_t(hidden_two, pair_grad).astype(BF),
                dot_left_t(cot_all, active).astype(BF),
            ],
            axis=1,
        )
    )
    draw, dtaps, dsmall, donorm = mixer_backward(
        me[None].astype(jnp.int32),
        part_rows,
        middle_low,
        w_out_t,
        (raw,) + tuple(saved),
        taps,
        rate,
        bias,
        onorm,
        heads,
    )
    normed_mixed = jnp.concatenate(normed_blocks, axis=0)
    output_total = sum_dp(dot_left_t(middle_low, normed_mixed))
    hidden_one_grad = scatter_sum(
        [dot_right_t(block_of(draw, flip), w_first) for flip in range(4)]
    )
    proj_total = sum_dp(dot_left_t(hidden_one, draw))

    inverse_one = lax.rsqrt(jnp.mean(inputs * inputs, axis=-1, keepdims=True) + EPS_NORM)
    unit_one = inputs * inverse_one
    gain_one_part = jnp.sum(hidden_one_grad * unit_one, axis=0)
    gained = hidden_one_grad * norm1_gain
    tokens_grad = (
        middle_grad
        + inverse_one * gained
        - unit_one * inverse_one * inverse_one * jnp.mean(inputs * gained, axis=-1, keepdims=True)
    )

    tap_count = taps.shape[0]
    tap_width = max(conv_width, width)
    own_rows = jnp.concatenate(
        [pad_columns(dtaps[:tap_count], tap_width), pad_columns(dsmall[:2], tap_width)], axis=0
    )
    own_count = tap_count + 2
    shared_rows = jnp.stack(
        [
            jnp.pad(gain_one_part, (0, tap_width - width)),
            jnp.pad(gain_two_part, (0, tap_width - width)),
            jnp.pad(donorm[0], (0, tap_width - value_dim)),
        ]
    )
    table = jnp.concatenate(
        [
            lax.dynamic_update_slice_in_dim(
                jnp.zeros((own_count * tensor_count, tap_width), F32), own_rows, own_count * me, 0
            ),
            shared_rows,
        ],
        axis=0,
    )
    table = lax.psum(table, ("dp", "tensor"))
    own_total = lax.dynamic_slice_in_dim(table, own_count * me, own_count, 0)
    shared = table[own_count * tensor_count :]
    gain_share = width // tensor_count
    onorm_share = value_dim // tensor_count
    at = 2 * query_cols
    small_at = conv_width + value_cols
    return (
        block_output,
        tokens_grad,
        lax.dynamic_slice_in_dim(shared[0], me * gain_share, gain_share, 0),
        lax.dynamic_slice_in_dim(shared[1], me * gain_share, gain_share, 0),
        proj_total[:, :query_cols],
        proj_total[:, query_cols:at],
        proj_total[:, at:conv_width],
        proj_total[:, conv_width:small_at],
        proj_total[:, small_at : small_at + heads],
        proj_total[:, small_at + heads : small_at + 2 * heads],
        own_total[:tap_count, :query_cols],
        own_total[:tap_count, query_cols:at],
        own_total[:tap_count, at:conv_width],
        own_total[tap_count, :heads],
        own_total[tap_count + 1, :heads],
        lax.dynamic_slice_in_dim(shared[2], me * onorm_share, onorm_share, 0),
        output_total.T,
        ffn_total[:, :units],
        ffn_total[:, padded : padded + units],
        ffn_total[:, 2 * padded : 2 * padded + units].T,
    )


def solution(mesh):
    return jax.shard_map(
        per_device,
        mesh=mesh,
        in_specs=(
            P("dp", None),
            P(("dp", "tensor"), None),
            P(),
            P(),
            P("dp", "tensor"),
            P("dp", "tensor"),
            P("dp", "tensor"),
            P("dp", "tensor"),
            P("dp", "tensor"),
            P("dp", "tensor"),
            P(None, "tensor"),
            P(None, "tensor"),
            P(None, "tensor"),
            P("tensor"),
            P("tensor"),
            P(),
            P("tensor", "dp"),
            P("dp", "tensor"),
            P("dp", "tensor"),
            P("tensor", "dp"),
        ),
        out_specs=(
            P(("dp", "tensor"), None),
            P(("dp", "tensor"), None),
            P("tensor"),
            P("tensor"),
            P("dp", "tensor"),
            P("dp", "tensor"),
            P("dp", "tensor"),
            P("dp", "tensor"),
            P("dp", "tensor"),
            P("dp", "tensor"),
            P(None, "tensor"),
            P(None, "tensor"),
            P(None, "tensor"),
            P("tensor"),
            P("tensor"),
            P("tensor"),
            P("tensor", "dp"),
            P("dp", "tensor"),
            P("dp", "tensor"),
            P("tensor", "dp"),
        ),
        check_vma=False,
    )
```

time: 2360 us -> 827 us (0.35)
  matrix products: 738 us -> 103 us
  waiting for transfers between devices: 927 us -> 533 us
  local copies, waits for them, and re-layouts: 324 us -> 31.8 us
  other arithmetic: 184 us -> 23.8 us
  blocking collectives: 145 us -> 0 us
  Pallas kernels: 0 us -> 101 us
    dot_general x465 -> x2, matrix products: 600 us -> 23.7 us  [dot_plain(): return jnp.dot(left_side, right_side, preferred_element_type=F32)]
    reduce_scatter x10 -> x3, waiting for transfers between devices: 495 us -> 169 us  [sum_dp(): lax.psum_scatter(value.astype(BF), 'dp', scatter_dimension=0, tiled=True)]
    psum x2 -> x1, waiting for transfers between devices: 286 us -> 122 us  [per_device(): table = lax.psum(table, ('dp', 'tensor'))]
    ppermute x0 -> x21, waiting for transfers between devices: none -> 136 us  [swap(): return lax.ppermute(value, 'tensor', [(i, i ^ flip) for i in range(count)])]
    squeeze x160 -> x1, local copies, waits for them, and re-layouts: 114 us -> 1.28 us  [per_device(): own_total[tap_count + 1, :heads]]
    all_gather x4 -> x0, blocking collectives: 101 us -> none  [the longest x1 34 us: per_device(): lax.all_gather(key_weight, 'dp', axis=0, tiled=True)]
    pallas_call x0 -> x2, Pallas kernels: none -> 101 us  [the longest x1 53.6 us: mixer_backward(): pl.pallas_call(functools.partial(backward_kernel, heads, SEQ // BLOCK), g...]
    reduce_sum x51 -> x2, other arithmetic: 84.4 us -> 2.95 us  [the longest x1 2.01 us: per_device(): jnp.mean(middle * middle, axis=-1, keepdims=True) + EPS_NORM]
  transfers between devices with their start and end apart: 21 -> 27, of which waited for: 13 -> 15; matrix products, arithmetic and copies ran while one was open for 29% -> 12% of each run, Pallas kernels for 0% -> 6%
where the time goes in v1:
time: 827 us; the launch traced here: 819 us
  waiting for transfers between devices  533 us (64%)
  matrix products  103 us (12%)
  Pallas kernels  101 us (12%)
  local copies, waits for them, and re-layouts  31.8 us (4%)
  other arithmetic  23.8 us (3%)
  between operations  15.2 us (2%)
  starting transfers between devices  12.6 us (2%)
    reduce_scatter x3, waiting for transfers between devices, sum_dp(): lax.psum_scatter(value.astype(BF), 'dp', scatter_dimension=0, tiled=True)  169 us
    ppermute x21, waiting for transfers between devices, swap(): return lax.ppermute(value, 'tensor', [(i, i ^ flip) for i in range(count)])  136 us
    psum x1, waiting for transfers between devices, per_device(): table = lax.psum(table, ('dp', 'tensor'))  122 us
    all_gather x1, waiting for transfers between devices, per_device(): lax.all_gather(jnp.concatenate([query_weight, key_weight, value_weight, o...  60 us
    pallas_call x1, Pallas kernels, mixer_backward(): pl.pallas_call(functools.partial(backward_kernel, heads, SEQ // BLOCK), g...  53.6 us
    pallas_call x1, Pallas kernels, mixer_forward(): pl.pallas_call(functools.partial(forward_kernel, heads, SEQ // BLOCK), gr...  47 us
    all_gather x1, waiting for transfers between devices, per_device(): lax.all_gather(jnp.concatenate([output_weight.T, pad_columns(gate_weight,...  45.2 us
    dot_general x10, matrix products, dot_right_t(): lax.dot_general(left_side, right_side, (((1,), (1,)), ((), ())), preferre...  42.3 us
  transfers between devices with their start and end apart: 27, of which 15 were waited for; matrix products, arithmetic and copies ran while one was open for 12% of the time, Pallas kernels for 6%

profile of v1, /device:TPU:0, one launch (start us, length us, event | category | flops | bytes accessed | tf_op | source)
XLA Modules:
  0.0 819.4 jit_solution(5334927732993811101)
XLA Ops:
  18.8 60.0 %all-gather.3.cloned.1.call-done.w_ref = bf16[1024,1664]{1,0:T(8,128)(2,1)} async-done(((bf16[128,1664]{1,0:T(8,128)(2,1)}), bf16[1024,1664]{1,0:T(8,128)(2,1)}) %all-gather.3.cloned.1.call-update) | async-done | bytes 3407888 | tf_op jit(solution)/shard_map/all_gather | solution.py:641
  78.8 47.0 %mixer_forward.1 = (bf16[2048,1024]{1,0:T(8,128)(2,1)}, f32[2048,1664]{1,0:T(8,128)}, bf16[2048,512]{1,0:T(8,128)(2,1)}, f32[2048,512]{1,0:T(8,128)}, f32[8,2,12...) custom-call(bf16[2048,1024]{1,0:T(8,128)(2,1)} %x_ref.1, ...), custom_call_target="tpu_custom_call" | custom-call | tf_op jit(solution)/shard_map/mixer_forward/pallas_call | solution.py:220
  127.5 45.2 %all-gather.5.cloned.1.call-done = bf16[1024,2816]{1,0:T(8,128)(2,1)} async-done(((bf16[128,2816]{1,0:T(8,128)(2,1)}), bf16[1024,2816]{1,0:T(8,128)(2,1)}) %all-gather.5.cloned.1.call-update) | async-done | bytes 5767184 | tf_op jit(solution)/shard_map/all_gather | solution.py:647
  181.2 23.2 %collective-permute-done.2 = bf16[512,1024]{1,0:T(8,128)(2,1)S(1)} collective-permute-done((bf16[512,1024]{1,0:T(8,128)(2,1)S(1)}, bf16[512,1024]{1,0:T(8,128)(2,1)S(1)}, u32[]{:S(2)}, u32[]{:S(2)}) %collective-permute-start.2) | collective-permute-done | bytes 1048608 | tf_op jit(solution)/shard_map/ppermute | solution.py:578
  208.4 18.6 %collective-permute-done.10 = bf16[512,1024]{1,0:T(8,128)(2,1)S(1)} collective-permute-done((bf16[512,1024]{1,0:T(8,128)(2,1)S(1)}, bf16[512,1024]{1,0:T(8,128)(2,1)S(1)}, u32[]{:S(2)}, u32[]{:S(2)}) %collective-permute-start.10) | collective-permute-done | bytes 1048608 | tf_op jit(solution)/shard_map/ppermute | solution.py:578
  227.4 21.2 %collective-permute-done.4 = bf16[512,1024]{1,0:T(8,128)(2,1)S(1)} collective-permute-done((bf16[512,1024]{1,0:T(8,128)(2,1)S(1)}, bf16[512,1024]{1,0:T(8,128)(2,1)S(1)}, u32[]{:S(2)}, u32[]{:S(2)}) %collective-permute-start.4) | collective-permute-done | bytes 1048608 | tf_op jit(solution)/shard_map/ppermute | solution.py:578
  251.4 12.9 %fusion.6 = f32[2048,1536]{0,1:T(8,128)} fusion(bf16[1024,2816]{1,0:T(8,128)(2,1)S(1)} %copy-done.8, bf16[512,1024]{1,0:T(8,128)(2,1)} %collective-permute-done.5, bf16[512,1024]{1,0:T(8,128)(2,1)S(1)} %collective-permute-done.4, bf16[512,1024]{1,0:T(8,128)(2,1)} %copy-done.28, bf16[512,1024]{1,0:T(8,128)(2,1)S(1)} %multiply_convert_fusion.3), kind=kOutput, calls=%fused_computation.20 | convolution fusion | flops 6459228160 | bytes 19922944 | tf_op jit(solution)/shard_map/dot_general | solution.py:561
  264.3 10.9 %multiply_convert_fusion.1 = (bf16[2048,768]{0,1:T(8,128)(2,1)}, bf16[2048,768]{0,1:T(8,128)(2,1)}, bf16[2048,768]{0,1:T(8,128)(2,1)S(1)}) fusion(f32[2048,1536]{0,1:T(8,128)} %fusion.6, bf16[2048,1024]{1,0:T(8,128)(2,1)S(1)} %constant_dynamic-update-slice_fusion.7, bf16[1024,2816]{1,0:T(8,128)(2,1)S(1)} %copy-done.8), kind=kOutput, calls=%fused_computation.2 | convolution fusion | flops 3244818432 | bytes 27787264 | tf_op jit(solution)/shard_map/dot_general | solution.py:561
  275.1 10.0 %fusion.3 = bf16[2048,1024]{1,0:T(8,128)(2,1)S(1)} fusion(bf16[2048,768]{0,1:T(8,128)(2,1)} %get-tuple-element.95, bf16[2048,768]{0,1:T(8,128)(2,1)} %get-tuple-element.94, bf16[1024,2816]{1,0:T(8,128)(2,1)S(1)} %copy-done.8), kind=kOutput, calls=%fused_computation.11 | convolution fusion | flops 6457131008 | bytes 13631488 | tf_op jit(solution)/shard_map/dot_general | solution.py:565
  294.4 22.3 %collective-permute-done.14 = bf16[512,1024]{1,0:T(8,128)(2,1)S(1)} collective-permute-done((bf16[512,1024]{1,0:T(8,128)(2,1)S(1)}, bf16[512,1024]{1,0:T(8,128)(2,1)S(1)}, u32[]{:S(2)}, u32[]{:S(2)}) %collective-permute-start.14) | collective-permute-done | bytes 1048608 | tf_op jit(solution)/shard_map/ppermute | solution.py:578
  317.7 21.0 %collective-permute-done.8 = bf16[512,1024]{1,0:T(8,128)(2,1)S(1)} collective-permute-done((bf16[512,1024]{1,0:T(8,128)(2,1)S(1)}, bf16[512,1024]{1,0:T(8,128)(2,1)S(1)}, u32[]{:S(2)}, u32[]{:S(2)}) %collective-permute-start.8) | collective-permute-done | bytes 1048608 | tf_op jit(solution)/shard_map/ppermute | solution.py:578
  343.3 23.2 %collective-permute-done.16 = bf16[512,1024]{1,0:T(8,128)(2,1)} collective-permute-done((bf16[512,1024]{1,0:T(8,128)(2,1)S(1)}, bf16[512,1024]{1,0:T(8,128)(2,1)}, u32[]{:S(2)}, u32[]{:S(2)}) %collective-permute-start.16) | collective-permute-done | bytes 1048608 | tf_op jit(solution)/shard_map/ppermute | solution.py:578
  373.1 53.6 %mixer_backward.1 = (bf16[2048,1664]{1,0:T(8,128)(2,1)}, f32[8,1024]{1,0:T(8,128)}, f32[8,128]{1,0:T(8,128)}, f32[1,256]{1,0:T(1,128)}) custom-call(s32[1]{0:T(128)} %bitcast.6.place_ref, bf16[2048,1024]{1,0:T(8,128)(2,1)} %pad_maximum_fusion.3.dmix_ref, bf16[1024,512]{1,0:T(8,128)(2,1)} %slice.132.wout_ref, ...), custom_call_target="tpu_custom_call" | custom-call | tf_op jit(solution)/shard_map/mixer_backward/pallas_call | solution.py:511
  431.7 5.2 fusion.32
  437.0 5.7 fusion.35
  443.1 5.1 add_convert_fusion
  449.6 11.7 %fusion.4 = bf16[1024,1536]{1,0:T(8,128)(2,1)} fusion(bf16[2048,768]{0,1:T(8,128)(2,1)} %get-tuple-element.95, bf16[2048,768]{0,1:T(8,128)(2,1)} %get-tuple-element.94, bf16[512,1024]{1,0:T(8,128)(2,1)} %collective-permute-done.5, bf16[512,1024]{1,0:T(8,128)(2,1)S(1)} %copy-done.27, bf16[512,1024]{1,0:T(8,128)(2,1)S(1)} %copy-done.29, ...), kind=kOutput, calls=%fused_computation.12 | convolution fusion | flops 6473383936 | bytes 13631488 | tf_op jit(solution)/shard_map/dot_general | solution.py:571
  461.3 7.0 convolution_convert_fusion.2
  473.6 7.2 fusion.13
  481.5 4.8 pad_maximum_fusion.1
  486.4 12.9 %convolution_convert_fusion = bf16[1024,1664]{1,0:T(8,128)(2,1)} fusion(bf16[2048,1024]{1,0:T(8,128)(2,1)} %get-tuple-element.45, bf16[2048,1664]{1,0:T(8,128)(2,1)} %get-tuple-element.41), kind=kOutput, calls=%fused_computation.13 | convolution fusion | flops 6981025792 | bytes 14417920 | tf_op jit(solution)/shard_map/dot_general | solution.py:571
  504.9 122.4 %all-reduce.10.cloned.1.call-done = f32[27,1024]{1,0:T(8,128)} async-done(((f32[27,1024]{1,0:T(8,128)}), f32[27,1024]{1,0:T(8,128)}) %all-reduce.10.cloned.1.call-update) | async-done | bytes 110608 | tf_op jit(solution)/shard_map/psum | solution.py:774
  633.4 92.1 %reduce-scatter.8.cloned.1.call-done = bf16[128,2304]{1,0:T(8,128)(2,1)} async-done(((bf16[1024,2304]{1,0:T(8,128)(2,1)}), bf16[128,2304]{1,0:T(8,128)(2,1)}) %reduce-scatter.8.cloned.1.call-update) | async-done | bytes 589840 | tf_op jit(solution)/shard_map/reduce_scatter | solution.py:603
  729.6 76.9 %reduce-scatter.4.cloned.1.call-done = bf16[128,1664]{1,0:T(8,128)(2,1)} async-done(((bf16[1024,1664]{1,0:T(8,128)(2,1)}), bf16[128,1664]{1,0:T(8,128)(2,1)}) %reduce-scatter.4.cloned.1.call-update) | async-done | bytes 426000 | tf_op jit(solution)/shard_map/reduce_scatter | solution.py:603
  (185 shorter events, 84.3 us)
Async XLA Ops:
  7.2 71.6 %all-gather.3.cloned.1.call-start = ((), (), s32[]{:S(2)}) async-start(), calls=%async_computation.3 | async-start | bytes 3833856 | tf_op jit(solution)/shard_map/all_gather | solution.py:641
  12.4 160.3 %all-gather.5.cloned.1.call-start = ((), (), s32[]{:S(2)}) async-start(), calls=%async_computation.4 | async-start | bytes 6488064 | tf_op jit(solution)/shard_map/all_gather | solution.py:647
  17.6 481.7 %reduce-scatter.6.cloned.1.call-start = ((), (), s32[]{:S(2)}) async-start(), calls=%async_computation.7 | async-start | bytes 1179648 | tf_op jit(solution)/shard_map/reduce_scatter | solution.py:603
  177.0 4.2 collective-permute-start
  178.4 26.1 %collective-permute-start.2 = (bf16[512,1024]{1,0:T(8,128)(2,1)S(1)}, bf16[512,1024]{1,0:T(8,128)(2,1)S(1)}, u32[]{:S(2)}, u32[]{:S(2)}) collective-permute-start(bf16[512,1024]{1,0:T(8,128)(2,1)S(1)} %add_convert_fusion.4), channel_id=1, source_target_pairs={{0,2},{1,3},{2,0},{3,1},{4,6},{5,7},{6,4},{7,5},{8,10},{9,11},{10,... | collective-permute-start | bytes 3145736 | tf_op jit(solution)/shard_map/ppermute | solution.py:578
  180.0 46.9 %collective-permute-start.10 = (bf16[512,1024]{1,0:T(8,128)(2,1)S(1)}, bf16[512,1024]{1,0:T(8,128)(2,1)S(1)}, u32[]{:S(2)}, u32[]{:S(2)}) collective-permute-start(bf16[512,1024]{1,0:T(8,128)(2,1)S(1)} %copy-done), channel_id=1, source_target_pairs={{0,2},{1,3},{2,0},{3,1},{4,6},{5,7},{6,4},{7,5},{8,10},{9,11},{10,... | collective-permute-start | bytes 3145736 | tf_op jit(solution)/shard_map/ppermute | solution.py:578
  206.7 41.8 %collective-permute-start.4 = (bf16[512,1024]{1,0:T(8,128)(2,1)S(1)}, bf16[512,1024]{1,0:T(8,128)(2,1)S(1)}, u32[]{:S(2)}, u32[]{:S(2)}) collective-permute-start(bf16[512,1024]{1,0:T(8,128)(2,1)S(1)} %multiply_convert_fusion.3), channel_id=1, source_target_pairs={{0,2},{1,3},{2,0},{3,1},{4,6},{5,7},{6,4},{7,5},{8,10},{9,11},{10,... | collective-permute-start | bytes 3145736 | tf_op jit(solution)/shard_map/ppermute | solution.py:578
  208.3 40.3 %collective-permute-start.9 = (bf16[512,1024]{1,0:T(8,128)(2,1)S(1)}, bf16[512,1024]{1,0:T(8,128)(2,1)S(1)}, u32[]{:S(2)}, u32[]{:S(2)}) collective-permute-start(bf16[512,1024]{1,0:T(8,128)(2,1)S(1)} %copy-done), channel_id=1, source_target_pairs={{0,1},{1,0},{2,3},{3,2},{4,5},{5,4},{6,7},{7,6},{8,9},{9,8},{10,11... | collective-permute-start | bytes 3145736 | tf_op jit(solution)/shard_map/ppermute | solution.py:578
  226.9 21.9 %collective-permute-start.11 = (bf16[512,1024]{1,0:T(8,128)(2,1)S(1)}, bf16[512,1024]{1,0:T(8,128)(2,1)S(1)}, u32[]{:S(2)}, u32[]{:S(2)}) collective-permute-start(bf16[512,1024]{1,0:T(8,128)(2,1)S(1)} %collective-permute-done.10), channel_id=1, source_target_pairs={{0,1},{1,0},{2,3},{3,2},{4,5},{5,4},{6,7},{7,6},{8,9},{9,8},{10,11... | collective-permute-start | bytes 3145736 | tf_op jit(solution)/shard_map/ppermute | solution.py:578
  226.9 22.0 %collective-permute-start.3 = (bf16[512,1024]{1,0:T(8,128)(2,1)S(1)}, bf16[512,1024]{1,0:T(8,128)(2,1)S(1)}, u32[]{:S(2)}, u32[]{:S(2)}) collective-permute-start(bf16[512,1024]{1,0:T(8,128)(2,1)S(1)} %multiply_convert_fusion.3), channel_id=1, source_target_pairs={{0,1},{1,0},{2,3},{3,2},{4,5},{5,4},{6,7},{7,6},{8,9},{9,8},{10,11... | collective-permute-start | bytes 3145736 | tf_op jit(solution)/shard_map/ppermute | solution.py:578
  285.3 4.9 collective-permute-start.13
  290.1 4.3 collective-permute-start.12
  290.7 26.1 %collective-permute-start.14 = (bf16[512,1024]{1,0:T(8,128)(2,1)S(1)}, bf16[512,1024]{1,0:T(8,128)(2,1)S(1)}, u32[]{:S(2)}, u32[]{:S(2)}) collective-permute-start(bf16[512,1024]{1,0:T(8,128)(2,1)S(1)} %add_convert_fusion.1), channel_id=1, source_target_pairs={{0,2},{1,3},{2,0},{3,1},{4,6},{5,7},{6,4},{7,5},{8,10},{9,11},{10,... | collective-permute-start | bytes 3145736 | tf_op jit(solution)/shard_map/ppermute | solution.py:578
  292.3 25.4 %collective-permute-start.6 = (bf16[512,1024]{1,0:T(8,128)(2,1)S(1)}, bf16[512,1024]{1,0:T(8,128)(2,1)S(1)}, u32[]{:S(2)}, u32[]{:S(2)}) collective-permute-start(bf16[512,1024]{1,0:T(8,128)(2,1)S(1)} %get-tuple-element.100), channel_id=1, source_target_pairs={{0,1},{1,0},{2,3},{3,2},{4,5},{5,4},{6,7},{7,6},{8,9},{9,8},{10,11... | collective-permute-start | bytes 3145736 | tf_op jit(solution)/shard_map/ppermute | solution.py:578
  292.8 45.8 %collective-permute-start.8 = (bf16[512,1024]{1,0:T(8,128)(2,1)S(1)}, bf16[512,1024]{1,0:T(8,128)(2,1)S(1)}, u32[]{:S(2)}, u32[]{:S(2)}) collective-permute-start(bf16[512,1024]{1,0:T(8,128)(2,1)S(1)} %add_convert_fusion.3), channel_id=1, source_target_pairs={{0,2},{1,3},{2,0},{3,1},{4,6},{5,7},{6,4},{7,5},{8,10},{9,11},{10,... | collective-permute-start | bytes 3145736 | tf_op jit(solution)/shard_map/ppermute | solution.py:578
  341.8 24.7 %collective-permute-start.16 = (bf16[512,1024]{1,0:T(8,128)(2,1)S(1)}, bf16[512,1024]{1,0:T(8,128)(2,1)}, u32[]{:S(2)}, u32[]{:S(2)}) collective-permute-start(bf16[512,1024]{1,0:T(8,128)(2,1)S(1)} %get-tuple-element.90), channel_id=1, source_target_pairs={{0,2},{1,3},{2,0},{3,1},{4,6},{5,7},{6,4},{7,5},{8,10},{9,11},{10,... | collective-permute-start | bytes 3145736 | tf_op jit(solution)/shard_map/ppermute | solution.py:578
  343.3 25.5 %collective-permute-start.15 = (bf16[512,1024]{1,0:T(8,128)(2,1)S(1)}, bf16[512,1024]{1,0:T(8,128)(2,1)}, u32[]{:S(2)}, u32[]{:S(2)}) collective-permute-start(bf16[512,1024]{1,0:T(8,128)(2,1)S(1)} %get-tuple-element.90), channel_id=1, source_target_pairs={{0,1},{1,0},{2,3},{3,2},{4,5},{5,4},{6,7},{7,6},{8,9},{9,8},{10,11... | collective-permute-start | bytes 3145736 | tf_op jit(solution)/shard_map/ppermute | solution.py:578
  366.5 3.0 collective-permute-start.17
  431.5 11.6 %collective-permute-start.19 = (bf16[512,1024]{1,0:T(8,128)(2,1)}, bf16[512,1024]{1,0:T(8,128)(2,1)}, u32[]{:S(2)}, u32[]{:S(2)}) collective-permute-start(bf16[512,1024]{1,0:T(8,128)(2,1)} %fusion.38), channel_id=1, source_target_pairs={{0,1},{1,0},{2,3},{3,2},{4,5},{5,4},{6,7},{7,6},{8,9},{9,8},{10,11... | collective-permute-start | bytes 3145736 | tf_op jit(solution)/shard_map/ppermute | solution.py:578
  436.9 190.4 %all-reduce.10.cloned.1.call-start = ((), (), s32[]{:S(2)}) async-start(), calls=%async_computation.5 | async-start | bytes 262144 | tf_op jit(solution)/shard_map/psum | solution.py:774
  442.7 26.6 %collective-permute-start.18 = (bf16[512,1024]{1,0:T(8,128)(2,1)}, bf16[512,1024]{1,0:T(8,128)(2,1)}, u32[]{:S(2)}, u32[]{:S(2)}) collective-permute-start(bf16[512,1024]{1,0:T(8,128)(2,1)} %fusion.35), channel_id=1, source_target_pairs={{0,1},{1,0},{2,3},{3,2},{4,5},{5,4},{6,7},{7,6},{8,9},{9,8},{10,11... | collective-permute-start | bytes 3145736 | tf_op jit(solution)/shard_map/ppermute | solution.py:578
  448.1 25.4 %collective-permute-start.20 = (bf16[512,1024]{1,0:T(8,128)(2,1)}, bf16[512,1024]{1,0:T(8,128)(2,1)}, u32[]{:S(2)}, u32[]{:S(2)}) collective-permute-start(bf16[512,1024]{1,0:T(8,128)(2,1)} %add_convert_fusion), channel_id=1, source_target_pairs={{0,2},{1,3},{2,0},{3,1},{4,6},{5,7},{6,4},{7,5},{8,10},{9,11},{10,... | collective-permute-start | bytes 3145736 | tf_op jit(solution)/shard_map/ppermute | solution.py:578
  481.5 244.1 %reduce-scatter.8.cloned.1.call-start = ((), (), s32[]{:S(2)}) async-start(), calls=%async_computation.8 | async-start | bytes 5308416 | tf_op jit(solution)/shard_map/reduce_scatter | solution.py:603
  486.3 320.2 %reduce-scatter.4.cloned.1.call-start = ((), (), s32[]{:S(2)}) async-start(), calls=%async_computation.6 | async-start | bytes 3833856 | tf_op jit(solution)/shard_map/reduce_scatter | solution.py:603
  (36 other events, 582.3 us)
Sparse Core Ops, SparseCore 0:
  12.6 66.2 all-gather.2
  81.6 91.1 all-gather.4
  437.0 61.7 reduce-scatter.5
  505.7 121.5 all-reduce.9
  631.2 94.2 reduce-scatter.7
  729.5 77.0 reduce-scatter.3

commit v2 on v1

v2 whole, which is shorter than its diff:
```python
import functools
import jax
import jax.numpy as jnp
from jax import lax
from jax.sharding import PartitionSpec as P
from jax.experimental import pallas as pl
from jax.experimental.pallas import tpu as pltpu

SEQ = 2048
BLOCK = 256
HALF = 128
EPS_NORM = 1e-05
EPS_UNIT = 1e-06
BF = jnp.bfloat16
F32 = jnp.float32
HIGH = lax.Precision.HIGHEST


def mm(left, right):
    return lax.dot_general(
        left.astype(BF), right.astype(BF), (((1,), (0,)), ((), ())), preferred_element_type=F32
    )


def mm_nt(left, right):
    return lax.dot_general(
        left.astype(BF), right.astype(BF), (((1,), (1,)), ((), ())), preferred_element_type=F32
    )


def mm_tn(left, right):
    return lax.dot_general(
        left.astype(BF), right.astype(BF), (((0,), (0,)), ((), ())), preferred_element_type=F32
    )


def mm_exact(left, right):
    return lax.dot_general(
        left, right, (((1,), (0,)), ((), ())), precision=HIGH, preferred_element_type=F32
    )


def iota2(rows, columns):
    return (
        lax.broadcasted_iota(jnp.int32, (rows, columns), 0),
        lax.broadcasted_iota(jnp.int32, (rows, columns), 1),
    )


def unit_lower_inverse(blocks):
    size = blocks[0].shape[0]
    row, col = iota2(size, size)
    eye = jnp.where(row == col, 1.0, 0.0).astype(F32)
    first = jnp.where((row ^ col) == 1, 1.0, 0.0).astype(F32)
    results = [eye - block * first for block in blocks]
    lows = [block.astype(BF) for block in blocks]
    shift = 1
    while (1 << shift) < size:
        mask = jnp.where(((row >> shift) ^ (col >> shift)) == 1, 1.0, 0.0).astype(BF)
        halves = [result.astype(BF) for result in results]
        inner = [mm(low * mask, half).astype(BF) for low, half in zip(lows, halves)]
        results = [
            result - mm(half, part) for result, half, part in zip(results, halves, inner)
        ]
        shift += 1
    return results


def softplus(value):
    return jnp.maximum(value, 0.0) + jnp.log1p(jnp.exp(-jnp.abs(value)))


def lower_ones(size):
    row, col = iota2(size, size)
    return jnp.where(row >= col, 1.0, 0.0).astype(F32)


def fades(total, total_t, index):
    row, col = iota2(BLOCK, BLOCK)
    gaps = total[:, index : index + 1] - total_t[index : index + 1, :]
    fading = jnp.exp(jnp.where(row >= col, gaps, -1e30))
    return fading, row > col


def forward_kernel(
    heads,
    per_seq,
    pieces,
    place_ref,
    x_ref,
    gain_ref,
    taps_ref,
    rate_ref,
    bias_ref,
    *refs,
):
    (
        w_ref,
        hidden_ref,
        raw_ref,
        mixed_ref,
        state_ref,
        inv_ref,
        solved_ref,
        query_eff_ref,
        keyw_ref,
        carry_ref,
        ext_ref,
    ) = refs[pieces:]
    key_dim = state_ref.shape[2]
    value_dim = state_ref.shape[3]
    conv_width = taps_ref.shape[1]
    head_width = conv_width // heads
    step = pl.program_id(0)

    @pl.when(step == 0)
    def _():
        rows = w_ref.shape[0] // pieces
        for index in range(pieces):
            start = pl.multiple_of((place_ref[0] ^ index) * rows, rows)
            w_ref[pl.ds(start, rows), :] = refs[index][...]

    @pl.when(step % per_seq == 0)
    def _():
        carry_ref[...] = jnp.zeros_like(carry_ref)
        ext_ref[0:8, :] = jnp.zeros((8, conv_width), F32)

    @pl.when(step % per_seq != 0)
    def _():
        ext_ref[0:8, :] = ext_ref[BLOCK : BLOCK + 8, :]

    inputs = x_ref[...].astype(F32)
    inverse = lax.rsqrt(jnp.mean(inputs * inputs, axis=-1, keepdims=True) + EPS_NORM)
    hidden = (inputs * inverse * gain_ref[...]).astype(BF)
    hidden_ref[...] = hidden
    ext_ref[8:, :] = mm(hidden, w_ref[:, :conv_width])
    raw_ref[:, :conv_width] = ext_ref[8:, :]
    raw_ref[:, conv_width:] = mm(hidden, w_ref[:, conv_width:])

    small = raw_ref[:, conv_width:]
    betas = jax.nn.sigmoid(small)
    decays = -rate_ref[...] * softplus(small + bias_ref[...])
    total = mm_exact(lower_ones(BLOCK), decays)
    total_t = total.T

    def conv(start, width):
        acc = taps_ref[0:1, start : start + width] * ext_ref[pl.ds(5, BLOCK), start : start + width]
        for tap in range(1, 4):
            acc = acc + (
                taps_ref[tap : tap + 1, start : start + width]
                * ext_ref[pl.ds(5 + tap, BLOCK), start : start + width]
            )
        return acc * jax.nn.sigmoid(acc)

    def unit(value):
        return value * lax.rsqrt(jnp.sum(value * value, axis=-1, keepdims=True) + EPS_UNIT)

    parts = []
    for head in range(heads):
        start = head * head_width
        query = unit(conv(start, key_dim)) * key_dim ** (-0.5)
        keys = unit(conv(start + key_dim, key_dim))
        values = conv(start + 2 * key_dim, value_dim)
        beta = betas[:, heads + head : heads + head + 1]
        fading, strict = fades(total, total_t, head)
        key_low = keys.astype(BF)
        coupling = jnp.where(strict, beta * fading * mm_nt(key_low, key_low), 0.0)
        scores = (mm_nt(query, key_low) * fading).astype(BF)
        parts.append((query, keys, values, beta, coupling, scores))
    blocks = []
    for part in parts:
        coupling = part[4]
        blocks += [coupling[:HALF, :HALF], coupling[HALF:, HALF:]]
    inverses = unit_lower_inverse(blocks)
    for head in range(heads):
        query, keys, values, beta, coupling, scores = parts[head]
        top, bottom = inverses[2 * head], inverses[2 * head + 1]
        cross = -mm(bottom, mm(coupling[HALF:, :HALF], top))
        inverse_low = jnp.concatenate(
            [
                jnp.concatenate([top.astype(BF), jnp.zeros((HALF, HALF), BF)], axis=1),
                jnp.concatenate([cross.astype(BF), bottom.astype(BF)], axis=1),
            ],
            axis=0,
        )
        inv_ref[0, head] = inverse_low
        column = total[:, head : head + 1]
        last = total[BLOCK - 1 :, head : head + 1]
        grown = jnp.exp(column)
        targets = jnp.concatenate(
            [(((beta * grown) * keys)).astype(BF), (beta * values).astype(BF)], axis=1
        )
        solved = mm(inverse_low, targets)
        solved_low = solved.astype(BF)
        solved_ref[0, head] = solved_low
        spread = mm(scores, solved_low)
        query_eff = (query * grown - spread[:, :key_dim]).astype(BF)
        query_eff_ref[0, head] = query_eff
        key_fade = keys * jnp.exp(last - column)
        gathered = mm_tn(key_fade, solved_low)
        keyw = gathered[:, :key_dim].astype(BF)
        keyw_ref[0, head] = keyw
        state = carry_ref[head]
        state_ref[0, head] = state
        state_low = state.astype(BF)
        mixed = mm(query_eff, state_low) + spread[:, key_dim:]
        carry_ref[head] = jnp.exp(last) * state - mm(keyw, state_low) + gathered[:, key_dim:]
        mixed_ref[:, head * value_dim : (head + 1) * value_dim] = mixed


def mixer_forward(tokens, gain, pieces, place, taps, rate, bias, heads, value_dim):
    rows, width = tokens.shape
    total_width = pieces[0].shape[1]
    conv_width = taps.shape[1]
    value_all = heads * value_dim
    key_dim = (conv_width - value_all) // (2 * heads)
    steps = rows // BLOCK
    whole = lambda shape: pl.BlockSpec(shape, lambda i, p: (0,) * len(shape))
    rows_of = lambda columns: pl.BlockSpec((BLOCK, columns), lambda i, p: (i, 0))
    each = lambda a, b: pl.BlockSpec((1, heads, a, b), lambda i, p: (i, 0, 0, 0))
    shape = jax.ShapeDtypeStruct
    return pl.pallas_call(
        functools.partial(forward_kernel, heads, SEQ // BLOCK, len(pieces)),
        grid_spec=pltpu.PrefetchScalarGridSpec(
            num_scalar_prefetch=1,
            grid=(steps,),
            in_specs=[
                rows_of(width),
                whole((1, width)),
                whole(taps.shape),
                whole(rate.shape),
                whole(bias.shape),
            ]
            + [whole(piece.shape) for piece in pieces],
            out_specs=[
                whole((width, total_width)),
                rows_of(width),
                rows_of(total_width),
                rows_of(value_all),
                each(key_dim, value_dim),
                each(BLOCK, BLOCK),
                each(BLOCK, key_dim + value_dim),
                each(BLOCK, key_dim),
                each(key_dim, key_dim),
            ],
            scratch_shapes=[
                pltpu.VMEM((heads, key_dim, value_dim), F32),
                pltpu.VMEM((BLOCK + 8, conv_width), F32),
            ],
        ),
        out_shape=[
            shape((width, total_width), BF),
            shape((rows, width), BF),
            shape((rows, total_width), F32),
            shape((rows, value_all), F32),
            shape((steps, heads, key_dim, value_dim), F32),
            shape((steps, heads, BLOCK, BLOCK), BF),
            shape((steps, heads, BLOCK, key_dim + value_dim), BF),
            shape((steps, heads, BLOCK, key_dim), BF),
            shape((steps, heads, key_dim, key_dim), BF),
        ],
        compiler_params=pltpu.CompilerParams(
            dimension_semantics=("arbitrary",), vmem_limit_bytes=48 * 1024 * 1024
        ),
        cost_estimate=pl.CostEstimate(
            flops=rows * 20_000_000, bytes_accessed=rows * 60_000, transcendentals=0
        ),
        name="mixer_forward",
    )(place, tokens, gain, taps, rate, bias, *pieces)


def gated_kernel(
    heads,
    place_ref,
    hidden_ref,
    mixed_ref,
    wgate_ref,
    wout_ref,
    onorm_ref,
    *out_refs,
):
    value_dim = onorm_ref.shape[1]
    gates = mm(hidden_ref[...], wgate_ref[...])
    columns = []
    for head in range(heads):
        span = slice(head * value_dim, (head + 1) * value_dim)
        mixed = mixed_ref[:, span]
        gate = gates[:, span]
        scale = lax.rsqrt(jnp.mean(mixed * mixed, axis=-1, keepdims=True) + EPS_NORM)
        columns.append(
            (mixed * scale * onorm_ref[...] * (gate * jax.nn.sigmoid(gate))).astype(BF)
        )
    normed = jnp.concatenate(columns, axis=1)
    part = mm_nt(normed, wout_ref[...]).astype(BF)
    for index in range(2):

        @pl.when(pl.program_id(0) == index)
        def _():
            out_refs[index][...] = normed
            out_refs[2 + index][...] = part


def gated_out(place, first, part_rows, hidden, mixed, weights, onorm, heads):
    width = hidden.shape[1]
    value_all = mixed.shape[1]
    whole = lambda block, at: pl.BlockSpec(block, lambda i, p: (0, at))
    theirs = lambda columns: pl.BlockSpec(
        (part_rows, columns), lambda i, p: ((first - i) ^ p[0], 0)
    )
    shape = jax.ShapeDtypeStruct
    return pl.pallas_call(
        functools.partial(gated_kernel, heads),
        grid_spec=pltpu.PrefetchScalarGridSpec(
            num_scalar_prefetch=1,
            grid=(2,),
            in_specs=[
                theirs(width),
                theirs(value_all),
                whole((width, value_all), 0),
                whole((width, value_all), 1),
                whole(onorm.shape, 0),
            ],
            out_specs=[whole((part_rows, value_all), 0)] * 2 + [whole((part_rows, width), 0)] * 2,
        ),
        out_shape=[shape((part_rows, value_all), BF)] * 2 + [shape((part_rows, width), BF)] * 2,
        compiler_params=pltpu.CompilerParams(
            dimension_semantics=("arbitrary",), vmem_limit_bytes=48 * 1024 * 1024
        ),
        cost_estimate=pl.CostEstimate(
            flops=part_rows * 8_000_000, bytes_accessed=part_rows * 24_000, transcendentals=0
        ),
        name="gated_out",
    )(place, hidden, mixed, weights, weights, onorm)


def backward_kernel(
    heads,
    per_seq,
    place_ref,
    *all_refs,
):
    dmix_refs = all_refs[:4]
    (
    wout_ref,
    raw_ref,
    halo_ref,
    hidden_ref,
    wgate_ref,
    mixed_ref,
    state_ref,
    inv_ref,
    solved_ref,
    query_eff_ref,
    keyw_ref,
    taps_ref,
    rate_ref,
    bias_ref,
    onorm_ref,
    draw_ref,
    dtaps_ref,
    dsmall_ref,
    donorm_ref,
    carry_ref,
    ext_ref,
    dext_ref,
    dmix_ref,
    ) = all_refs[4:]
    key_dim = state_ref.shape[2]
    value_dim = state_ref.shape[3]
    conv_width = taps_ref.shape[1]
    head_width = conv_width // heads
    full_width = head_width + value_dim
    step = pl.program_id(0)
    block = pl.num_programs(0) - 1 - step

    per = dmix_refs[0].shape[0] // BLOCK
    source = (block // per) ^ place_ref[0]
    start = pl.multiple_of((block % per) * BLOCK, BLOCK)
    for index in range(4):

        @pl.when(source == index)
        def _():
            dmix_ref[...] = dmix_refs[index][pl.ds(start, BLOCK), :]

    @pl.when(step == 0)
    def _():
        dtaps_ref[...] = jnp.zeros_like(dtaps_ref)
        dsmall_ref[...] = jnp.zeros_like(dsmall_ref)
        donorm_ref[...] = jnp.zeros_like(donorm_ref)

    @pl.when(step % per_seq == 0)
    def _():
        carry_ref[...] = jnp.zeros_like(carry_ref)
        dext_ref[BLOCK:, :] = jnp.zeros((8, conv_width), F32)

    @pl.when(step % per_seq != 0)
    def _():
        dext_ref[BLOCK:, :] = dext_ref[0:8, :]

    keep = jnp.where(block % per_seq == 0, 0.0, 1.0)
    ext_ref[0:8, :] = halo_ref[...] * keep
    ext_ref[8:, :] = raw_ref[:, :conv_width]

    small = raw_ref[:, conv_width:]
    betas = jax.nn.sigmoid(small)
    shifted = small + bias_ref[...]
    decays = -rate_ref[...] * softplus(shifted)
    lower = lower_ones(BLOCK)
    total = mm_exact(lower, decays)
    total_t = total.T
    lane = lax.broadcasted_iota(jnp.int32, (1, HALF), 1)

    def conv(start, width):
        acc = taps_ref[0:1, start : start + width] * ext_ref[pl.ds(5, BLOCK), start : start + width]
        for tap in range(1, 4):
            acc = acc + (
                taps_ref[tap : tap + 1, start : start + width]
                * ext_ref[pl.ds(5 + tap, BLOCK), start : start + width]
            )
        sig = jax.nn.sigmoid(acc)
        return acc * sig, sig * (1.0 + acc * (1.0 - sig))

    def back_unit(value, scale, grad):
        along = jnp.sum(value * grad, axis=-1, keepdims=True)
        return scale * grad - value * (scale * scale * scale * along)

    def inv_norm(value):
        return lax.rsqrt(jnp.sum(value * value, axis=-1, keepdims=True) + EPS_UNIT)

    results = {}

    def head_work(head):
        span = slice(head * value_dim, (head + 1) * value_dim)
        at = head * head_width
        out_at = head * full_width
        grad = mm(dmix_ref[...], wout_ref[:, span])
        gate = mm(hidden_ref[...], wgate_ref[:, span])
        yield
        sig = jax.nn.sigmoid(gate)
        silu = gate * sig
        mixed = mixed_ref[:, span]
        scale = lax.rsqrt(jnp.mean(mixed * mixed, axis=-1, keepdims=True) + EPS_NORM)
        unit_mixed = mixed * scale
        onorm = onorm_ref[...]
        grad_unit = grad * unit_mixed
        donorm_ref[...] += jnp.sum(grad_unit * silu, axis=0, keepdims=True)
        draw_ref[:, out_at + head_width : out_at + full_width] = (
            grad_unit * onorm * (sig * (1.0 + gate * (1.0 - sig)))
        ).astype(BF)
        grad_on = grad * onorm * silu
        along = jnp.mean(mixed * grad_on, axis=-1, keepdims=True)
        dmixed = scale * grad_on - mixed * (scale * scale * scale * along)
        dmixed_low = dmixed.astype(BF)
        yield

        query_pre, query_slope = conv(at, key_dim)
        key_pre, key_slope = conv(at + key_dim, key_dim)
        values, value_slope = conv(at + 2 * key_dim, value_dim)
        query_scale = inv_norm(query_pre)
        key_scale = inv_norm(key_pre)
        factor = key_dim ** (-0.5)
        query = query_pre * query_scale * factor
        keys = key_pre * key_scale
        beta = betas[:, heads + head : heads + head + 1]
        fading, strict = fades(total, total_t, head)
        query_low = query.astype(BF)
        key_low = keys.astype(BF)
        key_key = jnp.where(strict, mm_nt(key_low, key_low) * fading, 0.0)
        scores = mm_nt(query_low, key_low) * fading
        scores_low = scores.astype(BF)
        column = total[:, head : head + 1]
        last = total[BLOCK - 1 :, head : head + 1]
        grown = jnp.exp(column)
        rest = jnp.exp(last - column)
        key_fade = keys * rest
        key_fade_low = key_fade.astype(BF)
        yield

        state = state_ref[0, head]
        state_low = state.astype(BF)
        dstate = carry_ref[head]
        dstate_low = dstate.astype(BF)
        solved_low = solved_ref[0, head]
        key_part = solved_low[:, :key_dim]
        fresh = solved_low[:, key_dim:].astype(F32) - mm(key_part, state_low)
        fresh_low = fresh.astype(BF)
        yield
        dfresh = mm_tn(scores_low, dmixed_low) + mm(key_fade_low, dstate_low)
        dfresh_low = dfresh.astype(BF)
        yield
        carry_ref[head] = (
            jnp.exp(last) * dstate
            - mm_tn(keyw_ref[0, head], dstate_low)
            + mm_tn(query_eff_ref[0, head], dmixed_low)
        )
        dlast = jnp.exp(last) * jnp.sum(
            jnp.sum(state * dstate, axis=1, keepdims=True), axis=0, keepdims=True
        )
        yield
        dscores = mm_nt(dmixed_low, fresh_low)
        dquery_fade = mm_nt(dmixed_low, state_low)
        dkey_fade = mm_nt(fresh_low, dstate_low)
        dkey_part = -mm_nt(dfresh_low, state_low)
        yield
        dsolved = jnp.concatenate([dkey_part.astype(BF), dfresh_low], axis=1)
        dtargets = mm_tn(inv_ref[0, head], dsolved)
        yield
        dcoupling = -mm_nt(dtargets, solved_low)
        dkey_target = dtargets[:, :key_dim]
        dvalue_target = dtargets[:, key_dim:]

        yield
        pair = dcoupling * key_key
        dfade = beta * pair + dscores * scores
        dpair = (jnp.where(strict, dcoupling * (beta * fading), 0.0)).astype(BF)
        dquery_key = (dscores * fading).astype(BF)
        dquery = dquery_fade * grown + mm(dquery_key, key_low)
        fade_rows = jnp.sum(dkey_fade * key_fade, axis=-1, keepdims=True)
        grown_key = grown * keys
        target_rows = jnp.sum(dkey_target * grown_key, axis=-1, keepdims=True)
        dkeys = (
            dkey_fade * rest
            + dkey_target * (beta * grown)
            + mm(dpair, key_low)
            + mm_tn(dpair, key_low)
            + mm_tn(dquery_key, query_low)
        )
        yield
        dvalues = dvalue_target * beta
        dbeta = (
            jnp.sum(pair, axis=-1, keepdims=True)
            + target_rows
            + jnp.sum(dvalue_target * values, axis=-1, keepdims=True)
        )
        row_part = (
            jnp.sum(dfade, axis=-1, keepdims=True)
            + beta * target_rows
            + jnp.sum(dquery_fade * query, axis=-1, keepdims=True) * grown
            - fade_rows
        )
        dlast = dlast + jnp.sum(fade_rows, axis=0, keepdims=True)
        place = lax.broadcasted_iota(jnp.int32, (BLOCK, 1), 0)
        row_part = row_part + jnp.where(place == BLOCK - 1, dlast, 0.0)
        col_row = jnp.sum(dfade, axis=0, keepdims=True)
        results[head] = (row_part, col_row, dbeta)
        yield

        dquery_pre = back_unit(query_pre, query_scale, dquery * factor) * query_slope
        dkey_pre = back_unit(key_pre, key_scale, dkeys) * key_slope
        dext_ref[0:BLOCK, at : at + key_dim] = dquery_pre
        dext_ref[0:BLOCK, at + key_dim : at + 2 * key_dim] = dkey_pre
        dext_ref[0:BLOCK, at + 2 * key_dim : at + head_width] = dvalues * value_slope

    running = [head_work(head) for head in range(heads)]
    while running:
        running = [work for work in running if next(work, 0) is None]

    col_rows = [results[head][1] for head in range(heads)]
    col_part = jnp.concatenate(
        col_rows + [jnp.zeros((HALF - heads, BLOCK), F32)], axis=0
    ).T
    total_grad = -col_part
    small_grad = jnp.zeros((BLOCK, HALF), F32)
    for head in range(heads):
        total_grad = total_grad + jnp.where(lane == head, results[head][0], 0.0)
        small_grad = small_grad + jnp.where(lane == heads + head, results[head][2], 0.0)
    row, col = iota2(BLOCK, BLOCK)
    upper = jnp.where(row <= col, 1.0, 0.0).astype(F32)
    ddecay = mm_exact(upper, total_grad)
    dalpha = ddecay * (-rate_ref[...]) * jax.nn.sigmoid(shifted)
    dsmall_ref[0:1, :] += jnp.sum(ddecay * decays, axis=0, keepdims=True)
    dsmall_ref[1:2, :] += jnp.sum(dalpha, axis=0, keepdims=True)
    draw_ref[:, heads * full_width :] = (
        jnp.where(lane < heads, dalpha, small_grad * betas * (1.0 - betas))
    ).astype(BF)

    width = HALF
    for start in range(0, conv_width, width):
        span = slice(start, start + width)
        grad = dext_ref[0:BLOCK, span]
        acc = taps_ref[3:4, span] * grad
        for tap in range(3):
            acc = acc + taps_ref[tap : tap + 1, span] * dext_ref[pl.ds(3 - tap, BLOCK), span]
        out_at = (start // head_width) * full_width + start % head_width
        draw_ref[:, out_at : out_at + width] = acc.astype(BF)
        for tap in range(4):
            dtaps_ref[tap : tap + 1, span] += jnp.sum(
                grad * ext_ref[pl.ds(5 + tap, BLOCK), span], axis=0, keepdims=True
            )


def mixer_backward(place, part_rows, dmix, weights, saved, taps, rate, bias, onorm, heads):
    hidden, raw, mixed, states, inverses, solved, query_eff, keyw = saved
    rows, width = hidden.shape
    value_dim = onorm.shape[1]
    value_all = heads * value_dim
    conv_width = taps.shape[1]
    key_dim = states.shape[2]
    draw_width = conv_width + value_all + HALF
    steps = rows // BLOCK
    last = steps - 1
    whole = lambda shape, at=0: pl.BlockSpec(shape, lambda i, p: (0,) * (len(shape) - 1) + (at,))
    rows_of = lambda columns, at=0: pl.BlockSpec((BLOCK, columns), lambda i, p: (last - i, at))
    each = lambda a, b: pl.BlockSpec((1, heads, a, b), lambda i, p: (last - i, 0, 0, 0))
    shape = jax.ShapeDtypeStruct
    halo = pl.BlockSpec(
        (8, conv_width), lambda i, p: (jnp.maximum((last - i) * (BLOCK // 8) - 1, 0), 0)
    )

    return pl.pallas_call(
        functools.partial(backward_kernel, heads, SEQ // BLOCK),
        grid_spec=pltpu.PrefetchScalarGridSpec(
            num_scalar_prefetch=1,
            grid=(steps,),
            in_specs=[
                whole((part_rows, width)),
                whole((part_rows, width)),
                whole((part_rows, width)),
                whole((part_rows, width)),
                whole((width, value_all), 1),
                rows_of(conv_width + HALF),
                halo,
                rows_of(width),
                whole((width, value_all), 0),
                rows_of(value_all),
                each(key_dim, value_dim),
                each(BLOCK, BLOCK),
                each(BLOCK, key_dim + value_dim),
                each(BLOCK, key_dim),
                each(key_dim, key_dim),
                whole(taps.shape),
                whole(rate.shape),
                whole(bias.shape),
                whole(onorm.shape),
            ],
            out_specs=[
                rows_of(draw_width),
                whole((8, conv_width)),
                whole((8, HALF)),
                whole((1, value_dim)),
            ],
            scratch_shapes=[
                pltpu.VMEM((heads, key_dim, value_dim), F32),
                pltpu.VMEM((BLOCK + 8, conv_width), F32),
                pltpu.VMEM((BLOCK + 8, conv_width), F32),
                pltpu.VMEM((BLOCK, width), BF),
            ],
        ),
        out_shape=[
            shape((rows, draw_width), BF),
            shape((8, conv_width), F32),
            shape((8, HALF), F32),
            shape((1, value_dim), F32),
        ],
        compiler_params=pltpu.CompilerParams(
            dimension_semantics=("arbitrary",), vmem_limit_bytes=48 * 1024 * 1024
        ),
        cost_estimate=pl.CostEstimate(
            flops=rows * 24_000_000, bytes_accessed=rows * 50_000, transcendentals=0
        ),
        name="mixer_backward",
    )(
        place, *dmix, weights, raw, raw, hidden, weights, mixed, states, inverses, solved,
        query_eff, keyw, taps, rate, bias, onorm,
    )


def dot_plain(left_side, right_side):
    return jnp.dot(left_side, right_side, preferred_element_type=F32)


def dot_right_t(left_side, right_side):
    return lax.dot_general(
        left_side, right_side, (((1,), (1,)), ((), ())), preferred_element_type=F32
    )


def dot_left_t(left_side, right_side):
    return lax.dot_general(
        left_side, right_side, (((0,), (0,)), ((), ())), preferred_element_type=F32
    )


def hop(value, axis, flip):
    count = lax.axis_size(axis)
    return lax.ppermute(value, axis, [(i, i ^ flip) for i in range(count)])


def swap(value, flip):
    return hop(value, "tensor", flip)


def gather_blocks(block):
    far = swap(block, 2)
    near = swap(block, 1)
    return [block, near, far, swap(far, 1)]


def far_sum(parts):
    return (parts[2].astype(F32) + swap(parts[3].astype(BF), 1).astype(F32)).astype(BF)


def scatter_sum(parts):
    far = swap(far_sum(parts), 2).astype(F32)
    near = parts[0].astype(F32) + swap(parts[1].astype(BF), 1).astype(F32)
    return near + far


def by_permutes():
    return lax.axis_size("dp") in (2, 4, 8)


def gather_lines(piece):
    if not by_permutes():
        return [lax.all_gather(piece, "dp", axis=0, tiled=True)]
    return [piece] + [hop(piece, "dp", flip) for flip in range(2, lax.axis_size("dp"), 2)]


def gather_pairs(lines):
    if not by_permutes():
        return lines
    pieces = []
    for line in lines:
        pieces += [line, hop(line, "dp", 1)]
    return pieces


def sum_dp(value):
    return lax.psum_scatter(value, "dp", scatter_dimension=0, tiled=True).astype(F32)


def sum_small(value, axis):
    count = lax.axis_size(axis)
    if count not in (2, 4, 8):
        return lax.psum(value, axis)
    flip = 1
    while flip < count:
        value = value + hop(value, axis, flip)
        flip = 2 * flip
    return value


def pad_columns(value, width):
    return jnp.pad(value, ((0, 0), (0, width - value.shape[1])))


def round_up(value, unit):
    return -(-value // unit) * unit


def by_head(heads, *members):
    columns = []
    for head in range(heads):
        for member in members:
            span = member.shape[1] // heads
            columns.append(member[:, head * span : (head + 1) * span])
    return columns


def per_device(
    tokens,
    cotangent,
    norm1_gain,
    norm2_gain,
    query_weight,
    key_weight,
    value_weight,
    outgate_weight,
    alpha_weight,
    beta_weight,
    conv_query,
    conv_key,
    conv_value,
    decay_log,
    decay_bias,
    onorm_gain,
    output_weight,
    gate_weight,
    up_weight,
    down_weight,
):
    me = lax.axis_index("tensor")
    tensor_count = lax.axis_size("tensor")
    place = me[None].astype(jnp.int32)
    place_dp = lax.axis_index("dp")[None].astype(jnp.int32)
    part_rows = cotangent.shape[0]
    width = tokens.shape[1]
    heads = alpha_weight.shape[1]
    units = gate_weight.shape[1]
    padded = round_up(units, 256)
    key_dim = query_weight.shape[1] // heads
    value_dim = onorm_gain.shape[0]
    value_all = heads * value_dim
    head_width = 2 * key_dim + value_dim

    small = pad_columns(jnp.concatenate([alpha_weight, beta_weight], axis=1), HALF)
    lines = gather_lines(
        jnp.concatenate(
            by_head(heads, query_weight, key_weight, value_weight) + [small], axis=1
        )
    )
    pieces = gather_pairs(lines)
    if len(pieces) == 1:
        place_dp = jnp.zeros_like(place_dp)
    pieces, cot_local, gate_out_local, ffn_local = lax.optimization_barrier(
        (
            pieces,
            cotangent,
            jnp.concatenate([outgate_weight, output_weight.T], axis=1),
            jnp.concatenate(
                [
                    pad_columns(gate_weight, padded),
                    pad_columns(up_weight, padded),
                    pad_columns(down_weight.T, padded),
                ],
                axis=1,
            ),
        )
    )
    w_gate_out = lax.all_gather(gate_out_local, "dp", axis=0, tiled=True)
    w_ffn = lax.all_gather(ffn_local, "dp", axis=0, tiled=True)
    w_pair = w_ffn[:, : 2 * padded]
    w_down_t = w_ffn[:, 2 * padded :]
    cot_blocks = gather_blocks(cot_local)

    taps = jnp.concatenate(by_head(heads, conv_query, conv_key, conv_value), axis=1)
    rate = pad_columns(jnp.exp(decay_log)[None], HALF)
    bias = pad_columns(decay_bias[None], HALF)
    onorm = onorm_gain[None]
    w_first, hidden_one, raw, mixed, *saved = mixer_forward(
        tokens, norm1_gain[None], pieces, place_dp, taps, rate, bias, heads, value_dim
    )
    hidden_one, mixed, cot_far = lax.optimization_barrier((hidden_one, mixed, cot_blocks[2]))
    cot_blocks[2] = cot_far
    normed_blocks, mixer_parts = [None] * 4, [None] * 4
    for first in (3, 1):
        found = gated_out(place, first, part_rows, hidden_one, mixed, w_gate_out, onorm, heads)
        normed_blocks[first], normed_blocks[first - 1] = found[0], found[1]
        mixer_parts[first], mixer_parts[first - 1] = found[2], found[3]
    w_gates = w_gate_out[:, :value_all]
    columns = []
    for head in range(heads):
        columns.append(w_first[:, head * head_width : (head + 1) * head_width])
        columns.append(w_gates[:, head * value_dim : (head + 1) * value_dim])
    columns.append(w_first[:, heads * head_width :])
    w_all = jnp.concatenate(columns, axis=1)

    def block_of(value, flip):
        return lax.dynamic_slice_in_dim(value, (me ^ flip) * part_rows, part_rows, 0)

    mixer_rows = scatter_sum(mixer_parts)
    inputs = block_of(tokens, 0).astype(F32)
    middle = inputs + mixer_rows
    inverse_two = lax.rsqrt(jnp.mean(middle * middle, axis=-1, keepdims=True) + EPS_NORM)
    unit_two = middle * inverse_two
    hidden_blocks = gather_blocks((unit_two * norm2_gain).astype(BF))

    def feed_forward(first, second):
        hidden = jnp.concatenate([hidden_blocks[first], hidden_blocks[second]], axis=0)
        cot = jnp.concatenate([cot_blocks[first], cot_blocks[second]], axis=0)
        pair = dot_plain(hidden, w_pair)
        gate, upward = pair[:, :padded], pair[:, padded:]
        sig = jax.nn.sigmoid(gate)
        silu = gate * sig
        active = (silu * upward).astype(BF)
        active_grad = dot_plain(cot, w_down_t)
        pair_grad = jnp.concatenate(
            [
                (active_grad * upward * (sig * (1.0 + gate * (1.0 - sig)))).astype(BF),
                (active_grad * silu).astype(BF),
            ],
            axis=1,
        )
        hidden_part = dot_right_t(pair_grad, w_pair).astype(BF)
        return hidden, cot, active, pair_grad, hidden_part

    near = feed_forward(1, 0)
    far = feed_forward(3, 2)
    hidden_two_grad = scatter_sum(
        [near[4][part_rows:], near[4][:part_rows], far[4][part_rows:], far[4][:part_rows]]
    )
    gain_two_part = jnp.sum(hidden_two_grad * unit_two, axis=0)
    gained_two = hidden_two_grad * norm2_gain
    middle_grad = (
        cotangent.astype(F32)
        + inverse_two * gained_two
        - unit_two * inverse_two * inverse_two * jnp.mean(middle * gained_two, axis=-1, keepdims=True)
    )
    ffn_grad = jnp.concatenate(
        [
            (dot_left_t(near[0], near[3]) + dot_left_t(far[0], far[3])).astype(BF),
            (dot_left_t(near[1], near[2]) + dot_left_t(far[1], far[2])).astype(BF),
        ],
        axis=1,
    )
    ffn_total = sum_dp(ffn_grad)
    middle_rows, ffn_grad = lax.optimization_barrier((middle_grad.astype(BF), ffn_grad))
    middle_blocks = gather_blocks(middle_rows)
    near_branch = dot_right_t(near[2], w_down_t).astype(BF)
    far_branch = dot_right_t(far[2], w_down_t).astype(BF)
    branch_near = near_branch[part_rows:].astype(F32) + swap(near_branch[:part_rows], 1).astype(F32)
    branch_far = far_sum([None, None, far_branch[part_rows:], far_branch[:part_rows]])
    middle_blocks, branch_near, branch_far, w_all = lax.optimization_barrier(
        (middle_blocks, branch_near, branch_far, w_all)
    )
    block_output = (middle + branch_near + swap(branch_far, 2).astype(F32)).astype(BF)

    draw, dtaps, dsmall, donorm = mixer_backward(
        place,
        part_rows,
        middle_blocks,
        w_gate_out,
        (hidden_one, raw, mixed) + tuple(saved),
        taps,
        rate,
        bias,
        onorm,
        heads,
    )
    output_grad = sum(dot_left_t(block, rows) for block, rows in zip(middle_blocks, normed_blocks))
    weight_grad = dot_left_t(hidden_one, draw)
    gain_one_part = jnp.sum(weight_grad * w_all.astype(F32), axis=1) / norm1_gain
    weight_grad = jnp.concatenate([weight_grad.astype(BF), output_grad.astype(BF)], axis=1)
    weight_grad, draw = lax.optimization_barrier((weight_grad, draw))
    mixer_total = sum_dp(weight_grad)

    def hidden_part(value, flip):
        return dot_right_t(block_of(value, flip), w_all)

    far_low = far_sum([None, None, hidden_part(draw, 2), hidden_part(draw, 3)])
    far_low, draw, gain_one_part = lax.optimization_barrier((far_low, draw, gain_one_part))
    hidden_one_grad = (
        swap(far_low, 2).astype(F32)
        + hidden_part(draw, 0)
        + swap(hidden_part(draw, 1).astype(BF), 1).astype(F32)
    )
    full_width = head_width + value_dim
    output_total = mixer_total[:, draw.shape[1] :]
    smalls = mixer_total[:, heads * full_width : draw.shape[1]]
    totals = [
        mixer_total[:, head * full_width : (head + 1) * full_width] for head in range(heads)
    ]

    inverse_one = lax.rsqrt(jnp.mean(inputs * inputs, axis=-1, keepdims=True) + EPS_NORM)
    unit_one = inputs * inverse_one
    gained = hidden_one_grad * norm1_gain
    tokens_grad = (
        middle_grad
        + inverse_one * gained
        - unit_one * inverse_one * inverse_one * jnp.mean(inputs * gained, axis=-1, keepdims=True)
    )

    tap_count = taps.shape[0]
    shared = sum_small(
        jnp.stack(
            [gain_one_part, gain_two_part, jnp.pad(donorm[0], (0, width - value_dim))]
        ),
        "tensor",
    )
    tap_sums = dtaps[:tap_count]
    table_width = max(tap_sums.shape[1], width)
    table = sum_small(
        jnp.concatenate(
            [
                pad_columns(tap_sums, table_width),
                pad_columns(shared, table_width),
                pad_columns(dsmall[:2], table_width),
            ],
            axis=0,
        ),
        "dp",
    )
    shared = table[tap_count : tap_count + 3]
    own_total = table[tap_count + 3 :]
    gain_share = width // tensor_count
    onorm_share = value_dim // tensor_count

    def collect(values, start, span):
        return jnp.concatenate([value[:, start : start + span] for value in values], axis=1)

    table_heads = [
        table[:tap_count, head * head_width : (head + 1) * head_width] for head in range(heads)
    ]
    return (
        block_output,
        tokens_grad,
        lax.dynamic_slice_in_dim(shared[0], me * gain_share, gain_share, 0),
        lax.dynamic_slice_in_dim(shared[1], me * gain_share, gain_share, 0),
        collect(totals, 0, key_dim),
        collect(totals, key_dim, key_dim),
        collect(totals, 2 * key_dim, value_dim),
        collect(totals, head_width, value_dim),
        smalls[:, :heads],
        smalls[:, heads : 2 * heads],
        collect(table_heads, 0, key_dim),
        collect(table_heads, key_dim, key_dim),
        collect(table_heads, 2 * key_dim, value_dim),
        own_total[0, :heads],
        own_total[1, :heads],
        lax.dynamic_slice_in_dim(shared[2], me * onorm_share, onorm_share, 0),
        output_total.T,
        ffn_total[:, :units],
        ffn_total[:, padded : padded + units],
        ffn_total[:, 2 * padded : 2 * padded + units].T,
    )


def solution(mesh):
    return jax.shard_map(
        per_device,
        mesh=mesh,
        in_specs=(
            P("dp", None),
            P(("dp", "tensor"), None),
            P(),
            P(),
            P("dp", "tensor"),
            P("dp", "tensor"),
            P("dp", "tensor"),
            P("dp", "tensor"),
            P("dp", "tensor"),
            P("dp", "tensor"),
            P(None, "tensor"),
            P(None, "tensor"),
            P(None, "tensor"),
            P("tensor"),
            P("tensor"),
            P(),
            P("tensor", "dp"),
            P("dp", "tensor"),
            P("dp", "tensor"),
            P("tensor", "dp"),
        ),
        out_specs=(
            P(("dp", "tensor"), None),
            P(("dp", "tensor"), None),
            P("tensor"),
            P("tensor"),
            P("dp", "tensor"),
            P("dp", "tensor"),
            P("dp", "tensor"),
            P("dp", "tensor"),
            P("dp", "tensor"),
            P("dp", "tensor"),
            P(None, "tensor"),
            P(None, "tensor"),
            P(None, "tensor"),
            P("tensor"),
            P("tensor"),
            P("tensor"),
            P("tensor", "dp"),
            P("dp", "tensor"),
            P("dp", "tensor"),
            P("tensor", "dp"),
        ),
        check_vma=False,
    )
```

time: 827 us -> 485 us (0.59)
  waiting for transfers between devices: 533 us -> 161 us
  matrix products: 103 us -> 81.4 us
  starting transfers between devices: 12.6 us -> 28.8 us
  other arithmetic: 23.8 us -> 36 us
  local copies, waits for them, and re-layouts: 31.8 us -> 43.3 us
  Pallas kernels: 101 us -> 112 us
    reduce_scatter x3 -> x2, waiting for transfers between devices: 169 us -> 18.6 us  [sum_dp(): lax.psum_scatter(value, 'dp', scatter_dimension=0, tiled=True).astype(F32)]
    psum x1 -> x0, waiting for transfers between devices: 122 us -> none  [per_device(): table = lax.psum(table, ('dp', 'tensor'))]
    all_gather x2, waiting for transfers between devices: 105 us -> 7.73 us  [the longest x1 4.05 us: per_device(): w_ffn = lax.all_gather(ffn_local, 'dp', axis=0, tiled=True)]
    ppermute x21 -> x33, starting transfers between devices: 12.4 us -> 28.6 us  [hop(): return lax.ppermute(value, axis, [(i, i ^ flip) for i in range(count)])]
    unnamed x85 -> x125, local copies, waits for them, and re-layouts: 14.6 us -> 30.2 us
    dot_general x10 -> x8, matrix products: 42.3 us -> 31.6 us  [dot_right_t(): lax.dot_general(left_side, right_side, (((1,), (1,)), ((), ())), preferre...]
    dot_general x4 -> x9, matrix products: 36.8 us -> 29.4 us  [dot_left_t(): lax.dot_general(left_side, right_side, (((0,), (0,)), ((), ())), preferre...]
    pallas_call x1 -> x3, Pallas kernels: 47 us -> 53.1 us  [the longest x1 43.3 us: mixer_forward(): pl.pallas_call(functools.partial(forward_kernel, heads, SEQ // BLOCK, len...]
  transfers between devices with their start and end apart: 27 -> 37, of which waited for: 15 -> 18; matrix products, arithmetic and copies ran while one was open for 12% -> 28% of each run, Pallas kernels for 6% -> 23%
where the time goes in v2:
time: 485 us; the launch traced here: 478 us
  waiting for transfers between devices  161 us (33%)
  Pallas kernels  112 us (23%)
  matrix products  81.4 us (17%)
  local copies, waits for them, and re-layouts  43.3 us (9%)
  other arithmetic  36 us (7%)
  starting transfers between devices  28.8 us (6%)
  between operations  14.8 us (3%)
    ppermute x33, waiting for transfers between devices, hop(): return lax.ppermute(value, axis, [(i, i ^ flip) for i in range(count)])  135 us
    pallas_call x1, Pallas kernels, mixer_backward(): pl.pallas_call(functools.partial(backward_kernel, heads, SEQ // BLOCK), g...  58.8 us
    pallas_call x1, Pallas kernels, mixer_forward(): pl.pallas_call(functools.partial(forward_kernel, heads, SEQ // BLOCK, len...  43.3 us
    dot_general x8, matrix products, dot_right_t(): lax.dot_general(left_side, right_side, (((1,), (1,)), ((), ())), preferre...  31.6 us
    unnamed x125, local copies, waits for them, and re-layouts  30.2 us
    dot_general x9, matrix products, dot_left_t(): lax.dot_general(left_side, right_side, (((0,), (0,)), ((), ())), preferre...  29.4 us
    ppermute x33, starting transfers between devices, hop(): return lax.ppermute(value, axis, [(i, i ^ flip) for i in range(count)])  28.6 us
    dot_general x4, matrix products, dot_plain(): return jnp.dot(left_side, right_side, preferred_element_type=F32)  20.5 us
  transfers between devices with their start and end apart: 37, of which 18 were waited for; matrix products, arithmetic and copies ran while one was open for 28% of the time, Pallas kernels for 23%

profile of v2, /device:TPU:0, one launch (start us, length us, event | category | flops | bytes accessed | tf_op | source)
XLA Modules:
  0.0 477.6 jit_solution(13930301840434032801)
XLA Ops:
  22.9 5.6 %collective-permute-done.1.refs_2_ = bf16[128,1152]{1,0:T(8,128)(2,1)S(1)} collective-permute-done((bf16[128,1152]{1,0:T(8,128)(2,1)S(1)}, bf16[128,1152]{1,0:T(8,128)(2,1)S(1)}, u32[]{:S(2)}, u32[]{:S(2)}) %collective-permute-start.1) | collective-permute-done | bytes 294944 | tf_op jit(solution)/shard_map/ppermute | solution.py:686
  30.2 9.3 %collective-permute-done.3.refs_4_ = bf16[128,1152]{1,0:T(8,128)(2,1)S(1)} collective-permute-done((bf16[128,1152]{1,0:T(8,128)(2,1)S(1)}, bf16[128,1152]{1,0:T(8,128)(2,1)S(1)}, u32[]{:S(2)}, u32[]{:S(2)}) %collective-permute-start.3) | collective-permute-done | bytes 294944 | tf_op jit(solution)/shard_map/ppermute | solution.py:686
  51.3 43.3 %mixer_forward.1 = (bf16[1024,1152]{1,0:T(8,128)(2,1)}, bf16[2048,1024]{1,0:T(8,128)(2,1)}, f32[2048,1152]{1,0:T(8,128)}, f32[2048,512]{1,0:T(8,128)}, f32[8,2,1...) custom-call(s32[1]{0:T(128)} %bitcast.1.place_ref, ...), custom_call_target="tpu_custom_call" | custom-call | flops 40960000000 | bytes 122880000 | tf_op jit(solution)/shard_map/mixer_forward/pallas_call | solution.py:222
  102.3 4.7 gated_out.3
  107.1 5.1 %gated_out.2 = (bf16[512,512]{1,0:T(8,128)(2,1)S(1)}, bf16[512,512]{1,0:T(8,128)(2,1)S(1)}, bf16[512,1024]{1,0:T(8,128)(2,1)S(1)}, bf16[512,1024]{1,0:T(8,128)(2,1)S(1)}) custom-call(s32[1]{0:T(128)} %bitcast.place_ref, bf16[2048,1024]{1,0:T(8,128)(2,1)} %get-tuple-element.79.hidden_ref.all_refs_7_, f32[2048,512]{1,0:T(8,128)} %get-tuple-element.80.mixed_ref.all_refs_9_, ...), custom_call_target="tpu_custom_call" | custom-call | flops 4096000000 | bytes 12288000 | tf_op jit(solution)/shard_map/gated_out/pallas_call | solution.py:311
  115.6 24.0 %collective-permute-done.10 = bf16[512,1024]{1,0:T(8,128)(2,1)} collective-permute-done((bf16[512,1024]{1,0:T(8,128)(2,1)}, bf16[512,1024]{1,0:T(8,128)(2,1)}, u32[]{:S(2)}, u32[]{:S(2)}) %collective-permute-start.10) | collective-permute-done | bytes 1048608 | tf_op jit(solution)/shard_map/ppermute | solution.py:686
  144.5 22.3 %collective-permute-done.15 = bf16[512,1024]{1,0:T(8,128)(2,1)S(1)} collective-permute-done((bf16[512,1024]{1,0:T(8,128)(2,1)S(1)}, bf16[512,1024]{1,0:T(8,128)(2,1)S(1)}, u32[]{:S(2)}, u32[]{:S(2)}) %collective-permute-start.15) | collective-permute-done | bytes 1048608 | tf_op jit(solution)/shard_map/ppermute | solution.py:686
  182.3 6.2 %fusion.12 = f32[1024,1536]{0,1:T(8,128)S(1)} fusion(bf16[1024,1024]{1,0:T(8,128)(2,1)} %constant_dynamic-update-slice_fusion.15, bf16[1024,2304]{0,1:T(8,128)(2,1)} %all-gather.5.cloned.1.call-done), kind=kOutput, calls=%fused_computation.46 | convolution fusion | flops 3221225472 | bytes 11534336 | tf_op jit(solution)/shard_map/dot_general | solution.py:669
  196.3 5.1 %fusion.8 = f32[1024,1536]{1,0:T(8,128)S(1)} fusion(bf16[1024,1024]{1,0:T(8,128)(2,1)} %constant_dynamic-update-slice_fusion.15, bf16[1024,768]{0,1:T(8,128)(2,1)S(1)} %get-tuple-element.167, bf16[1024,768]{0,1:T(8,128)(2,1)S(1)} %get-tuple-element.166), kind=kOutput, calls=%fused_computation.42 | convolution fusion | flops 3227516928 | bytes 11534336 | tf_op jit(solution)/shard_map/dot_general | solution.py:679
  201.4 5.3 %fusion.15 = f32[1024,1536]{0,1:T(8,128)} fusion(bf16[1024,2304]{0,1:T(8,128)(2,1)S(1)} %copy-done.37, bf16[512,1024]{1,0:T(8,128)(2,1)S(1)} %multiply_convert_fusion.6, bf16[512,1024]{1,0:T(8,128)(2,1)S(1)} %collective-permute-done.12), kind=kOutput, calls=%fused_computation.49 | convolution fusion | flops 3225419776 | bytes 11534336 | tf_op jit(solution)/shard_map/dot_general | solution.py:669
  206.8 5.0 %multiply_convert_fusion.5 = (bf16[1024,768]{0,1:T(8,128)(2,1)S(1)}, bf16[1024,768]{0,1:T(8,128)(2,1)S(1)}, bf16[1024,768]{0,1:T(8,128)(2,1)S(1)}) fusion(f32[1024,1536]{0,1:T(8,128)} %fusion.15, bf16[1024,1024]{1,0:T(8,128)(2,1)S(1)} %copy-done.32, bf16[1024,2304]{0,1:T(8,128)(2,1)S(1)} %copy-done.37), kind=kOutput, calls=%fused_computation.18 | convolution fusion | flops 1622409216 | bytes 14680064 | tf_op jit(solution)/shard_map/dot_general | solution.py:669
  220.5 5.4 %add_convert_fusion = bf16[1024,1536]{1,0:T(8,128)(2,1)S(1)} fusion(f32[1024,1536]{1,0:T(8,128)S(1)} %fusion.8, bf16[1024,768]{0,1:T(8,128)(2,1)} %copy-done.47, bf16[1024,768]{0,1:T(8,128)(2,1)} %copy-done.46, bf16[512,1024]{1,0:T(8,128)(2,1)S(1)} %multiply_convert_fusion.6, bf16[512,1024]{1,0:T(8,128)(2,1)S(1)} %collective-permute-done.12), kind=kOutput, calls=%fused_computation.1 | convolution fusion | flops 3234856960 | bytes 14680064 | tf_op jit(solution)/shard_map/dot_general | solution.py:679
  233.1 19.6 %collective-permute-done.18 = bf16[512,1024]{1,0:T(8,128)(2,1)} collective-permute-done((bf16[512,1024]{1,0:T(8,128)(2,1)}, bf16[512,1024]{1,0:T(8,128)(2,1)}, u32[]{:S(2)}, u32[]{:S(2)}) %collective-permute-start.18) | collective-permute-done | bytes 1048608 | tf_op jit(solution)/shard_map/ppermute | solution.py:686
  255.7 4.4 fusion.63
  272.5 11.8 %collective-permute-done.20.all_refs_2_ = bf16[512,1024]{1,0:T(8,128)(2,1)S(1)} collective-permute-done((bf16[512,1024]{1,0:T(8,128)(2,1)S(1)}, bf16[512,1024]{1,0:T(8,128)(2,1)S(1)}, u32[]{:S(2)}, u32[]{:S(2)}) %collective-permute-start.20) | collective-permute-done | bytes 1048608 | tf_op jit(solution)/shard_map/ppermute | solution.py:686
  297.9 58.8 %mixer_backward.1 = (bf16[2048,1664]{1,0:T(8,128)(2,1)}, f32[8,1024]{1,0:T(8,128)S(1)}, f32[8,128]{1,0:T(8,128)S(1)}, f32[1,256]{1,0:T(1,128)S(1)}) custom-call(s32[1]{0:T(128)} %bitcast.place_ref, bf16[512,1024]{1,0:T(8,128)(2,1)S(1)} %get-tuple-element.92.all_refs_0_, bf16[512,1024]{1,0:T(8,128)(2,1)S(1)} %collective-permute-done.19.all_refs_1_, ...), custom_call_target="tpu_custom_call" | custom-call | flops 49152000000 | bytes 102400000 | tf_op jit(solution)/shard_map/mixer_backward/pallas_call | solution.py:610
  356.7 12.1 %multiply_reduce_fusion = (f32[1024]{0:T(1024)S(1)}, bf16[1024,1664]{1,0:T(8,128)(2,1)S(1)}) fusion(bf16[1024,1664]{1,0:T(8,128)(2,1)} %slice_dynamic-update-slice_fusion.4, bf16[2048,1024]{1,0:T(8,128)(2,1)S(1)} %copy-done.41, bf16[2048,1664]{1,0:T(8,128)(2,1)} %get-tuple-element.110), kind=kOutput, calls=%fused_computation | convolution fusion | flops 6986136576 | bytes 17829888 | tf_op jit(solution)/shard_map/dot_general | solution.py:679
  371.3 4.6 fusion.31
  378.8 5.8 %add_convert_fusion.2 = bf16[512,1024]{1,0:T(8,128)(2,1)} fusion(bf16[512,1024]{1,0:T(8,128)(2,1)} %collective-permute-done.25, bf16[1024,1664]{1,0:T(8,128)(2,1)} %slice_dynamic-update-slice_fusion.4, bf16[2048,1664]{1,0:T(8,128)(2,1)} %get-tuple-element.110, s32[]{:T(128)S(6)} %select_n.21), kind=kOutput, calls=%fused_computation.30 | convolution fusion | flops 1746403328 | bytes 7208964 | tf_op jit(solution)/shard_map/dot_general | solution.py:673
  394.2 4.9 %fusion.34 = bf16[512,1024]{1,0:T(8,128)(2,1)S(1)} fusion(bf16[1024,1664]{1,0:T(8,128)(2,1)} %slice_dynamic-update-slice_fusion.4, bf16[2048,1664]{1,0:T(8,128)(2,1)} %get-tuple-element.110, s32[]{:T(128)S(6)} %select_n.23), kind=kOutput, calls=%fused_computation.66 | convolution fusion | flops 1745354752 | bytes 6160388 | tf_op jit(solution)/shard_map/dot_general | solution.py:673
  403.3 10.2 %collective-permute-done.24 = bf16[512,1024]{1,0:T(8,128)(2,1)S(1)} collective-permute-done((bf16[512,1024]{1,0:T(8,128)(2,1)S(1)}, bf16[512,1024]{1,0:T(8,128)(2,1)S(1)}, u32[]{:S(2)}, u32[]{:S(2)}) %collective-permute-start.24) | collective-permute-done | bytes 1048608 | tf_op jit(solution)/shard_map/ppermute | solution.py:686
  418.0 17.1 %collective-permute-done.26 = bf16[512,1024]{1,0:T(8,128)(2,1)S(1)} collective-permute-done((bf16[512,1024]{1,0:T(8,128)(2,1)S(1)}, bf16[512,1024]{1,0:T(8,128)(2,1)S(1)}, u32[]{:S(2)}, u32[]{:S(2)}) %collective-permute-start.26) | collective-permute-done | bytes 1048608 | tf_op jit(solution)/shard_map/ppermute | solution.py:686
  435.1 5.0 %fusion.2 = (f32[512]{0:T(512)S(1)}, f32[512]{0:T(512)S(1)}, f32[512,1024]{1,0:T(8,128)S(1)}) fusion(bf16[2048,1024]{1,0:T(8,128)(2,1)S(1)} %copy-done.28, s32[]{:T(128)S(6)} %select_n.20, f32[1024]{0:T(1024)S(1)} %copy-done.7, bf16[512,1024]{1,0:T(8,128)(2,1)S(1)} %collective-permute-done.27, bf16[512,1024]{1,0:T(8,128)(2,1)S(1)} %collective-permute-done.26, ...), kind=kOutput, calls=%fused_computation.21 | convolution fusion | flops 1750072320 | bytes 10363904 | tf_op jit(solution)/shard_map/dot_general | solution.py:673
  446.4 18.6 %reduce-scatter.3.cloned.1.call-done = bf16[128,2176]{1,0:T(8,128)(2,1)} async-done(((bf16[1024,2176]{1,0:T(8,128)(2,1)}), bf16[128,2176]{1,0:T(8,128)(2,1)}) %reduce-scatter.3.cloned.1.call-update) | async-done | bytes 557072 | tf_op jit(solution)/shard_map/reduce_scatter | solution.py:729
  (266 shorter events, 148.6 us)
Async XLA Ops:
  7.3 93.4 %all-gather.3.cloned.1.call-start = ((), (), s32[]{:S(2)}) async-start(), calls=%async_computation.2 | async-start | bytes 2359296 | tf_op jit(solution)/shard_map/all_gather | solution.py:820
  12.9 15.6 %collective-permute-start.1 = (bf16[128,1152]{1,0:T(8,128)(2,1)S(1)}, bf16[128,1152]{1,0:T(8,128)(2,1)S(1)}, u32[]{:S(2)}, u32[]{:S(2)}) collective-permute-start(bf16[128,1152]{1,0:T(8,128)(2,1)S(1)} %constant_dynamic-update-slice_fusion.6.refs_0_), channel_id=1, source_target_pairs={{0,8},{4,12},{8,0},{12,4},{16,24},{20,28},{24,16},{28,20},{1,9},{5... | collective-permute-start | bytes 884744 | tf_op jit(solution)/shard_map/ppermute | solution.py:686
  16.0 23.5 %collective-permute-start.3 = (bf16[128,1152]{1,0:T(8,128)(2,1)S(1)}, bf16[128,1152]{1,0:T(8,128)(2,1)S(1)}, u32[]{:S(2)}, u32[]{:S(2)}) collective-permute-start(bf16[128,1152]{1,0:T(8,128)(2,1)S(1)} %constant_dynamic-update-slice_fusion.6.refs_0_), channel_id=1, source_target_pairs={{0,16},{4,20},{8,24},{12,28},{16,0},{20,4},{24,8},{28,12},{1,17},{... | collective-permute-start | bytes 884744 | tf_op jit(solution)/shard_map/ppermute | solution.py:686
  18.6 22.4 %collective-permute-start.5 = (bf16[128,1152]{1,0:T(8,128)(2,1)S(1)}, bf16[128,1152]{1,0:T(8,128)(2,1)S(1)}, u32[]{:S(2)}, u32[]{:S(2)}) collective-permute-start(bf16[128,1152]{1,0:T(8,128)(2,1)S(1)} %constant_dynamic-update-slice_fusion.6.refs_0_), channel_id=1, source_target_pairs={{0,24},{4,28},{8,16},{12,20},{16,8},{20,12},{24,0},{28,4},{1,25},{... | collective-permute-start | bytes 884744 | tf_op jit(solution)/shard_map/ppermute | solution.py:686
  18.6 24.9 %collective-permute-start = (bf16[128,1152]{1,0:T(8,128)(2,1)S(1)}, bf16[128,1152]{1,0:T(8,128)(2,1)S(1)}, u32[]{:S(2)}, u32[]{:S(2)}) collective-permute-start(bf16[128,1152]{1,0:T(8,128)(2,1)S(1)} %constant_dynamic-update-slice_fusion.6.refs_0_), channel_id=1, source_target_pairs={{0,4},{4,0},{8,12},{12,8},{16,20},{20,16},{24,28},{28,24},{1,5},{5... | collective-permute-start | bytes 884744 | tf_op jit(solution)/shard_map/ppermute | solution.py:686
  49.4 132.9 %all-gather.5.cloned.1.call-start = ((), (), s32[]{:S(2)}) async-start(), calls=%async_computation.3 | async-start | bytes 5308416 | tf_op jit(solution)/shard_map/all_gather | solution.py:821
  49.6 47.4 %collective-permute-start.7 = (bf16[512,1024]{1,0:T(8,128)(2,1)}, bf16[512,1024]{1,0:T(8,128)(2,1)}, u32[]{:S(2)}, u32[]{:S(2)}) collective-permute-start(bf16[512,1024]{1,0:T(8,128)(2,1)} %param.21), channel_id=1, source_target_pairs={{0,2},{1,3},{2,0},{3,1},{4,6},{5,7},{6,4},{7,5},{8,10},{9,11},{10,... | collective-permute-start | bytes 3145736 | tf_op jit(solution)/shard_map/ppermute | solution.py:686
  51.2 391.2 %reduce-scatter.5.cloned.1.call-start = ((), (), s32[]{:S(2)}) async-start(), calls=%async_computation.5 | async-start | bytes 5308416 | tf_op jit(solution)/shard_map/reduce_scatter | solution.py:729
  114.2 25.4 %collective-permute-start.10 = (bf16[512,1024]{1,0:T(8,128)(2,1)}, bf16[512,1024]{1,0:T(8,128)(2,1)}, u32[]{:S(2)}, u32[]{:S(2)}) collective-permute-start(bf16[512,1024]{1,0:T(8,128)(2,1)} %add_convert_fusion.7), channel_id=1, source_target_pairs={{0,2},{1,3},{2,0},{3,1},{4,6},{5,7},{6,4},{7,5},{8,10},{9,11},{10,... | collective-permute-start | bytes 3145736 | tf_op jit(solution)/shard_map/ppermute | solution.py:686
  142.5 24.3 %collective-permute-start.15 = (bf16[512,1024]{1,0:T(8,128)(2,1)S(1)}, bf16[512,1024]{1,0:T(8,128)(2,1)S(1)}, u32[]{:S(2)}, u32[]{:S(2)}) collective-permute-start(bf16[512,1024]{1,0:T(8,128)(2,1)S(1)} %multiply_convert_fusion.6), channel_id=1, source_target_pairs={{0,2},{1,3},{2,0},{3,1},{4,6},{5,7},{6,4},{7,5},{8,10},{9,11},{10,... | collective-permute-start | bytes 3145736 | tf_op jit(solution)/shard_map/ppermute | solution.py:686
  144.0 25.2 %collective-permute-start.11 = (bf16[512,1024]{1,0:T(8,128)(2,1)}, bf16[512,1024]{1,0:T(8,128)(2,1)S(1)}, u32[]{:S(2)}, u32[]{:S(2)}) collective-permute-start(bf16[512,1024]{1,0:T(8,128)(2,1)} %param.21), channel_id=1, source_target_pairs={{0,1},{1,0},{2,3},{3,2},{4,5},{5,4},{6,7},{7,6},{8,9},{9,8},{10,11... | collective-permute-start | bytes 3145736 | tf_op jit(solution)/shard_map/ppermute | solution.py:686
  144.0 28.0 %collective-permute-start.14 = (bf16[512,1024]{1,0:T(8,128)(2,1)}, bf16[512,1024]{1,0:T(8,128)(2,1)S(1)}, u32[]{:S(2)}, u32[]{:S(2)}) collective-permute-start(bf16[512,1024]{1,0:T(8,128)(2,1)} %collective-permute-done.7), channel_id=1, source_target_pairs={{0,1},{1,0},{2,3},{3,2},{4,5},{5,4},{6,7},{7,6},{8,9},{9,8},{10,11... | collective-permute-start | bytes 3145736 | tf_op jit(solution)/shard_map/ppermute | solution.py:686
  175.6 25.8 %collective-permute-start.12 = (bf16[512,1024]{1,0:T(8,128)(2,1)S(1)}, bf16[512,1024]{1,0:T(8,128)(2,1)S(1)}, u32[]{:S(2)}, u32[]{:S(2)}) collective-permute-start(bf16[512,1024]{1,0:T(8,128)(2,1)S(1)} %multiply_convert_fusion.6), channel_id=1, source_target_pairs={{0,1},{1,0},{2,3},{3,2},{4,5},{5,4},{6,7},{7,6},{8,9},{9,8},{10,11... | collective-permute-start | bytes 3145736 | tf_op jit(solution)/shard_map/ppermute | solution.py:686
  196.3 29.6 %collective-permute-start.17 = (bf16[512,1024]{1,0:T(8,128)(2,1)S(1)}, bf16[512,1024]{1,0:T(8,128)(2,1)S(1)}, u32[]{:S(2)}, u32[]{:S(2)}) collective-permute-start(bf16[512,1024]{1,0:T(8,128)(2,1)S(1)} %slice.272), channel_id=1, source_target_pairs={{0,1},{1,0},{2,3},{3,2},{4,5},{5,4},{6,7},{7,6},{8,9},{9,8},{10,11... | collective-permute-start | bytes 3145736 | tf_op jit(solution)/shard_map/ppermute | solution.py:686
  218.1 15.0 %collective-permute-start.13 = (bf16[512,1024]{1,0:T(8,128)(2,1)}, bf16[512,1024]{1,0:T(8,128)(2,1)}, u32[]{:S(2)}, u32[]{:S(2)}) collective-permute-start(bf16[512,1024]{1,0:T(8,128)(2,1)} %slice.268), channel_id=1, source_target_pairs={{0,1},{1,0},{2,3},{3,2},{4,5},{5,4},{6,7},{7,6},{8,9},{9,8},{10,11... | collective-permute-start | bytes 3145736 | tf_op jit(solution)/shard_map/ppermute | solution.py:686
  227.3 25.4 %collective-permute-start.18 = (bf16[512,1024]{1,0:T(8,128)(2,1)}, bf16[512,1024]{1,0:T(8,128)(2,1)}, u32[]{:S(2)}, u32[]{:S(2)}) collective-permute-start(bf16[512,1024]{1,0:T(8,128)(2,1)} %add_convert_fusion.6), channel_id=1, source_target_pairs={{0,2},{1,3},{2,0},{3,1},{4,6},{5,7},{6,4},{7,5},{8,10},{9,11},{10,... | collective-permute-start | bytes 3145736 | tf_op jit(solution)/shard_map/ppermute | solution.py:686
  260.1 24.2 %collective-permute-start.20 = (bf16[512,1024]{1,0:T(8,128)(2,1)S(1)}, bf16[512,1024]{1,0:T(8,128)(2,1)S(1)}, u32[]{:S(2)}, u32[]{:S(2)}) collective-permute-start(bf16[512,1024]{1,0:T(8,128)(2,1)S(1)} %get-tuple-element.92.all_refs_0_), channel_id=1, source_target_pairs={{0,2},{1,3},{2,0},{3,1},{4,6},{5,7},{6,4},{7,5},{8,10},{9,11},{10,... | collective-permute-start | bytes 3145736 | tf_op jit(solution)/shard_map/ppermute | solution.py:686
  264.9 23.0 %collective-permute-start.23 = (bf16[512,1024]{1,0:T(8,128)(2,1)}, bf16[512,1024]{1,0:T(8,128)(2,1)}, u32[]{:S(2)}, u32[]{:S(2)}) collective-permute-start(bf16[512,1024]{1,0:T(8,128)(2,1)} %slice.276), channel_id=1, source_target_pairs={{0,1},{1,0},{2,3},{3,2},{4,5},{5,4},{6,7},{7,6},{8,9},{9,8},{10,11... | collective-permute-start | bytes 3145736 | tf_op jit(solution)/shard_map/ppermute | solution.py:686
  269.5 21.3 %collective-permute-start.22 = (bf16[512,1024]{1,0:T(8,128)(2,1)}, bf16[512,1024]{1,0:T(8,128)(2,1)}, u32[]{:S(2)}, u32[]{:S(2)}) collective-permute-start(bf16[512,1024]{1,0:T(8,128)(2,1)} %slice.274), channel_id=1, source_target_pairs={{0,1},{1,0},{2,3},{3,2},{4,5},{5,4},{6,7},{7,6},{8,9},{9,8},{10,11... | collective-permute-start | bytes 3145736 | tf_op jit(solution)/shard_map/ppermute | solution.py:686
  271.9 193.1 %reduce-scatter.3.cloned.1.call-start = ((), (), s32[]{:S(2)}) async-start(), calls=%async_computation.4 | async-start | bytes 5013504 | tf_op jit(solution)/shard_map/reduce_scatter | solution.py:729
  271.9 21.9 %collective-permute-start.19 = (bf16[512,1024]{1,0:T(8,128)(2,1)S(1)}, bf16[512,1024]{1,0:T(8,128)(2,1)S(1)}, u32[]{:S(2)}, u32[]{:S(2)}) collective-permute-start(bf16[512,1024]{1,0:T(8,128)(2,1)S(1)} %get-tuple-element.92.all_refs_0_), channel_id=1, source_target_pairs={{0,1},{1,0},{2,3},{3,2},{4,5},{5,4},{6,7},{7,6},{8,9},{9,8},{10,11... | collective-permute-start | bytes 3145736 | tf_op jit(solution)/shard_map/ppermute | solution.py:686
  387.5 26.0 %collective-permute-start.24 = (bf16[512,1024]{1,0:T(8,128)(2,1)S(1)}, bf16[512,1024]{1,0:T(8,128)(2,1)S(1)}, u32[]{:S(2)}, u32[]{:S(2)}) collective-permute-start(bf16[512,1024]{1,0:T(8,128)(2,1)S(1)} %copy-done.27), channel_id=1, source_target_pairs={{0,2},{1,3},{2,0},{3,1},{4,6},{5,7},{6,4},{7,5},{8,10},{9,11},{10,... | collective-permute-start | bytes 3145736 | tf_op jit(solution)/shard_map/ppermute | solution.py:686
  399.1 18.9 %collective-permute-start.27 = (bf16[512,1024]{1,0:T(8,128)(2,1)S(1)}, bf16[512,1024]{1,0:T(8,128)(2,1)S(1)}, u32[]{:S(2)}, u32[]{:S(2)}) collective-permute-start(bf16[512,1024]{1,0:T(8,128)(2,1)S(1)} %fusion.34), channel_id=1, source_target_pairs={{0,1},{1,0},{2,3},{3,2},{4,5},{5,4},{6,7},{7,6},{8,9},{9,8},{10,11... | collective-permute-start | bytes 3145736 | tf_op jit(solution)/shard_map/ppermute | solution.py:686
  399.2 35.9 %collective-permute-start.26 = (bf16[512,1024]{1,0:T(8,128)(2,1)S(1)}, bf16[512,1024]{1,0:T(8,128)(2,1)S(1)}, u32[]{:S(2)}, u32[]{:S(2)}) collective-permute-start(bf16[512,1024]{1,0:T(8,128)(2,1)S(1)} %copy-done.38), channel_id=1, source_target_pairs={{0,2},{1,3},{2,0},{3,1},{4,6},{5,7},{6,4},{7,5},{8,10},{9,11},{10,... | collective-permute-start | bytes 3145736 | tf_op jit(solution)/shard_map/ppermute | solution.py:686
  (63 other events, 791.6 us)
Sparse Core Ops, SparseCore 0:
  49.5 51.1 all-gather.2
  102.7 79.5 all-gather.4
  272.0 92.6 reduce-scatter.4
  371.4 93.5 reduce-scatter.2

commit v3 on v2

--- a/solution.py
+++ b/solution.py
@@ -13,7 +13,6 @@
 EPS_UNIT = 1e-06
 BF = jnp.bfloat16
 F32 = jnp.float32
-HIGH = lax.Precision.HIGHEST
 
 
 def mm(left, right):
@@ -34,10 +33,12 @@
     )
 
 
-def mm_exact(left, right):
-    return lax.dot_general(
-        left, right, (((1,), (0,)), ((), ())), precision=HIGH, preferred_element_type=F32
-    )
+def mm_exact(ones, right):
+    first = right.astype(BF)
+    rest = right - first.astype(F32)
+    second = rest.astype(BF)
+    third = (rest - second.astype(F32)).astype(BF)
+    return mm(ones, first) + (mm(ones, second) + mm(ones, third))
 
 
 def iota2(rows, columns):
@@ -98,6 +99,8 @@
         w_ref,
         hidden_ref,
         raw_ref,
+        conv_ref,
+        total_ref,
         mixed_ref,
         state_ref,
         inv_ref,
@@ -141,6 +144,7 @@
     betas = jax.nn.sigmoid(small)
     decays = -rate_ref[...] * softplus(small + bias_ref[...])
     total = mm_exact(lower_ones(BLOCK), decays)
+    total_ref[...] = total
     total_t = total.T
 
     def conv(start, width):
@@ -150,6 +154,7 @@
                 taps_ref[tap : tap + 1, start : start + width]
                 * ext_ref[pl.ds(5 + tap, BLOCK), start : start + width]
             )
+        conv_ref[:, start : start + width] = acc
         return acc * jax.nn.sigmoid(acc)
 
     def unit(value):
@@ -236,6 +241,8 @@
                 whole((width, total_width)),
                 rows_of(width),
                 rows_of(total_width),
+                rows_of(conv_width),
+                rows_of(HALF),
                 rows_of(value_all),
                 each(key_dim, value_dim),
                 each(BLOCK, BLOCK),
@@ -252,6 +259,8 @@
             shape((width, total_width), BF),
             shape((rows, width), BF),
             shape((rows, total_width), F32),
+            shape((rows, conv_width), F32),
+            shape((rows, HALF), F32),
             shape((rows, value_all), F32),
             shape((steps, heads, key_dim, value_dim), F32),
             shape((steps, heads, BLOCK, BLOCK), BF),
@@ -343,7 +352,8 @@
     (
     wout_ref,
     raw_ref,
-    halo_ref,
+    conv_ref,
+    total_ref,
     hidden_ref,
     wgate_ref,
     mixed_ref,
@@ -361,7 +371,6 @@
     dsmall_ref,
     donorm_ref,
     carry_ref,
-    ext_ref,
     dext_ref,
     dmix_ref,
     ) = all_refs[4:]
@@ -369,7 +378,7 @@
     value_dim = state_ref.shape[3]
     conv_width = taps_ref.shape[1]
     head_width = conv_width // heads
-    full_width = head_width + value_dim
+    gate_at = conv_width + HALF
     step = pl.program_id(0)
     block = pl.num_programs(0) - 1 - step
 
@@ -397,26 +406,16 @@
     def _():
         dext_ref[BLOCK:, :] = dext_ref[0:8, :]
 
-    keep = jnp.where(block % per_seq == 0, 0.0, 1.0)
-    ext_ref[0:8, :] = halo_ref[...] * keep
-    ext_ref[8:, :] = raw_ref[:, :conv_width]
-
     small = raw_ref[:, conv_width:]
     betas = jax.nn.sigmoid(small)
     shifted = small + bias_ref[...]
     decays = -rate_ref[...] * softplus(shifted)
-    lower = lower_ones(BLOCK)
-    total = mm_exact(lower, decays)
+    total = total_ref[...]
     total_t = total.T
     lane = lax.broadcasted_iota(jnp.int32, (1, HALF), 1)
 
     def conv(start, width):
-        acc = taps_ref[0:1, start : start + width] * ext_ref[pl.ds(5, BLOCK), start : start + width]
-        for tap in range(1, 4):
-            acc = acc + (
-                taps_ref[tap : tap + 1, start : start + width]
-                * ext_ref[pl.ds(5 + tap, BLOCK), start : start + width]
-            )
+        acc = conv_ref[:, start : start + width]
         sig = jax.nn.sigmoid(acc)
         return acc * sig, sig * (1.0 + acc * (1.0 - sig))
 
@@ -432,7 +431,6 @@
     def head_work(head):
         span = slice(head * value_dim, (head + 1) * value_dim)
         at = head * head_width
-        out_at = head * full_width
         grad = mm(dmix_ref[...], wout_ref[:, span])
         gate = mm(hidden_ref[...], wgate_ref[:, span])
         yield
@@ -444,7 +442,7 @@
         onorm = onorm_ref[...]
         grad_unit = grad * unit_mixed
         donorm_ref[...] += jnp.sum(grad_unit * silu, axis=0, keepdims=True)
-        draw_ref[:, out_at + head_width : out_at + full_width] = (
+        draw_ref[:, gate_at + head * value_dim : gate_at + (head + 1) * value_dim] = (
             grad_unit * onorm * (sig * (1.0 + gate * (1.0 - sig)))
         ).astype(BF)
         grad_on = grad * onorm * silu
@@ -570,27 +568,24 @@
     dalpha = ddecay * (-rate_ref[...]) * jax.nn.sigmoid(shifted)
     dsmall_ref[0:1, :] += jnp.sum(ddecay * decays, axis=0, keepdims=True)
     dsmall_ref[1:2, :] += jnp.sum(dalpha, axis=0, keepdims=True)
-    draw_ref[:, heads * full_width :] = (
+    draw_ref[:, conv_width:gate_at] = (
         jnp.where(lane < heads, dalpha, small_grad * betas * (1.0 - betas))
     ).astype(BF)
 
     width = HALF
     for start in range(0, conv_width, width):
         span = slice(start, start + width)
-        grad = dext_ref[0:BLOCK, span]
-        acc = taps_ref[3:4, span] * grad
-        for tap in range(3):
-            acc = acc + taps_ref[tap : tap + 1, span] * dext_ref[pl.ds(3 - tap, BLOCK), span]
-        out_at = (start // head_width) * full_width + start % head_width
-        draw_ref[:, out_at : out_at + width] = acc.astype(BF)
+        raw = raw_ref[:, span]
+        acc = jnp.zeros((BLOCK, width), F32)
         for tap in range(4):
-            dtaps_ref[tap : tap + 1, span] += jnp.sum(
-                grad * ext_ref[pl.ds(5 + tap, BLOCK), span], axis=0, keepdims=True
-            )
+            grad = dext_ref[pl.ds(3 - tap, BLOCK), span]
+            acc = acc + taps_ref[tap : tap + 1, span] * grad
+            dtaps_ref[tap : tap + 1, span] += jnp.sum(grad * raw, axis=0, keepdims=True)
+        draw_ref[:, span] = acc.astype(BF)
 
 
 def mixer_backward(place, part_rows, dmix, weights, saved, taps, rate, bias, onorm, heads):
-    hidden, raw, mixed, states, inverses, solved, query_eff, keyw = saved
+    hidden, raw, conv, total, mixed, states, inverses, solved, query_eff, keyw = saved
     rows, width = hidden.shape
     value_dim = onorm.shape[1]
     value_all = heads * value_dim
@@ -603,10 +598,6 @@
     rows_of = lambda columns, at=0: pl.BlockSpec((BLOCK, columns), lambda i, p: (last - i, at))
     each = lambda a, b: pl.BlockSpec((1, heads, a, b), lambda i, p: (last - i, 0, 0, 0))
     shape = jax.ShapeDtypeStruct
-    halo = pl.BlockSpec(
-        (8, conv_width), lambda i, p: (jnp.maximum((last - i) * (BLOCK // 8) - 1, 0), 0)
-    )
-
     return pl.pallas_call(
         functools.partial(backward_kernel, heads, SEQ // BLOCK),
         grid_spec=pltpu.PrefetchScalarGridSpec(
@@ -619,7 +610,8 @@
                 whole((part_rows, width)),
                 whole((width, value_all), 1),
                 rows_of(conv_width + HALF),
-                halo,
+                rows_of(conv_width),
+                rows_of(HALF),
                 rows_of(width),
                 whole((width, value_all), 0),
                 rows_of(value_all),
@@ -642,7 +634,6 @@
             scratch_shapes=[
                 pltpu.VMEM((heads, key_dim, value_dim), F32),
                 pltpu.VMEM((BLOCK + 8, conv_width), F32),
-                pltpu.VMEM((BLOCK + 8, conv_width), F32),
                 pltpu.VMEM((BLOCK, width), BF),
             ],
         ),
@@ -656,11 +647,11 @@
             dimension_semantics=("arbitrary",), vmem_limit_bytes=48 * 1024 * 1024
         ),
         cost_estimate=pl.CostEstimate(
-            flops=rows * 24_000_000, bytes_accessed=rows * 50_000, transcendentals=0
+            flops=rows * 2_000_000, bytes_accessed=rows * 5_000, transcendentals=0
         ),
         name="mixer_backward",
     )(
-        place, *dmix, weights, raw, raw, hidden, weights, mixed, states, inverses, solved,
+        place, *dmix, weights, raw, conv, total, hidden, weights, mixed, states, inverses, solved,
         query_eff, keyw, taps, rate, bias, onorm,
     )
 
@@ -827,7 +818,7 @@
     rate = pad_columns(jnp.exp(decay_log)[None], HALF)
     bias = pad_columns(decay_bias[None], HALF)
     onorm = onorm_gain[None]
-    w_first, hidden_one, raw, mixed, *saved = mixer_forward(
+    w_first, hidden_one, raw, conv_rows, totals, mixed, *saved = mixer_forward(
         tokens, norm1_gain[None], pieces, place_dp, taps, rate, bias, heads, value_dim
     )
     hidden_one, mixed, cot_far = lax.optimization_barrier((hidden_one, mixed, cot_blocks[2]))
@@ -837,14 +828,6 @@
         found = gated_out(place, first, part_rows, hidden_one, mixed, w_gate_out, onorm, heads)
         normed_blocks[first], normed_blocks[first - 1] = found[0], found[1]
         mixer_parts[first], mixer_parts[first - 1] = found[2], found[3]
-    w_gates = w_gate_out[:, :value_all]
-    columns = []
-    for head in range(heads):
-        columns.append(w_first[:, head * head_width : (head + 1) * head_width])
-        columns.append(w_gates[:, head * value_dim : (head + 1) * value_dim])
-    columns.append(w_first[:, heads * head_width :])
-    w_all = jnp.concatenate(columns, axis=1)
-
     def block_of(value, flip):
         return lax.dynamic_slice_in_dim(value, (me ^ flip) * part_rows, part_rows, 0)
 
@@ -896,21 +879,12 @@
     ffn_total = sum_dp(ffn_grad)
     middle_rows, ffn_grad = lax.optimization_barrier((middle_grad.astype(BF), ffn_grad))
     middle_blocks = gather_blocks(middle_rows)
-    near_branch = dot_right_t(near[2], w_down_t).astype(BF)
-    far_branch = dot_right_t(far[2], w_down_t).astype(BF)
-    branch_near = near_branch[part_rows:].astype(F32) + swap(near_branch[:part_rows], 1).astype(F32)
-    branch_far = far_sum([None, None, far_branch[part_rows:], far_branch[:part_rows]])
-    middle_blocks, branch_near, branch_far, w_all = lax.optimization_barrier(
-        (middle_blocks, branch_near, branch_far, w_all)
-    )
-    block_output = (middle + branch_near + swap(branch_far, 2).astype(F32)).astype(BF)
-
     draw, dtaps, dsmall, donorm = mixer_backward(
         place,
         part_rows,
         middle_blocks,
         w_gate_out,
-        (hidden_one, raw, mixed) + tuple(saved),
+        (hidden_one, raw, conv_rows, totals, mixed) + tuple(saved),
         taps,
         rate,
         bias,
@@ -919,26 +893,52 @@
     )
     output_grad = sum(dot_left_t(block, rows) for block, rows in zip(middle_blocks, normed_blocks))
     weight_grad = dot_left_t(hidden_one, draw)
-    gain_one_part = jnp.sum(weight_grad * w_all.astype(F32), axis=1) / norm1_gain
     weight_grad = jnp.concatenate([weight_grad.astype(BF), output_grad.astype(BF)], axis=1)
-    weight_grad, draw = lax.optimization_barrier((weight_grad, draw))
+    weight_grad, draw, near_active, far_active, w_first = lax.optimization_barrier(
+        (weight_grad, draw, near[2], far[2], w_first)
+    )
     mixer_total = sum_dp(weight_grad)
+    w_gates = w_gate_out[:, :value_all]
+    gate_at = w_first.shape[1]
 
     def hidden_part(value, flip):
-        return dot_right_t(block_of(value, flip), w_all)
+        rows = block_of(value, flip)
+        return dot_right_t(rows[:, :gate_at], w_first) + dot_right_t(rows[:, gate_at:], w_gates)
 
     far_low = far_sum([None, None, hidden_part(draw, 2), hidden_part(draw, 3)])
-    far_low, draw, gain_one_part = lax.optimization_barrier((far_low, draw, gain_one_part))
+    far_low, draw, near_active, far_active, weight_grad = lax.optimization_barrier(
+        (far_low, draw, near_active, far_active, weight_grad)
+    )
+    gain_one_part = (
+        jnp.sum(weight_grad[:, :gate_at].astype(F32) * w_first.astype(F32), axis=1)
+        + jnp.sum(
+            weight_grad[:, gate_at : draw.shape[1]].astype(F32) * w_gates.astype(F32), axis=1
+        )
+    ) / norm1_gain
+    near_branch = dot_right_t(near_active, w_down_t).astype(BF)
+    far_branch = dot_right_t(far_active, w_down_t).astype(BF)
+    far_term = swap(far_low, 2)
     hidden_one_grad = (
-        swap(far_low, 2).astype(F32)
+        far_term.astype(F32)
         + hidden_part(draw, 0)
         + swap(hidden_part(draw, 1).astype(BF), 1).astype(F32)
     )
-    full_width = head_width + value_dim
+    far_term, near_branch, far_branch = lax.optimization_barrier(
+        (far_term, near_branch, far_branch)
+    )
+    branch_rows = scatter_sum(
+        [
+            near_branch[part_rows:],
+            near_branch[:part_rows],
+            far_branch[part_rows:],
+            far_branch[:part_rows],
+        ]
+    )
+    block_output = (middle + branch_rows).astype(BF)
     output_total = mixer_total[:, draw.shape[1] :]
-    smalls = mixer_total[:, heads * full_width : draw.shape[1]]
-    totals = [
-        mixer_total[:, head * full_width : (head + 1) * full_width] for head in range(heads)
+    smalls = mixer_total[:, heads * head_width : gate_at]
+    head_totals = [
+        mixer_total[:, head * head_width : (head + 1) * head_width] for head in range(heads)
     ]
 
     inverse_one = lax.rsqrt(jnp.mean(inputs * inputs, axis=-1, keepdims=True) + EPS_NORM)
@@ -986,10 +986,10 @@
         tokens_grad,
         lax.dynamic_slice_in_dim(shared[0], me * gain_share, gain_share, 0),
         lax.dynamic_slice_in_dim(shared[1], me * gain_share, gain_share, 0),
-        collect(totals, 0, key_dim),
-        collect(totals, key_dim, key_dim),
-        collect(totals, 2 * key_dim, value_dim),
-        collect(totals, head_width, value_dim),
+        collect(head_totals, 0, key_dim),
+        collect(head_totals, key_dim, key_dim),
+        collect(head_totals, 2 * key_dim, value_dim),
+        mixer_total[:, gate_at : draw.shape[1]],
         smalls[:, :heads],
         smalls[:, heads : 2 * heads],
         collect(table_heads, 0, key_dim),

time: 485 us -> 469 us (0.967)
  local copies, waits for them, and re-layouts: 43.3 us -> 28.9 us
  waiting for transfers between devices: 161 us -> 169 us
  other arithmetic: 36 us -> 28.3 us
  Pallas kernels: 112 us -> 105 us
    ppermute x33, waiting for transfers between devices: 135 us -> 153 us  [hop(): return lax.ppermute(value, axis, [(i, i ^ flip) for i in range(count)])]
    reduce_scatter x2, waiting for transfers between devices: 18.6 us -> 3.49 us  [sum_dp(): lax.psum_scatter(value, 'dp', scatter_dimension=0, tiled=True).astype(F32)]
    unnamed x125 -> x123, local copies, waits for them, and re-layouts: 30.2 us -> 21.7 us
    pallas_call x1, Pallas kernels: 58.8 us -> 52.8 us  [mixer_backward(): pl.pallas_call(functools.partial(backward_kernel, heads, SEQ // BLOCK), g...]
    dot_general x8 -> x12, matrix products: 31.6 us -> 37.5 us  [dot_right_t(): lax.dot_general(left_side, right_side, (((1,), (1,)), ((), ())), preferre...]
    all_gather x1, waiting for transfers between devices: 4.05 us -> 9.07 us  [per_device(): w_ffn = lax.all_gather(ffn_local, 'dp', axis=0, tiled=True)]
  transfers between devices with their start and end apart: 37 -> 37, of which waited for: 18 -> 18; matrix products, arithmetic and copies ran while one was open for 28% -> 19% of each run, Pallas kernels for 23% -> 23%
where the time goes in v3:
time: 469 us; the launch traced here: 461 us
  waiting for transfers between devices  169 us (36%)
  Pallas kernels  105 us (22%)
  matrix products  84.1 us (18%)
  starting transfers between devices  30.2 us (6%)
  local copies, waits for them, and re-layouts  28.9 us (6%)
  other arithmetic  28.3 us (6%)
  between operations  15.5 us (3%)
    ppermute x33, waiting for transfers between devices, hop(): return lax.ppermute(value, axis, [(i, i ^ flip) for i in range(count)])  153 us
    pallas_call x1, Pallas kernels, mixer_backward(): pl.pallas_call(functools.partial(backward_kernel, heads, SEQ // BLOCK), g...  52.8 us
    pallas_call x1, Pallas kernels, mixer_forward(): pl.pallas_call(functools.partial(forward_kernel, heads, SEQ // BLOCK, len...  43 us
    dot_general x12, matrix products, dot_right_t(): lax.dot_general(left_side, right_side, (((1,), (1,)), ((), ())), preferre...  37.5 us
    ppermute x33, starting transfers between devices, hop(): return lax.ppermute(value, axis, [(i, i ^ flip) for i in range(count)])  30.1 us
    dot_general x9, matrix products, dot_left_t(): lax.dot_general(left_side, right_side, (((0,), (0,)), ((), ())), preferre...  29.7 us
    unnamed x123, local copies, waits for them, and re-layouts  21.7 us
    dot_general x4, matrix products, dot_plain(): return jnp.dot(left_side, right_side, preferred_element_type=F32)  17 us
  transfers between devices with their start and end apart: 37, of which 18 were waited for; matrix products, arithmetic and copies ran while one was open for 19% of the time, Pallas kernels for 23%

profile of v3, /device:TPU:0, one launch (start us, length us, event | category | flops | bytes accessed | tf_op | source)
XLA Modules:
  0.0 461.1 jit_solution(17212166348144171561)
XLA Ops:
  22.9 5.6 %collective-permute-done.1.refs_2_ = bf16[128,1152]{1,0:T(8,128)(2,1)S(1)} collective-permute-done((bf16[128,1152]{1,0:T(8,128)(2,1)S(1)}, bf16[128,1152]{1,0:T(8,128)(2,1)S(1)}, u32[]{:S(2)}, u32[]{:S(2)}) %collective-permute-start.1) | collective-permute-done | bytes 294944 | tf_op jit(solution)/shard_map/ppermute | solution.py:677
  30.2 9.3 %collective-permute-done.3.refs_4_ = bf16[128,1152]{1,0:T(8,128)(2,1)S(1)} collective-permute-done((bf16[128,1152]{1,0:T(8,128)(2,1)S(1)}, bf16[128,1152]{1,0:T(8,128)(2,1)S(1)}, u32[]{:S(2)}, u32[]{:S(2)}) %collective-permute-start.3) | collective-permute-done | bytes 294944 | tf_op jit(solution)/shard_map/ppermute | solution.py:677
  51.3 43.0 %mixer_forward.1 = (bf16[1024,1152]{1,0:T(8,128)(2,1)}, bf16[2048,1024]{1,0:T(8,128)(2,1)}, f32[2048,1152]{1,0:T(8,128)}, f32[2048,1024]{1,0:T(8,128)}, f32[2048...) custom-call(s32[1]{0:T(128)} %bitcast.1.place_ref, ...), custom_call_target="tpu_custom_call" | custom-call | flops 40960000000 | bytes 122880000 | tf_op jit(solution)/shard_map/mixer_forward/pallas_call | solution.py:227
  101.7 4.5 gated_out.3
  107.8 4.9 %gated_out.2 = (bf16[512,512]{1,0:T(8,128)(2,1)S(1)}, bf16[512,512]{1,0:T(8,128)(2,1)S(1)}, bf16[512,1024]{1,0:T(8,128)(2,1)S(1)}, bf16[512,1024]{1,0:T(8,128)(2,1)S(1)}) custom-call(s32[1]{0:T(128)} %bitcast.place_ref, bf16[2048,1024]{1,0:T(8,128)(2,1)} %get-tuple-element.81.hidden_ref.all_refs_8_, f32[2048,512]{1,0:T(8,128)} %get-tuple-element.82.mixed_ref.all_refs_10_, ...), custom_call_target="tpu_custom_call" | custom-call | flops 4096000000 | bytes 12288000 | tf_op jit(solution)/shard_map/gated_out/pallas_call | solution.py:320
  115.8 23.8 %collective-permute-done.10 = bf16[512,1024]{1,0:T(8,128)(2,1)} collective-permute-done((bf16[512,1024]{1,0:T(8,128)(2,1)S(1)}, bf16[512,1024]{1,0:T(8,128)(2,1)}, u32[]{:S(2)}, u32[]{:S(2)}) %collective-permute-start.10) | collective-permute-done | bytes 1048608 | tf_op jit(solution)/shard_map/ppermute | solution.py:677
  145.0 22.6 %collective-permute-done.15 = bf16[512,1024]{1,0:T(8,128)(2,1)S(1)} collective-permute-done((bf16[512,1024]{1,0:T(8,128)(2,1)S(1)}, bf16[512,1024]{1,0:T(8,128)(2,1)S(1)}, u32[]{:S(2)}, u32[]{:S(2)}) %collective-permute-start.15) | collective-permute-done | bytes 1048608 | tf_op jit(solution)/shard_map/ppermute | solution.py:677
  173.2 9.1 %all-gather.5.cloned.1.call-done = bf16[1024,2304]{0,1:T(8,128)(2,1)} async-done(((bf16[128,2304]{0,1:T(8,128)(2,1)}), bf16[1024,2304]{0,1:T(8,128)(2,1)}) %all-gather.5.cloned.1.call-update) | async-done | bytes 4718608 | tf_op jit(solution)/shard_map/all_gather | solution.py:812
  182.2 5.9 %fusion.15 = f32[1024,1536]{0,1:T(8,128)S(1)} fusion(bf16[1024,2304]{0,1:T(8,128)(2,1)} %all-gather.5.cloned.1.call-done, bf16[512,1024]{1,0:T(8,128)(2,1)S(1)} %multiply_convert_fusion.6, bf16[512,1024]{1,0:T(8,128)(2,1)} %collective-permute-done.12), kind=kOutput, calls=%fused_computation.52 | convolution fusion | flops 3225419776 | bytes 11534336 | tf_op jit(solution)/shard_map/dot_general | solution.py:660
  188.2 4.0 multiply_convert_fusion.5
  194.9 3.5 fusion.12
  198.4 3.6 multiply_convert_fusion.3
  207.7 5.9 %add_convert_fusion = bf16[1024,1536]{1,0:T(8,128)(2,1)S(1)} fusion(f32[1024,1536]{1,0:T(8,128)S(1)} %fusion.8, bf16[1024,768]{0,1:T(8,128)(2,1)S(1)} %copy-done.45, bf16[1024,768]{0,1:T(8,128)(2,1)S(1)} %get-tuple-element.168, bf16[512,1024]{1,0:T(8,128)(2,1)S(1)} %multiply_convert_fusion.6, bf16[512,1024]{1,0:T(8,128)(2,1)} %collective-permute-done.12), kind=kOutput, calls=%fused_computation | convolution fusion | flops 3234856960 | bytes 14680064 | tf_op jit(solution)/shard_map/dot_general | solution.py:670
  216.1 6.4 %fusion.20 = bf16[1024,1024]{1,0:T(8,128)(2,1)S(1)} fusion(bf16[1024,2304]{0,1:T(8,128)(2,1)} %all-gather.5.cloned.1.call-done, bf16[1024,768]{0,1:T(8,128)(2,1)} %copy-done.48, bf16[1024,768]{0,1:T(8,128)(2,1)} %copy-done.47), kind=kOutput, calls=%fused_computation.55 | convolution fusion | flops 3228565504 | bytes 8388608 | tf_op jit(solution)/shard_map/dot_general | solution.py:664
  223.9 5.8 %fusion.17 = bf16[1024,1024]{1,0:T(8,128)(2,1)S(1)} fusion(bf16[1024,2304]{0,1:T(8,128)(2,1)} %all-gather.5.cloned.1.call-done, bf16[1024,768]{0,1:T(8,128)(2,1)S(1)} %copy-done.46, bf16[1024,768]{0,1:T(8,128)(2,1)S(1)} %copy-done.44), kind=kOutput, calls=%fused_computation.54 | convolution fusion | flops 3228565504 | bytes 8388608 | tf_op jit(solution)/shard_map/dot_general | solution.py:664
  232.5 23.4 %collective-permute-done.18 = bf16[512,1024]{1,0:T(8,128)(2,1)S(1)} collective-permute-done((bf16[512,1024]{1,0:T(8,128)(2,1)S(1)}, bf16[512,1024]{1,0:T(8,128)(2,1)S(1)}, u32[]{:S(2)}, u32[]{:S(2)}) %collective-permute-start.18) | collective-permute-done | bytes 1048608 | tf_op jit(solution)/shard_map/ppermute | solution.py:677
  260.7 23.4 %collective-permute-done.20.all_refs_2_ = bf16[512,1024]{1,0:T(8,128)(2,1)S(1)} collective-permute-done((bf16[512,1024]{1,0:T(8,128)(2,1)S(1)}, bf16[512,1024]{1,0:T(8,128)(2,1)S(1)}, u32[]{:S(2)}, u32[]{:S(2)}) %collective-permute-start.20) | collective-permute-done | bytes 1048608 | tf_op jit(solution)/shard_map/ppermute | solution.py:677
  288.3 52.8 %mixer_backward.1 = (bf16[2048,1664]{1,0:T(8,128)(2,1)}, f32[8,1024]{1,0:T(8,128)S(1)}, f32[8,128]{1,0:T(8,128)S(1)}, f32[1,256]{1,0:T(1,128)S(1)}) custom-call(s32[1]{0:T(128)} %bitcast.place_ref, bf16[512,1024]{1,0:T(8,128)(2,1)S(1)} %get-tuple-element.90.all_refs_0_, bf16[512,1024]{1,0:T(8,128)(2,1)S(1)} %collective-permute-done.19.all_refs_1_, ...), custom_call_target="tpu_custom_call" | custom-call | flops 4096000000 | bytes 10240000 | tf_op jit(solution)/shard_map/mixer_backward/pallas_call | solution.py:601
  343.6 11.1 %convolution_convert_fusion = bf16[1024,1664]{1,0:T(8,128)(2,1)S(1)} fusion(bf16[2048,1024]{1,0:T(8,128)(2,1)S(1)} %copy-done.21, bf16[2048,1664]{1,0:T(8,128)(2,1)} %get-tuple-element.115), kind=kOutput, calls=%fused_computation.4 | convolution fusion | flops 6981025792 | bytes 14417920 | tf_op jit(solution)/shard_map/dot_general | solution.py:670
  357.2 3.7 fusion.27
  363.2 3.6 fusion.29
  381.4 13.4 %collective-permute-done.29 = f32[3,1024]{1,0:T(4,128)S(1)} collective-permute-done((f32[3,1024]{1,0:T(4,128)S(1)}, f32[3,1024]{1,0:T(4,128)S(1)}, u32[]{:S(2)}, u32[]{:S(2)}) %collective-permute-start.29) | collective-permute-done | bytes 12320 | tf_op jit(solution)/shard_map/ppermute | solution.py:677
  419.5 19.0 %collective-permute-done.26 = bf16[512,1024]{1,0:T(8,128)(2,1)S(1)} collective-permute-done((bf16[512,1024]{1,0:T(8,128)(2,1)S(1)}, bf16[512,1024]{1,0:T(8,128)(2,1)S(1)}, u32[]{:S(2)}, u32[]{:S(2)}) %collective-permute-start.26) | collective-permute-done | bytes 1048608 | tf_op jit(solution)/shard_map/ppermute | solution.py:677
  444.2 3.5 reduce-scatter.3.cloned.1.call-done
  (269 shorter events, 133.8 us)
Async XLA Ops:
  7.3 92.8 %all-gather.3.cloned.1.call-start = ((), (), s32[]{:S(2)}) async-start(), calls=%async_computation.2 | async-start | bytes 2359296 | tf_op jit(solution)/shard_map/all_gather | solution.py:811
  12.9 15.6 %collective-permute-start.1 = (bf16[128,1152]{1,0:T(8,128)(2,1)S(1)}, bf16[128,1152]{1,0:T(8,128)(2,1)S(1)}, u32[]{:S(2)}, u32[]{:S(2)}) collective-permute-start(bf16[128,1152]{1,0:T(8,128)(2,1)S(1)} %constant_dynamic-update-slice_fusion.6.refs_0_), channel_id=1, source_target_pairs={{0,8},{4,12},{8,0},{12,4},{16,24},{20,28},{24,16},{28,20},{1,9},{5... | collective-permute-start | bytes 884744 | tf_op jit(solution)/shard_map/ppermute | solution.py:677
  16.0 23.5 %collective-permute-start.3 = (bf16[128,1152]{1,0:T(8,128)(2,1)S(1)}, bf16[128,1152]{1,0:T(8,128)(2,1)S(1)}, u32[]{:S(2)}, u32[]{:S(2)}) collective-permute-start(bf16[128,1152]{1,0:T(8,128)(2,1)S(1)} %constant_dynamic-update-slice_fusion.6.refs_0_), channel_id=1, source_target_pairs={{0,16},{4,20},{8,24},{12,28},{16,0},{20,4},{24,8},{28,12},{1,17},{... | collective-permute-start | bytes 884744 | tf_op jit(solution)/shard_map/ppermute | solution.py:677
  18.6 22.4 %collective-permute-start.5 = (bf16[128,1152]{1,0:T(8,128)(2,1)S(1)}, bf16[128,1152]{1,0:T(8,128)(2,1)S(1)}, u32[]{:S(2)}, u32[]{:S(2)}) collective-permute-start(bf16[128,1152]{1,0:T(8,128)(2,1)S(1)} %constant_dynamic-update-slice_fusion.6.refs_0_), channel_id=1, source_target_pairs={{0,24},{4,28},{8,16},{12,20},{16,8},{20,12},{24,0},{28,4},{1,25},{... | collective-permute-start | bytes 884744 | tf_op jit(solution)/shard_map/ppermute | solution.py:677
  18.6 24.9 %collective-permute-start = (bf16[128,1152]{1,0:T(8,128)(2,1)S(1)}, bf16[128,1152]{1,0:T(8,128)(2,1)S(1)}, u32[]{:S(2)}, u32[]{:S(2)}) collective-permute-start(bf16[128,1152]{1,0:T(8,128)(2,1)S(1)} %constant_dynamic-update-slice_fusion.6.refs_0_), channel_id=1, source_target_pairs={{0,4},{4,0},{8,12},{12,8},{16,20},{20,16},{24,28},{28,24},{1,5},{5... | collective-permute-start | bytes 884744 | tf_op jit(solution)/shard_map/ppermute | solution.py:677
  28.6 15.0 %collective-permute-start.2 = (bf16[128,1152]{1,0:T(8,128)(2,1)S(1)}, bf16[128,1152]{1,0:T(8,128)(2,1)S(1)}, u32[]{:S(2)}, u32[]{:S(2)}) collective-permute-start(bf16[128,1152]{1,0:T(8,128)(2,1)S(1)} %collective-permute-done.1.refs_2_), channel_id=1, source_target_pairs={{0,4},{4,0},{8,12},{12,8},{16,20},{20,16},{24,28},{28,24},{1,5},{5... | collective-permute-start | bytes 884744 | tf_op jit(solution)/shard_map/ppermute | solution.py:677
  41.0 8.4 %collective-permute-start.6 = (bf16[128,1152]{1,0:T(8,128)(2,1)S(1)}, bf16[128,1152]{1,0:T(8,128)(2,1)S(1)}, u32[]{:S(2)}, u32[]{:S(2)}) collective-permute-start(bf16[128,1152]{1,0:T(8,128)(2,1)S(1)} %collective-permute-done.5.refs_6_), channel_id=1, source_target_pairs={{0,4},{4,0},{8,12},{12,8},{16,20},{20,16},{24,28},{28,24},{1,5},{5... | collective-permute-start | bytes 884744 | tf_op jit(solution)/shard_map/ppermute | solution.py:677
  49.4 132.8 %all-gather.5.cloned.1.call-start = ((), (), s32[]{:S(2)}) async-start(), calls=%async_computation.3 | async-start | bytes 5308416 | tf_op jit(solution)/shard_map/all_gather | solution.py:812
  49.6 47.4 %collective-permute-start.7 = (bf16[512,1024]{1,0:T(8,128)(2,1)}, bf16[512,1024]{1,0:T(8,128)(2,1)}, u32[]{:S(2)}, u32[]{:S(2)}) collective-permute-start(bf16[512,1024]{1,0:T(8,128)(2,1)} %param.21), channel_id=1, source_target_pairs={{0,2},{1,3},{2,0},{3,1},{4,6},{5,7},{6,4},{7,5},{8,10},{9,11},{10,... | collective-permute-start | bytes 3145736 | tf_op jit(solution)/shard_map/ppermute | solution.py:677
  51.2 389.0 %reduce-scatter.5.cloned.1.call-start = ((), (), s32[]{:S(2)}) async-start(), calls=%async_computation.5 | async-start | bytes 5308416 | tf_op jit(solution)/shard_map/reduce_scatter | solution.py:720
  113.7 25.9 %collective-permute-start.10 = (bf16[512,1024]{1,0:T(8,128)(2,1)S(1)}, bf16[512,1024]{1,0:T(8,128)(2,1)}, u32[]{:S(2)}, u32[]{:S(2)}) collective-permute-start(bf16[512,1024]{1,0:T(8,128)(2,1)S(1)} %add_convert_fusion.9), channel_id=1, source_target_pairs={{0,2},{1,3},{2,0},{3,1},{4,6},{5,7},{6,4},{7,5},{8,10},{9,11},{10,... | collective-permute-start | bytes 3145736 | tf_op jit(solution)/shard_map/ppermute | solution.py:677
  142.6 25.0 %collective-permute-start.15 = (bf16[512,1024]{1,0:T(8,128)(2,1)S(1)}, bf16[512,1024]{1,0:T(8,128)(2,1)S(1)}, u32[]{:S(2)}, u32[]{:S(2)}) collective-permute-start(bf16[512,1024]{1,0:T(8,128)(2,1)S(1)} %multiply_convert_fusion.6), channel_id=1, source_target_pairs={{0,2},{1,3},{2,0},{3,1},{4,6},{5,7},{6,4},{7,5},{8,10},{9,11},{10,... | collective-permute-start | bytes 3145736 | tf_op jit(solution)/shard_map/ppermute | solution.py:677
  144.5 23.6 %collective-permute-start.11 = (bf16[512,1024]{1,0:T(8,128)(2,1)S(1)}, bf16[512,1024]{1,0:T(8,128)(2,1)S(1)}, u32[]{:S(2)}, u32[]{:S(2)}) collective-permute-start(bf16[512,1024]{1,0:T(8,128)(2,1)S(1)} %copy-done.19), channel_id=1, source_target_pairs={{0,1},{1,0},{2,3},{3,2},{4,5},{5,4},{6,7},{7,6},{8,9},{9,8},{10,11... | collective-permute-start | bytes 3145736 | tf_op jit(solution)/shard_map/ppermute | solution.py:677
  144.5 23.8 %collective-permute-start.14 = (bf16[512,1024]{1,0:T(8,128)(2,1)}, bf16[512,1024]{1,0:T(8,128)(2,1)S(1)}, u32[]{:S(2)}, u32[]{:S(2)}) collective-permute-start(bf16[512,1024]{1,0:T(8,128)(2,1)} %collective-permute-done.7), channel_id=1, source_target_pairs={{0,1},{1,0},{2,3},{3,2},{4,5},{5,4},{6,7},{7,6},{8,9},{9,8},{10,11... | collective-permute-start | bytes 3145736 | tf_op jit(solution)/shard_map/ppermute | solution.py:677
  216.0 231.7 %reduce-scatter.3.cloned.1.call-start = ((), (), s32[]{:S(2)}) async-start(), calls=%async_computation.4 | async-start | bytes 5013504 | tf_op jit(solution)/shard_map/reduce_scatter | solution.py:720
  222.6 7.3 %collective-permute-start.17 = (bf16[512,1024]{1,0:T(8,128)(2,1)S(1)}, bf16[512,1024]{1,0:T(8,128)(2,1)S(1)}, u32[]{:S(2)}, u32[]{:S(2)}) collective-permute-start(bf16[512,1024]{1,0:T(8,128)(2,1)S(1)} %slice.287), channel_id=1, source_target_pairs={{0,1},{1,0},{2,3},{3,2},{4,5},{5,4},{6,7},{7,6},{8,9},{9,8},{10,11... | collective-permute-start | bytes 3145736 | tf_op jit(solution)/shard_map/ppermute | solution.py:677
  230.3 25.6 %collective-permute-start.18 = (bf16[512,1024]{1,0:T(8,128)(2,1)S(1)}, bf16[512,1024]{1,0:T(8,128)(2,1)S(1)}, u32[]{:S(2)}, u32[]{:S(2)}) collective-permute-start(bf16[512,1024]{1,0:T(8,128)(2,1)S(1)} %add_convert_fusion.8), channel_id=1, source_target_pairs={{0,2},{1,3},{2,0},{3,1},{4,6},{5,7},{6,4},{7,5},{8,10},{9,11},{10,... | collective-permute-start | bytes 3145736 | tf_op jit(solution)/shard_map/ppermute | solution.py:677
  259.2 24.9 %collective-permute-start.20 = (bf16[512,1024]{1,0:T(8,128)(2,1)S(1)}, bf16[512,1024]{1,0:T(8,128)(2,1)S(1)}, u32[]{:S(2)}, u32[]{:S(2)}) collective-permute-start(bf16[512,1024]{1,0:T(8,128)(2,1)S(1)} %get-tuple-element.90.all_refs_0_), channel_id=1, source_target_pairs={{0,2},{1,3},{2,0},{3,1},{4,6},{5,7},{6,4},{7,5},{8,10},{9,11},{10,... | collective-permute-start | bytes 3145736 | tf_op jit(solution)/shard_map/ppermute | solution.py:677
  260.7 26.0 %collective-permute-start.19 = (bf16[512,1024]{1,0:T(8,128)(2,1)S(1)}, bf16[512,1024]{1,0:T(8,128)(2,1)S(1)}, u32[]{:S(2)}, u32[]{:S(2)}) collective-permute-start(bf16[512,1024]{1,0:T(8,128)(2,1)S(1)} %get-tuple-element.90.all_refs_0_), channel_id=1, source_target_pairs={{0,1},{1,0},{2,3},{3,2},{4,5},{5,4},{6,7},{7,6},{8,9},{9,8},{10,11... | collective-permute-start | bytes 3145736 | tf_op jit(solution)/shard_map/ppermute | solution.py:677
  369.2 40.0 %collective-permute-start.23 = (bf16[512,1024]{1,0:T(8,128)(2,1)S(1)}, bf16[512,1024]{1,0:T(8,128)(2,1)S(1)}, u32[]{:S(2)}, u32[]{:S(2)}) collective-permute-start(bf16[512,1024]{1,0:T(8,128)(2,1)S(1)} %add_convert_fusion.5), channel_id=1, source_target_pairs={{0,2},{1,3},{2,0},{3,1},{4,6},{5,7},{6,4},{7,5},{8,10},{9,11},{10,... | collective-permute-start | bytes 3145736 | tf_op jit(solution)/shard_map/ppermute | solution.py:677
  378.1 16.7 %collective-permute-start.29 = (f32[3,1024]{1,0:T(4,128)S(1)}, f32[3,1024]{1,0:T(4,128)S(1)}, u32[]{:S(2)}, u32[]{:S(2)}) collective-permute-start(f32[3,1024]{1,0:T(4,128)S(1)} %fusion.61), channel_id=1, source_target_pairs={{0,2},{1,3},{2,0},{3,1},{4,6},{5,7},{6,4},{7,5},{8,10},{9,11},{10,... | collective-permute-start | bytes 36872 | tf_op jit(solution)/shard_map/ppermute | solution.py:677
  398.4 16.5 %collective-permute-start.27 = (bf16[512,1024]{1,0:T(8,128)(2,1)S(1)}, bf16[512,1024]{1,0:T(8,128)(2,1)S(1)}, u32[]{:S(2)}, u32[]{:S(2)}) collective-permute-start(bf16[512,1024]{1,0:T(8,128)(2,1)S(1)} %add_convert_fusion.2), channel_id=1, source_target_pairs={{0,1},{1,0},{2,3},{3,2},{4,5},{5,4},{6,7},{7,6},{8,9},{9,8},{10,11... | collective-permute-start | bytes 3145736 | tf_op jit(solution)/shard_map/ppermute | solution.py:677
  412.3 7.2 %collective-permute-start.24 = (bf16[512,1024]{1,0:T(8,128)(2,1)S(1)}, bf16[512,1024]{1,0:T(8,128)(2,1)S(1)}, u32[]{:S(2)}, u32[]{:S(2)}) collective-permute-start(bf16[512,1024]{1,0:T(8,128)(2,1)S(1)} %slice.243), channel_id=1, source_target_pairs={{0,1},{1,0},{2,3},{3,2},{4,5},{5,4},{6,7},{7,6},{8,9},{9,8},{10,11... | collective-permute-start | bytes 3145736 | tf_op jit(solution)/shard_map/ppermute | solution.py:677
  413.3 25.2 %collective-permute-start.26 = (bf16[512,1024]{1,0:T(8,128)(2,1)S(1)}, bf16[512,1024]{1,0:T(8,128)(2,1)S(1)}, u32[]{:S(2)}, u32[]{:S(2)}) collective-permute-start(bf16[512,1024]{1,0:T(8,128)(2,1)S(1)} %add_convert_fusion.4), channel_id=1, source_target_pairs={{0,2},{1,3},{2,0},{3,1},{4,6},{5,7},{6,4},{7,5},{8,10},{9,11},{10,... | collective-permute-start | bytes 3145736 | tf_op jit(solution)/shard_map/ppermute | solution.py:677
  (64 other events, 735.0 us)
Sparse Core Ops, SparseCore 0:
  49.5 50.4 all-gather.2
  102.1 80.0 all-gather.4
  216.1 93.4 reduce-scatter.4
  357.3 90.3 reduce-scatter.2
